TPU v7x, 32 devices: a whole 2x2x4 slice. The times are simulated.
32 devices in a mesh: grp: 2 (over y), exp: 4 (over z), col: 4 (over x, core).
Axes of the slice: x: 2, y: 2, z: 4, core: 2. Of those that a mesh axis runs over, the one named last changes fastest.
Arguments:
- weights: bfloat16 [24, 768, 4096], P(('grp', 'exp'), None, 'col'), parts along dimension 0, may hold values from -6 to 6
- fisher: bfloat16 [24, 768], P(('grp', 'exp')), parts along dimension 0, may hold values from 0.5 to 2
- members: int32 [24, 4], P('grp'), parts along dimension 0, may hold values from 0 to 1, as said below
- sketch: bfloat16 [24, 4096, 128], P(('grp', 'exp'), 'col'), parts along dimension 0, may hold values from -6 to 6
Outputs:
- base: bfloat16 [8, 768, 4096], P('grp', 'exp', 'col'), parts along dimension 0
- basis: bfloat16 [24, 768, 128], P(('grp', 'exp')), parts along dimension 0
- coeff: bfloat16 [24, 128, 4096], P(('grp', 'exp'), None, 'col'), parts along dimension 0
There are 2 independent parts, one for each index of `grp`. A program takes and returns all parts, laid end to end along the dimension named above; each array names one. Nothing has to cross between parts.
Inputs may be any that keep to these rules, and one draw needn't show every extreme that they name: `members`: each row holds a single 1; every cluster has 2 or more experts.
All inputs are finite; a program needn't handle non-finite values.
Results may differ from a plain program's by a relative error of at most 0.0077.
Values may be sent and summed in bfloat16 or wider, within the bound.
No kernel may reach another device: no remote copies, remote signals or barrier semaphores. Data moves between devices by JAX's collectives and lax.ppermute only.
A program may use at most 128 MiB of HBM per device.

v0:
```python
import functools
import math

import jax
import jax.numpy as jnp
from jax import lax
from jax.experimental import pallas as pl
from jax.experimental.pallas import tpu as pltpu
from jax.sharding import PartitionSpec as P

HIGH = lax.Precision.HIGHEST
UNIT = 32
VMEM_LIMIT = 20 * 1024 * 1024
SMEM = pl.BlockSpec(memory_space=pltpu.SMEM)


def params():
    return pltpu.CompilerParams(vmem_limit_bytes=VMEM_LIMIT)


COST = pl.CostEstimate(flops=10**10, transcendentals=0, bytes_accessed=1)
ANY = pl.BlockSpec(memory_space=pl.ANY)
HBM = pl.BlockSpec(memory_space=pltpu.HBM)


def in_hbm(array):
    return pltpu.with_memory_space_constraint(array, pltpu.HBM)


def sums_kernel(ahead, inner, mask, w_ref, a_ref, f_ref, *refs):
    experts, rows, cols = w_ref.shape
    out_ref = refs[-2] if ahead else refs[-1]
    if ahead:

        @pl.when(inner[0] == 0)
        def _():
            refs[-1][...] = refs[0][...]

    @pl.when(inner[0] == 1)
    def _():
        clusters = out_ref.shape[0]
        strip, width = 16, 512
        across = cols // width

        def one(n, carry):
            r = pl.multiple_of((n // across) * strip, strip)
            c = pl.multiple_of((n % across) * width, width)
            at = (pl.ds(r, strip), pl.ds(c, width))
            totals = [jnp.zeros((strip, width), jnp.float32) for _ in range(clusters)]
            for e in range(2 * experts):
                source = w_ref if e < experts else a_ref
                block = source[e % experts, at[0], at[1]].astype(jnp.float32)
                block = block * f_ref[pl.ds(r, strip), e : e + 1]
                for k in range(clusters):
                    totals[k] = totals[k] + block * mask[e, k]
            for k in range(clusters):
                out_ref[k, at[0], at[1]] = totals[k].astype(jnp.bfloat16)
            return carry

        lax.fori_loop(0, (rows // strip) * across, one, 0)


def cluster_sums(inner, mask, weights, arrived, fcols, start, rows, ahead, after):
    experts, _, cols = weights.shape
    clusters = mask.shape[1]
    first = start // UNIT
    steps = rows // UNIT
    out_specs = [pl.BlockSpec((clusters, UNIT, cols), lambda i, on: (0, i * on[0], 0))]
    out_shape = [jax.ShapeDtypeStruct((clusters, rows, cols), jnp.bfloat16)]
    extra, extra_specs = list(after), [ANY] * len(after)
    if ahead is not None:
        begin, length = ahead
        split = length % (16 * steps) == 0 and begin % (length // steps) == 0
        part = length // steps if split else length
        shape = (experts, part, cols)
        if part != length:
            at = begin // part
            extra_specs.insert(0, pl.BlockSpec(shape, lambda i, on: (0, at + i * (1 - on[0]), 0)))
            out_specs.append(pl.BlockSpec(shape, lambda i, on: (0, i * (1 - on[0]), 0)))
        else:
            place = (pl.Element(experts), pl.Element(length), pl.Element(cols))
            extra_specs.insert(0, pl.BlockSpec(place, lambda i, on: (0, begin, 0)))
            out_specs.append(pl.BlockSpec(shape, lambda i, on: (0, 0, 0)))
        out_shape.append(jax.ShapeDtypeStruct((experts, length, cols), jnp.bfloat16))
        extra.insert(0, in_hbm(weights))
    return pl.pallas_call(
        functools.partial(sums_kernel, ahead is not None),
        grid_spec=pltpu.PrefetchScalarGridSpec(
            num_scalar_prefetch=1,
            grid=(steps,),
            in_specs=[
                SMEM,
                pl.BlockSpec((experts, UNIT, cols), lambda i, on: (0, first + i * on[0], 0)),
                pl.BlockSpec((experts, UNIT, cols), lambda i, on: (0, i * on[0], 0)),
                pl.BlockSpec((UNIT, fcols.shape[1]), lambda i, on: (first + i * on[0], 0)),
            ]
            + extra_specs,
            out_specs=out_specs,
        ),
        out_shape=out_shape,
        cost_estimate=COST,
        compiler_params=params(),
    )(inner, mask, in_hbm(weights), arrived, fcols, *extra)


def base_kernel(inner, labels, p_ref, q_ref, d_ref, *refs):
    clusters, rows, cols = p_ref.shape
    out_ref, chosen_ref = refs[-2:] if labels is not None else (refs[-1], None)

    @pl.when(inner[0] == 1)
    def _():
        scale = 1.0 / d_ref[...]
        for k in range(clusters):
            total = p_ref[k].astype(jnp.float32) + q_ref[k].astype(jnp.float32)
            out_ref[k] = (total * scale[:, k : k + 1]).astype(jnp.bfloat16)
        if chosen_ref is not None:
            for e in range(chosen_ref.shape[0]):
                chosen_ref[e] = out_ref[labels[e]]


def whole_base_kernel(inner, *refs):
    base_kernel(inner, None, *refs)


def make_base(inner, mine, other, denom, start, labels, after):
    clusters, rows, cols = mine.shape
    first = start // UNIT
    block = lambda lead: pl.BlockSpec((lead, UNIT, cols), lambda i, on: (0, i * on[0], 0))
    in_specs = [
        block(clusters),
        block(clusters),
        pl.BlockSpec((UNIT, clusters), lambda i, on: (first + i * on[0], 0)),
    ]
    shape = jax.ShapeDtypeStruct(mine.shape, jnp.bfloat16)
    kernel, operands, outs, shapes = whole_base_kernel, (), block(clusters), shape
    if labels is not None:
        kernel, operands = base_kernel, (labels,)
        in_specs = [SMEM] + in_specs
        experts = labels.shape[0]
        outs = [block(clusters), block(experts)]
        shapes = [shape, jax.ShapeDtypeStruct((experts, rows, cols), jnp.bfloat16)]
    return pl.pallas_call(
        kernel,
        grid_spec=pltpu.PrefetchScalarGridSpec(
            num_scalar_prefetch=1,
            grid=(rows // UNIT,),
            in_specs=in_specs + [ANY] * len(after),
            out_specs=outs,
        ),
        out_shape=shapes,
        cost_estimate=COST,
        compiler_params=params(),
    )(inner, *operands, mine, other, denom, *after)


def residual_kernel(meta, w_ref, b_ref, r_ref, s_ref, *refs):
    delta_ref, base_ref, first_ref = refs[-3:]
    experts = w_ref.shape[0]
    by_expert = r_ref.shape[0] == experts
    inner = meta[experts] == 1
    labels = [meta[e] for e in range(experts)]
    base_ref[...] = b_ref[...] if by_expert else r_ref[...]

    def subtract(source, indices):
        for e in range(experts):
            chosen = source[indices[e]].astype(jnp.float32)
            delta_ref[e] = (w_ref[e].astype(jnp.float32) - chosen).astype(jnp.bfloat16)

    @pl.when(inner)
    def _():
        subtract(b_ref, labels)

    @pl.when(jnp.logical_not(inner))
    def _():
        subtract(r_ref, range(experts) if by_expert else labels)

    for e in range(experts):
        first_ref[e] = jnp.dot(delta_ref[e], s_ref[e], preferred_element_type=jnp.float32)


def residual_chunk(meta, weights, base, arrived, sketch, quarter, start, held, after):
    experts, units, cols = weights.shape
    clusters, rows, _ = base.shape
    rank = sketch.shape[2]
    first = start // UNIT
    quarter_blocks = units // 4 // UNIT
    local = first - quarter * quarter_blocks
    own = lambda meta: meta[experts + 1] == quarter

    def keep(i, meta):
        return (0, jnp.where(own(meta), local + i, quarter_blocks), 0)

    chunk = lambda lead: pl.BlockSpec((lead, UNIT, cols), lambda i, meta: (0, i, 0))
    placed = pl.BlockSpec((experts, UNIT, cols), lambda i, meta: (0, first + i, 0))
    return pl.pallas_call(
        residual_kernel,
        grid_spec=pltpu.PrefetchScalarGridSpec(
            num_scalar_prefetch=1,
            grid=(rows // UNIT,),
            in_specs=[
                placed,
                chunk(clusters),
                chunk(arrived.shape[0]),
                pl.BlockSpec(sketch.shape, lambda i, meta: (0, 0, 0)),
            ]
            + [HBM] * len(held)
            + [ANY] * len(after),
            out_specs=[
                placed,
                pl.BlockSpec((clusters, UNIT, cols), keep),
                pl.BlockSpec((experts, UNIT, rank), lambda i, meta: (0, i, 0)),
            ],
        ),
        out_shape=[
            pltpu.HBM((experts, units, cols), jnp.bfloat16),
            pltpu.HBM((clusters, units // 4 + UNIT, cols), jnp.bfloat16),
            jax.ShapeDtypeStruct((experts, rows, rank), jnp.float32),
        ],
        cost_estimate=COST,
        input_output_aliases={5 + i: i for i in range(len(held))},
        compiler_params=params(),
    )(meta, in_hbm(weights), base, arrived, sketch, *held, *after)


def copy_kernel(in_ref, out_ref):
    out_ref[...] = in_ref[...]


def leading_rows(array, rows):
    lead, _, cols = array.shape
    block = pl.BlockSpec((lead, rows, cols // 2), lambda i: (0, 0, i))
    return pl.pallas_call(
        copy_kernel,
        grid=(2,),
        in_specs=[block],
        out_specs=block,
        out_shape=jax.ShapeDtypeStruct((lead, rows, cols), array.dtype),
        compiler_params=params(),
    )(array)


GROUP = 8


def inverse_factors(grams):
    size = grams[0].shape[0]
    lane = lax.broadcasted_iota(jnp.int32, (GROUP, size), 1)
    sub = lax.broadcasted_iota(jnp.int32, (GROUP, size), 0)
    groups = range(size // GROUP)
    tables = [[g[i * GROUP : (i + 1) * GROUP] for i in groups] for g in grams]
    for at in groups:
        first = at * GROUP
        block = (lane >= first) & (lane < first + GROUP)
        unit = jnp.where(lane - first == sub, 1.0, 0.0)
        for table in tables:
            own = table[at]
            cols = [
                jnp.broadcast_to(own[:, first + t : first + t + 1], (GROUP, size))
                for t in range(GROUP)
            ]
            rows = jnp.where(block, unit, own)
            diag = cols[0]
            for t in range(GROUP - 1):
                factor = jnp.where(sub > t, cols[t] * (1.0 / cols[t][t : t + 1]), 0.0)
                for s in range(t + 1, GROUP):
                    cols[s] = cols[s] - factor * cols[s][t : t + 1]
                rows = rows - factor * rows[t : t + 1]
                diag = jnp.where(sub > t, cols[t + 1], diag)
            inverse = 1.0 / diag
            table[at] = rows * lax.rsqrt(diag)
            solved = rows * inverse
            for t in range(GROUP - 1, 0, -1):
                upper = jnp.where(sub < t, cols[t] * inverse, 0.0)
                solved = solved - upper * solved[t : t + 1]
            for i in range(at + 1, size // GROUP):
                value = table[i]
                rest = jnp.where(block, 0.0, value)
                for t in range(GROUP):
                    col = jnp.broadcast_to(value[:, first + t : first + t + 1], (GROUP, size))
                    rest = rest - col * solved[t : t + 1]
                table[i] = rest
    out = []
    for table in tables:
        parts = [jnp.where(lane <= sub + i * GROUP, table[i], 0.0) for i in groups]
        out.append(jnp.concatenate(parts, axis=0))
    return out


def contract(left, right, dims, precision=None):
    return lax.dot_general(
        left, right, (dims, ((), ())), precision=precision, preferred_element_type=jnp.float32
    )


def ranges(values, units):
    grams = [contract(y, y, ((0,), (0,)), HIGH) for y in values]
    factors = inverse_factors(grams)
    return [
        (contract(y, m, ((1,), (1,)), HIGH) * math.sqrt(units)).astype(jnp.bfloat16)
        for y, m in zip(values, factors)
    ]


def power_kernel(splits, pieces, side, *refs):
    parts = refs[: sum(splits)]
    delta_ref = refs[sum(splits)]
    keep_ref, send_ref, value, held, sem = refs[-5:]
    experts, units, _ = delta_ref.shape
    half = units // 2
    copy = pltpu.make_async_copy(delta_ref, held, sem)
    copy.start()
    at = 0
    for count, places in zip(splits, pieces):
        total = parts[at][...].astype(jnp.float32)
        for part in parts[at + 1 : at + count]:
            total = total + part[...].astype(jnp.float32)
        row = 0
        for start, rows in places:
            value[:, start : start + rows] = total[:, row : row + rows]
            row += rows
        at = at + count
    start = ranges([value[e] for e in range(experts)], units)
    copy.wait()
    own = pl.multiple_of(side[0] * half, half)
    other = pl.multiple_of((1 - side[0]) * half, half)
    for e in range(experts):
        back = contract(start[e], held[e], ((0,), (0,))).astype(jnp.bfloat16)
        keep_ref[e] = contract(held[e, pl.ds(own, half)], back, ((1,), (1,)))
        send_ref[e] = contract(held[e, pl.ds(other, half)], back, ((1,), (1,)))


def power_step(side, groups, delta):
    experts, units, _ = delta.shape
    pieces, groups = zip(*groups)
    rank = groups[0][0].shape[2]
    part = jax.ShapeDtypeStruct((experts, units // 2, rank), jnp.float32)
    vmem = pl.BlockSpec(memory_space=pltpu.VMEM)
    splits = tuple(len(g) for g in groups)
    return pl.pallas_call(
        functools.partial(power_kernel, splits, pieces),
        in_specs=[SMEM] + [vmem] * sum(splits) + [HBM],
        out_specs=[vmem] * 2,
        out_shape=[part, part],
        scratch_shapes=[
            pltpu.VMEM((experts, units, rank), jnp.float32),
            pltpu.VMEM(delta.shape, jnp.bfloat16),
            pltpu.SemaphoreType.DMA,
        ],
        compiler_params=params(),
    )(side, *[term for g in groups for term in g], delta)


def project_kernel(side, *refs):
    parts, (delta_ref, basis_ref, coeff_ref, value, held, sem) = refs[:-6], refs[-6:]
    experts, half, _ = parts[0].shape
    units = 2 * half
    copy = pltpu.make_async_copy(delta_ref, held, sem)
    copy.start()
    count = len(parts) // 2
    for place, group in ((side[0], parts[:count]), (1 - side[0], parts[count:])):
        total = group[0][...].astype(jnp.float32)
        for part in group[1:]:
            total = total + part[...].astype(jnp.float32)
        value[:, pl.ds(pl.multiple_of(place * half, half), half)] = total
    basis = ranges([value[e] for e in range(experts)], units)
    copy.wait()
    for e in range(experts):
        basis_ref[e] = basis[e]
        coeff = contract(basis[e], held[e], ((0,), (0,)))
        coeff_ref[e] = (coeff * (1.0 / math.sqrt(units))).astype(jnp.bfloat16)


def project(side, mine, others, delta):
    experts, units, _ = delta.shape
    rank = mine[0].shape[2]
    vmem = pl.BlockSpec(memory_space=pltpu.VMEM)
    return pl.pallas_call(
        project_kernel,
        in_specs=[SMEM] + [vmem] * (len(mine) + len(others)) + [HBM],
        out_specs=[vmem] * 2,
        out_shape=[
            jax.ShapeDtypeStruct((experts, units, rank), jnp.bfloat16),
            jax.ShapeDtypeStruct((experts, rank, delta.shape[2]), jnp.bfloat16),
        ],
        scratch_shapes=[
            pltpu.VMEM((experts, units, rank), jnp.float32),
            pltpu.VMEM(delta.shape, jnp.bfloat16),
            pltpu.SemaphoreType.DMA,
        ],
        compiler_params=params(),
    )(side, *mine, *others, delta)


def swap(value, bit, size):
    return lax.ppermute(value, "col", [(i, i ^ bit) for i in range(size)])


def sum_columns(value, size):
    bit = 1
    while 2 * bit < size:
        value = value + swap(value, bit, size)
        bit *= 2
    value = value.astype(jnp.bfloat16)
    return value, swap(value, bit, size)


def sum_halves(keep, send, size):
    total = (keep + swap(send, 1, size)).astype(jnp.bfloat16)
    bit = 2
    while 2 * bit < size:
        total = (total.astype(jnp.float32) + swap(total, bit, size).astype(jnp.float32)).astype(
            jnp.bfloat16
        )
        bit *= 2
    far = swap(total, bit, size)
    return (total, far), (swap(total, 1, size), swap(far, 1, size))


def merge_folded(weights, fisher, member_mask, sketch, col_size):
    inwards, across, outwards = [(0, 1), (3, 2)], [(1, 2), (2, 1)], [(1, 0), (2, 3)]
    experts, units, cols = weights.shape
    clusters = member_mask.shape[1]
    place = lax.axis_index("exp")
    inner = ((place == 1) | (place == 2)).astype(jnp.int32)[None]
    mine = lax.dynamic_slice_in_dim(member_mask, place * experts, experts)
    partner = lax.dynamic_slice_in_dim(member_mask, (place ^ 1) * experts, experts)
    mask = jnp.concatenate([mine, partner], axis=0)
    meta = jnp.concatenate([jnp.argmax(mine, axis=1).astype(jnp.int32), inner, place[None]])
    opening = weights[:, : UNIT]
    fisher, opening = lax.optimization_barrier((fisher, opening))
    near = [fisher.astype(jnp.float32)]
    for hop in (1, 2, 3):
        pairs = [(i, i ^ hop) for i in range(4)]
        near.append(lax.ppermute(fisher, "exp", pairs).astype(jnp.float32))
    denom = jnp.zeros((units, clusters), jnp.float32)
    for hop, value in enumerate(near):
        rows = lax.dynamic_slice_in_dim(member_mask, (place ^ hop) * experts, experts)
        denom = denom + jnp.sum(value[:, :, None] * rows[:, None, :], axis=0)
    fcols = jnp.concatenate(near[:2], axis=0).T

    chunks = [(0, 1), (0, 2), (0, 3), (3, 3), (3, 3), (1, 3), (1, 3), (2, 3), (2, 2), (2, 1)]
    groups = [(0, 1, 2, 3, 4), (5, 6, 7), (8, 9)]
    lead, lag = 2, 2
    spans, used = [], [0] * 4
    for q, size in chunks:
        spans.append((q * (units // 4) + used[q], size * UNIT))
        used[q] += size * UNIT
    count = len(chunks)
    their_labels = jnp.argmax(partner, axis=1).astype(jnp.int32)
    arrived, sums, others, base, moved, firsts = {}, {}, {}, {}, {}, {}
    held, after, terms, ready = (), (), [], {}
    for c in range(lead):
        block = weights[:, spans[c][0] : sum(spans[c])] if c else opening
        arrived[c] = lax.ppermute(block, "exp", inwards)
    order = []
    for step in range(count):
        order += [("sums", step), ("base", step - 1), ("residual", step - lag)]
    order += [("base", count - 1)] + [("residual", c) for c in range(count - lag, count)]
    for kind, c in order:
        if c < 0:
            continue
        if kind == "sums":
            ahead = spans[c + lead] if c + lead < count else None
            sums[c], *copied = cluster_sums(
                inner, mask, weights, arrived[c], fcols, *spans[c], ahead, after
            )
            others[c] = lax.ppermute(sums[c], "exp", across)
            if copied:
                arrived[c + lead] = lax.ppermute(copied[0], "exp", inwards)
            after = (sums[c],)
        elif kind == "base":
            whole = chunks[c][0] in (0, 3)
            labels = None if whole else their_labels
            result = make_base(inner, sums[c], others[c], denom, spans[c][0], labels, after)
            base[c], leaving = (result, result) if whole else result
            moved[c] = lax.ppermute(leaving, "exp", outwards)
            after = (base[c],)
        else:
            if c == count - 2:
                after = after + (moved[count - 1],)
            *held, firsts[c] = residual_chunk(
                meta,
                weights,
                base[c],
                moved[c],
                sketch,
                chunks[c][0],
                spans[c][0],
                held,
                after + ready.pop(c, ()),
            )
            after = (firsts[c],)
            for group in groups:
                if c == group[-1]:
                    joined = jnp.concatenate([firsts[g] for g in group], axis=1)
                    total = sum_columns(joined, col_size)
                    terms.append((tuple(spans[g] for g in group), total))
                    ready[c + 2] = total[1:]
    delta, bases = held
    base = leading_rows(bases, units // 4)
    return base, delta, terms


def merge_spread(weights, fisher, member_mask, sketch, col_size):
    moved = lax.all_to_all(weights, "exp", split_axis=1, concat_axis=0, tiled=True)
    f_rows = lax.all_to_all(fisher, "exp", split_axis=1, concat_axis=0, tiled=True)
    f_wide = f_rows.astype(jnp.float32)
    weighted = f_wide[:, :, None] * moved.astype(jnp.float32)
    numer = jnp.einsum("ek,erc->krc", member_mask, weighted, precision=HIGH)
    denom = jnp.einsum("ek,er->kr", member_mask, f_wide, precision=HIGH)
    base = (numer / denom[:, :, None]).astype(jnp.bfloat16)
    chosen = jnp.take(base, jnp.argmax(member_mask, axis=1), axis=0)
    residual = (moved.astype(jnp.float32) - chosen.astype(jnp.float32)).astype(jnp.bfloat16)
    delta = lax.all_to_all(residual, "exp", split_axis=0, concat_axis=1, tiled=True)
    first = jnp.einsum("nrc,nck->nrk", delta, sketch, preferred_element_type=jnp.float32)
    return base, delta, [(((0, first.shape[1]),), sum_columns(first, col_size))]


def body(exp_size, col_size, weights, fisher, members, sketch):
    member_mask = members.astype(jnp.float32)
    folded = exp_size == 4 and weights.shape[1] == 24 * UNIT
    merge = merge_folded if folded else merge_spread
    base, delta, first = merge(weights, fisher, member_mask, sketch, col_size)
    side = lax.rem(lax.axis_index("col"), 2)[None]
    mine, others = sum_halves(*power_step(side, first, delta), col_size)
    basis, coeff = project(side, mine, others, delta)
    return base, basis, coeff


def solution(mesh):
    in_specs = (
        P(("grp", "exp"), None, "col"),
        P(("grp", "exp"), None),
        P("grp", None),
        P(("grp", "exp"), "col", None),
    )
    out_specs = (
        P("grp", "exp", "col"),
        P(("grp", "exp"), None, None),
        P(("grp", "exp"), None, "col"),
    )
    run = functools.partial(body, mesh.shape["exp"], mesh.shape["col"])
    return jax.shard_map(run, mesh=mesh, in_specs=in_specs, out_specs=out_specs, check_vma=False)
```

profile of v0, /device:TPU:0, one launch (start us, length us, event | category | flops | bytes accessed | tf_op | source)
XLA Modules:
  0.0 229.3 jit_solution(18191184824942301529)
XLA Ops:
  1.6 3.1 %collective-permute-start.1 = (bf16[3,768]{1,0:T(4,128)(2,1)}, bf16[3,768]{1,0:T(4,128)(2,1)S(1)}, u32[]{:S(2)}, u32[]{:S(2)}) collective-permute-start(bf16[3,768]{1,0:T(4,128)(2,1)} %param.5), channel_id=1, source_target_pairs={{0,4},{4,0},{8,12},{12,8},{1,5},{5,1},{9,13},{13,9},{2,6},{6,2},{1... | collective-permute-start | bytes 13832 | tf_op jit(solution)/shard_map/ppermute | solution.py:434
  4.7 2.6 %collective-permute-start.5 = (bf16[3,768]{1,0:T(4,128)(2,1)}, bf16[3,768]{1,0:T(4,128)(2,1)S(1)}, u32[]{:S(2)}, u32[]{:S(2)}) collective-permute-start(bf16[3,768]{1,0:T(4,128)(2,1)} %param.5), channel_id=1, source_target_pairs={{0,8},{4,12},{8,0},{12,4},{1,9},{5,13},{9,1},{13,5},{2,10},{6,14},... | collective-permute-start | bytes 13832 | tf_op jit(solution)/shard_map/ppermute | solution.py:434
  7.3 2.8 %collective-permute-start.2 = (bf16[3,32,1024]{2,1,0:T(8,128)(2,1)S(1)}, bf16[3,32,1024]{2,1,0:T(8,128)(2,1)S(1)}, u32[]{:S(2)}, u32[]{:S(2)}) collective-permute-start(bf16[3,32,1024]{2,1,0:T(8,128)(2,1)S(1)} %slice.7), channel_id=1, source_target_pairs={{0,4},{12,8},{1,5},{13,9},{2,6},{14,10},{3,7},{15,11},{16,20},{28,... | collective-permute-start | bytes 589832 | tf_op jit(solution)/shard_map/ppermute | solution.py:454
  11.1 1.3 collective-permute-start
  18.3 6.7 %collective-permute-start.9 = (bf16[3,96,1024]{2,1,0:T(8,128)(2,1)S(1)}, bf16[3,96,1024]{2,1,0:T(8,128)(2,1)S(1)}, u32[]{:S(2)}, u32[]{:S(2)}) collective-permute-start(bf16[3,96,1024]{2,1,0:T(8,128)(2,1)S(1)} %get-tuple-element.74), channel_id=1, source_target_pairs={{0,4},{12,8},{1,5},{13,9},{2,6},{14,10},{3,7},{15,11},{16,20},{28,... | collective-permute-start | bytes 1769480 | tf_op jit(solution)/shard_map/ppermute | solution.py:469
  25.1 1.4 shard_map.68
  27.1 6.4 %collective-permute-start.3 = (bf16[3,96,1024]{2,1,0:T(8,128)(2,1)S(1)}, bf16[3,96,1024]{2,1,0:T(8,128)(2,1)S(1)}, u32[]{:S(2)}, u32[]{:S(2)}) collective-permute-start(bf16[3,96,1024]{2,1,0:T(8,128)(2,1)S(1)} %get-tuple-element.72), channel_id=1, source_target_pairs={{0,4},{12,8},{1,5},{13,9},{2,6},{14,10},{3,7},{15,11},{16,20},{28,... | collective-permute-start | bytes 1769480 | tf_op jit(solution)/shard_map/ppermute | solution.py:469
  34.9 3.6 %collective-permute-done.9.a_ref = bf16[3,96,1024]{2,1,0:T(8,128)(2,1)S(1)} collective-permute-done((bf16[3,96,1024]{2,1,0:T(8,128)(2,1)S(1)}, bf16[3,96,1024]{2,1,0:T(8,128)(2,1)S(1)}, u32[]{:S(2)}, u32[]{:S(2)}) %collective-permute-start.9) | collective-permute-done | bytes 589856 | tf_op jit(solution)/shard_map/ppermute | solution.py:469
  38.5 2.2 shard_map.70
  41.4 7.4 %collective-permute-start.15 = (bf16[3,96,1024]{2,1,0:T(8,128)(2,1)S(1)}, bf16[3,96,1024]{2,1,0:T(8,128)(2,1)S(1)}, u32[]{:S(2)}, u32[]{:S(2)}) collective-permute-start(bf16[3,96,1024]{2,1,0:T(8,128)(2,1)S(1)} %get-tuple-element.83), channel_id=1, source_target_pairs={{0,4},{12,8},{1,5},{13,9},{2,6},{14,10},{3,7},{15,11},{16,20},{28,... | collective-permute-start | bytes 1769480 | tf_op jit(solution)/shard_map/ppermute | solution.py:469
  50.3 2.5 %shard_map.72 = (bf16[3,768,1024]{2,1,0:T(8,128)(2,1)}, bf16[4,224,1024]{2,1,0:T(8,128)(2,1)}, f32[3,32,128]{2,1,0:T(8,128)S(1)}) custom-call(s32[5]{0:T(128)S(1)} %pad_add_fusion.meta, bf16[3,768,1024]{2,1,0:T(8,128)(2,1)} %w_ref.39, bf16[4,32,1024]{2,1,0:T(8,128)(2,1)S(1)} %shard_map.69.refs_1_.b_ref, ...), custom_call_target="tpu_custom_call" | custom-call | flops 10000000000 | bytes 1 | tf_op jit(solution)/shard_map/pallas_call | solution.py:195
  52.9 2.2 shard_map.73
  55.8 8.3 %collective-permute-start.10 = (bf16[3,96,1024]{2,1,0:T(8,128)(2,1)S(1)}, bf16[3,96,1024]{2,1,0:T(8,128)(2,1)S(1)}, u32[]{:S(2)}, u32[]{:S(2)}) collective-permute-start(bf16[3,96,1024]{2,1,0:T(8,128)(2,1)S(1)} %get-tuple-element.77), channel_id=1, source_target_pairs={{0,4},{12,8},{1,5},{13,9},{2,6},{14,10},{3,7},{15,11},{16,20},{28,... | collective-permute-start | bytes 1769480 | tf_op jit(solution)/shard_map/ppermute | solution.py:469
  65.7 3.0 %shard_map.75 = (bf16[3,768,1024]{2,1,0:T(8,128)(2,1)}, bf16[4,224,1024]{2,1,0:T(8,128)(2,1)}, f32[3,64,128]{2,1,0:T(8,128)S(1)}) custom-call(s32[5]{0:T(128)S(1)} %pad_add_fusion.meta, bf16[3,768,1024]{2,1,0:T(8,128)(2,1)} %w_ref.39, bf16[4,64,1024]{2,1,0:T(8,128)(2,1)S(1)} %shard_map.71.refs_0_.b_ref, ...), custom_call_target="tpu_custom_call", output_to_operand_aliasing={{0}: (5, {}), {1}: (6, {})} | custom-call | flops 10000000000 | bytes 1 | tf_op jit(solution)/shard_map/pallas_call | solution.py:195
  68.6 2.2 shard_map.76
  71.6 7.5 %collective-permute-start.21 = (bf16[3,96,1024]{2,1,0:T(8,128)(2,1)S(1)}, bf16[3,96,1024]{2,1,0:T(8,128)(2,1)S(1)}, u32[]{:S(2)}, u32[]{:S(2)}) collective-permute-start(bf16[3,96,1024]{2,1,0:T(8,128)(2,1)S(1)} %get-tuple-element.93), channel_id=1, source_target_pairs={{0,4},{12,8},{1,5},{13,9},{2,6},{14,10},{3,7},{15,11},{16,20},{28,... | collective-permute-start | bytes 1769480 | tf_op jit(solution)/shard_map/ppermute | solution.py:469
  80.6 4.0 %shard_map.78 = (bf16[3,768,1024]{2,1,0:T(8,128)(2,1)}, bf16[4,224,1024]{2,1,0:T(8,128)(2,1)}, f32[3,96,128]{2,1,0:T(8,128)S(1)}) custom-call(s32[5]{0:T(128)S(1)} %pad_add_fusion.meta, bf16[3,768,1024]{2,1,0:T(8,128)(2,1)} %w_ref.39, bf16[4,96,1024]{2,1,0:T(8,128)(2,1)S(1)} %shard_map.74.refs_2_.b_ref, ...), custom_call_target="tpu_custom_call", output_to_operand_aliasing={{0}: (5, {}), {1}: (6, {})} | custom-call | flops 10000000000 | bytes 1 | tf_op jit(solution)/shard_map/pallas_call | solution.py:195
  84.6 2.2 shard_map.79
  89.1 12.2 %collective-permute-start.16 = (bf16[3,96,1024]{2,1,0:T(8,128)(2,1)S(1)}, bf16[3,96,1024]{2,1,0:T(8,128)(2,1)S(1)}, u32[]{:S(2)}, u32[]{:S(2)}) collective-permute-start(bf16[3,96,1024]{2,1,0:T(8,128)(2,1)S(1)} %get-tuple-element.87), channel_id=1, source_target_pairs={{0,4},{12,8},{1,5},{13,9},{2,6},{14,10},{3,7},{15,11},{16,20},{28,... | collective-permute-start | bytes 1769480 | tf_op jit(solution)/shard_map/ppermute | solution.py:469
  101.3 3.9 %shard_map.81 = (bf16[3,768,1024]{2,1,0:T(8,128)(2,1)}, bf16[4,224,1024]{2,1,0:T(8,128)(2,1)}, f32[3,96,128]{2,1,0:T(8,128)S(1)}) custom-call(s32[5]{0:T(128)S(1)} %pad_add_fusion.meta, bf16[3,768,1024]{2,1,0:T(8,128)(2,1)} %w_ref.39, bf16[4,96,1024]{2,1,0:T(8,128)(2,1)S(1)} %shard_map.77.refs_2_.b_ref, ...), custom_call_target="tpu_custom_call", output_to_operand_aliasing={{0}: (5, {}), {1}: (6, {})} | custom-call | flops 10000000000 | bytes 1 | tf_op jit(solution)/shard_map/pallas_call | solution.py:195
  105.2 1.4 shard_map.82
  107.4 6.1 %collective-permute-start.27 = (bf16[3,64,1024]{2,1,0:T(8,128)(2,1)S(1)}, bf16[3,64,1024]{2,1,0:T(8,128)(2,1)S(1)}, u32[]{:S(2)}, u32[]{:S(2)}) collective-permute-start(bf16[3,64,1024]{2,1,0:T(8,128)(2,1)S(1)} %get-tuple-element.107), channel_id=1, source_target_pairs={{0,4},{12,8},{1,5},{13,9},{2,6},{14,10},{3,7},{15,11},{16,20},{28,... | collective-permute-start | bytes 1179656 | tf_op jit(solution)/shard_map/ppermute | solution.py:469
  114.3 3.9 %shard_map.84 = (bf16[3,768,1024]{2,1,0:T(8,128)(2,1)}, bf16[4,224,1024]{2,1,0:T(8,128)(2,1)}, f32[3,96,128]{2,1,0:T(8,128)S(1)}) custom-call(s32[5]{0:T(128)S(1)} %pad_add_fusion.meta, bf16[3,768,1024]{2,1,0:T(8,128)(2,1)} %w_ref.39, bf16[4,96,1024]{2,1,0:T(8,128)(2,1)S(1)} %shard_map.80.refs_2_.b_ref, ...), custom_call_target="tpu_custom_call", output_to_operand_aliasing={{0}: (5, {}), {1}: (6, {})} | custom-call | flops 10000000000 | bytes 1 | tf_op jit(solution)/shard_map/pallas_call | solution.py:195
  118.4 1.3 collective-permute-start.25
  119.7 1.3 shard_map.85
  121.7 8.0 %collective-permute-start.22 = (bf16[3,32,1024]{2,1,0:T(8,128)(2,1)S(1)}, bf16[3,32,1024]{2,1,0:T(8,128)(2,1)S(1)}, u32[]{:S(2)}, u32[]{:S(2)}) collective-permute-start(bf16[3,32,1024]{2,1,0:T(8,128)(2,1)S(1)} %get-tuple-element.98), channel_id=1, source_target_pairs={{0,4},{12,8},{1,5},{13,9},{2,6},{14,10},{3,7},{15,11},{16,20},{28,... | collective-permute-start | bytes 589832 | tf_op jit(solution)/shard_map/ppermute | solution.py:469
  132.0 4.4 %collective-permute-done.25.r_ref = bf16[3,96,1024]{2,1,0:T(8,128)(2,1)S(1)} collective-permute-done((bf16[3,96,1024]{2,1,0:T(8,128)(2,1)S(1)}, bf16[3,96,1024]{2,1,0:T(8,128)(2,1)S(1)}, u32[]{:S(2)}, u32[]{:S(2)}) %collective-permute-start.25) | collective-permute-done | bytes 589856 | tf_op jit(solution)/shard_map/ppermute | solution.py:476
  136.4 1.5 collective-permute-start.29
  137.9 3.9 %shard_map.87 = (bf16[3,768,1024]{2,1,0:T(8,128)(2,1)}, bf16[4,224,1024]{2,1,0:T(8,128)(2,1)}, f32[3,96,128]{2,1,0:T(8,128)S(1)}) custom-call(s32[5]{0:T(128)S(1)} %pad_add_fusion.meta, bf16[3,768,1024]{2,1,0:T(8,128)(2,1)} %w_ref.39, bf16[4,96,1024]{2,1,0:T(8,128)(2,1)S(1)} %get-tuple-element.96.refs_2_.b_ref, ...), custom_call_target="tpu_custom_call", output_to_operand_aliasing={{0}: (5, {}), {1}: (6, {})} | custom-call | flops 10000000000 | bytes 1 | tf_op jit(solution)/shard_map/pallas_call | solution.py:195
  145.7 2.9 %collective-permute-done.24.r_ref = bf16[3,96,1024]{2,1,0:T(8,128)(2,1)S(1)} collective-permute-done((bf16[3,96,1024]{2,1,0:T(8,128)(2,1)S(1)}, bf16[3,96,1024]{2,1,0:T(8,128)(2,1)S(1)}, u32[]{:S(2)}, u32[]{:S(2)}) %collective-permute-start.24) | collective-permute-done | bytes 589856 | tf_op jit(solution)/shard_map/ppermute | solution.py:476
  148.6 3.9 %shard_map.90 = (bf16[3,768,1024]{2,1,0:T(8,128)(2,1)}, bf16[4,224,1024]{2,1,0:T(8,128)(2,1)}, f32[3,96,128]{2,1,0:T(8,128)S(1)}) custom-call(s32[5]{0:T(128)S(1)} %pad_add_fusion.meta, bf16[3,768,1024]{2,1,0:T(8,128)(2,1)} %w_ref.39, bf16[4,96,1024]{2,1,0:T(8,128)(2,1)S(1)} %get-tuple-element.100.refs_2_.b_ref, ...), custom_call_target="tpu_custom_call", output_to_operand_aliasing={{0}: (5, {}), {1}: (6, {})} | custom-call | flops 10000000000 | bytes 1 | tf_op jit(solution)/shard_map/pallas_call | solution.py:195
  155.0 1.5 collective-permute-start.34
  156.4 7.4 %collective-permute-done.31.r_ref = bf16[3,96,1024]{2,1,0:T(8,128)(2,1)S(1)} collective-permute-done((bf16[3,96,1024]{2,1,0:T(8,128)(2,1)S(1)}, bf16[3,96,1024]{2,1,0:T(8,128)(2,1)S(1)}, u32[]{:S(2)}, u32[]{:S(2)}) %collective-permute-start.31) | collective-permute-done | bytes 589856 | tf_op jit(solution)/shard_map/ppermute | solution.py:476
  163.9 3.9 %shard_map.93 = (bf16[3,768,1024]{2,1,0:T(8,128)(2,1)}, bf16[4,224,1024]{2,1,0:T(8,128)(2,1)}, f32[3,96,128]{2,1,0:T(8,128)S(1)}) custom-call(s32[5]{0:T(128)S(1)} %pad_add_fusion.meta, bf16[3,768,1024]{2,1,0:T(8,128)(2,1)} %w_ref.39, bf16[4,96,1024]{2,1,0:T(8,128)(2,1)S(1)} %get-tuple-element.109.refs_2_.b_ref, ...), custom_call_target="tpu_custom_call", output_to_operand_aliasing={{0}: (5, {}), {1}: (6, {})} | custom-call | flops 10000000000 | bytes 1 | tf_op jit(solution)/shard_map/pallas_call | solution.py:195
  169.8 2.0 collective-permute-start.36
  171.8 5.8 %collective-permute-done.33.refs_3_.r_ref = bf16[3,32,1024]{2,1,0:T(8,128)(2,1)S(1)} collective-permute-done((bf16[3,32,1024]{2,1,0:T(8,128)(2,1)S(1)}, bf16[3,32,1024]{2,1,0:T(8,128)(2,1)S(1)}, u32[]{:S(2)}, u32[]{:S(2)}) %collective-permute-start.33) | collective-permute-done | bytes 196640 | tf_op jit(solution)/shard_map/ppermute | solution.py:476
  177.6 3.0 %shard_map.95 = (bf16[3,768,1024]{2,1,0:T(8,128)(2,1)}, bf16[4,224,1024]{2,1,0:T(8,128)(2,1)}, f32[3,64,128]{2,1,0:T(8,128)S(1)}) custom-call(s32[5]{0:T(128)S(1)} %pad_add_fusion.meta, bf16[3,768,1024]{2,1,0:T(8,128)(2,1)} %w_ref.39, bf16[4,64,1024]{2,1,0:T(8,128)(2,1)S(1)} %get-tuple-element.114.refs_2_.b_ref, ...), custom_call_target="tpu_custom_call", output_to_operand_aliasing={{0}: (5, {}), {1}: (6, {})} | custom-call | flops 10000000000 | bytes 1 | tf_op jit(solution)/shard_map/pallas_call | solution.py:195
  180.6 2.6 %shard_map.96 = (bf16[3,768,1024]{2,1,0:T(8,128)(2,1)}, bf16[4,224,1024]{2,1,0:T(8,128)(2,1)}, f32[3,32,128]{2,1,0:T(8,128)S(1)}) custom-call(s32[5]{0:T(128)S(1)} %pad_add_fusion.meta, bf16[3,768,1024]{2,1,0:T(8,128)(2,1)} %w_ref.39, bf16[4,32,1024]{2,1,0:T(8,128)(2,1)S(1)} %get-tuple-element.116.refs_2_.b_ref, ...), custom_call_target="tpu_custom_call", output_to_operand_aliasing={{0}: (5, {}), {1}: (6, {})} | custom-call | flops 10000000000 | bytes 1 | tf_op jit(solution)/shard_map/pallas_call | solution.py:195
  183.2 1.4 collective-permute-done.37
  184.6 2.0 collective-permute-start.38
  186.6 2.6 %collective-permute-done.38.refs_5_ = bf16[3,96,128]{2,1,0:T(8,128)(2,1)S(1)} collective-permute-done((bf16[3,96,128]{2,1,0:T(8,128)(2,1)S(1)}, bf16[3,96,128]{2,1,0:T(8,128)(2,1)S(1)}, u32[]{:S(2)}, u32[]{:S(2)}) %collective-permute-start.38) | collective-permute-done | bytes 73760 | tf_op jit(solution)/shard_map/ppermute | solution.py:395
  189.2 2.3 %copy-done = bf16[3,768,1024]{2,1,0:T(8,128)(2,1)S(1)} copy-done((bf16[3,768,1024]{2,1,0:T(8,128)(2,1)S(1)}, bf16[3,768,1024]{2,1,0:T(8,128)(2,1)}, u32[]{:S(2)}) %copy-start) | copy-done | bytes 4718616
  191.5 12.4 %shard_map.98 = (f32[3,384,128]{2,1,0:T(8,128)S(1)}, f32[3,384,128]{2,1,0:T(8,128)S(1)}) custom-call(s32[1]{0:T(128)} %bitcast.3.side, bf16[3,384,128]{2,1,0:T(8,128)(2,1)S(1)} %add_convert_fusion.1.refs_0_, bf16[3,384,128]{2,1,0:T(8,128)(2,1)S(1)} %collective-permute-done.29.refs_3_.refs_1_, bf16[3,288,128]{2,1,0:T(8,128)(2,1)S(1)} %add_convert_fusion.2.refs_2_, ...), custom_call_target="tpu_custom_call" | custom-call | tf_op jit(solution)/shard_map/pallas_call | solution.py:339
  204.0 2.0 collective-permute-done.39
  206.1 1.8 collective-permute-start.40
  207.9 7.3 %collective-permute-done.40.refs_1_ = bf16[3,384,128]{2,1,0:T(8,128)(2,1)S(1)} collective-permute-done((bf16[3,384,128]{2,1,0:T(8,128)(2,1)S(1)}, bf16[3,384,128]{2,1,0:T(8,128)(2,1)S(1)}, u32[]{:S(2)}, u32[]{:S(2)}) %collective-permute-start.40) | collective-permute-done | bytes 294944 | tf_op jit(solution)/shard_map/ppermute | solution.py:395
  215.2 1.3 shard_map.97
  216.8 12.4 %shard_map.99 = (bf16[3,768,128]{2,1,0:T(8,128)(2,1)}, bf16[3,128,1024]{2,1,0:T(8,128)(2,1)}) custom-call(s32[1]{0:T(128)} %bitcast.3.side, bf16[3,384,128]{2,1,0:T(8,128)(2,1)S(1)} %add_convert_fusion.refs_0_, bf16[3,384,128]{2,1,0:T(8,128)(2,1)S(1)} %collective-permute-done.40.refs_1_, bf16[3,384,128]{2,1,0:T(8,128)(2,1)S(1)} %collective-permute-done.41.refs_2_, ...), custom_call_target="tpu_custom_call" | custom-call | tf_op jit(solution)/shard_map/pallas_call | solution.py:377
  (116 shorter events, 31.8 us)
Async XLA Ops:
  1.6 13.8 %collective-permute-start.1 = (bf16[3,768]{1,0:T(4,128)(2,1)}, bf16[3,768]{1,0:T(4,128)(2,1)S(1)}, u32[]{:S(2)}, u32[]{:S(2)}) collective-permute-start(bf16[3,768]{1,0:T(4,128)(2,1)} %param.5), channel_id=1, source_target_pairs={{0,4},{4,0},{8,12},{12,8},{1,5},{5,1},{9,13},{13,9},{2,6},{6,2},{1... | collective-permute-start | bytes 13832 | tf_op jit(solution)/shard_map/ppermute | solution.py:434
  4.7 10.8 %collective-permute-start.5 = (bf16[3,768]{1,0:T(4,128)(2,1)}, bf16[3,768]{1,0:T(4,128)(2,1)S(1)}, u32[]{:S(2)}, u32[]{:S(2)}) collective-permute-start(bf16[3,768]{1,0:T(4,128)(2,1)} %param.5), channel_id=1, source_target_pairs={{0,8},{4,12},{8,0},{12,4},{1,9},{5,13},{9,1},{13,5},{2,10},{6,14},... | collective-permute-start | bytes 13832 | tf_op jit(solution)/shard_map/ppermute | solution.py:434
  7.3 8.7 %collective-permute-start.6 = (bf16[3,768]{1,0:T(4,128)(2,1)}, bf16[3,768]{1,0:T(4,128)(2,1)S(1)}, u32[]{:S(2)}, u32[]{:S(2)}) collective-permute-start(bf16[3,768]{1,0:T(4,128)(2,1)} %param.5), channel_id=1, source_target_pairs={{0,12},{4,8},{8,4},{12,0},{1,13},{5,9},{9,5},{13,1},{2,14},{6,10},... | collective-permute-start | bytes 13832 | tf_op jit(solution)/shard_map/ppermute | solution.py:434
  7.3 9.1 %collective-permute-start.2 = (bf16[3,32,1024]{2,1,0:T(8,128)(2,1)S(1)}, bf16[3,32,1024]{2,1,0:T(8,128)(2,1)S(1)}, u32[]{:S(2)}, u32[]{:S(2)}) collective-permute-start(bf16[3,32,1024]{2,1,0:T(8,128)(2,1)S(1)} %slice.7), channel_id=1, source_target_pairs={{0,4},{12,8},{1,5},{13,9},{2,6},{14,10},{3,7},{15,11},{16,20},{28,... | collective-permute-start | bytes 589832 | tf_op jit(solution)/shard_map/ppermute | solution.py:454
  11.1 14.0 %collective-permute-start = (bf16[3,64,1024]{2,1,0:T(8,128)(2,1)S(1)}, bf16[3,64,1024]{2,1,0:T(8,128)(2,1)S(1)}, u32[]{:S(2)}, u32[]{:S(2)}) collective-permute-start(bf16[3,64,1024]{2,1,0:T(8,128)(2,1)S(1)} %slice.6), channel_id=1, source_target_pairs={{0,4},{12,8},{1,5},{13,9},{2,6},{14,10},{3,7},{15,11},{16,20},{28,... | collective-permute-start | bytes 1179656 | tf_op jit(solution)/shard_map/ppermute | solution.py:454
  17.6 16.0 %collective-permute-start.4 = (bf16[4,32,1024]{2,1,0:T(8,128)(2,1)S(1)}, bf16[4,32,1024]{2,1,0:T(8,128)(2,1)S(1)}, u32[]{:S(2)}, u32[]{:S(2)}) collective-permute-start(bf16[4,32,1024]{2,1,0:T(8,128)(2,1)S(1)} %get-tuple-element.71.refs_1_.refs_0_), channel_id=1, source_target_pairs={{4,8},{8,4},{5,9},{9,5},{6,10},{10,6},{7,11},{11,7},{20,24},{24,20... | collective-permute-start | bytes 786440 | tf_op jit(solution)/shard_map/ppermute | solution.py:467
  18.3 20.2 %collective-permute-start.9 = (bf16[3,96,1024]{2,1,0:T(8,128)(2,1)S(1)}, bf16[3,96,1024]{2,1,0:T(8,128)(2,1)S(1)}, u32[]{:S(2)}, u32[]{:S(2)}) collective-permute-start(bf16[3,96,1024]{2,1,0:T(8,128)(2,1)S(1)} %get-tuple-element.74), channel_id=1, source_target_pairs={{0,4},{12,8},{1,5},{13,9},{2,6},{14,10},{3,7},{15,11},{16,20},{28,... | collective-permute-start | bytes 1769480 | tf_op jit(solution)/shard_map/ppermute | solution.py:469
  26.4 22.4 %collective-permute-start.8 = (bf16[4,64,1024]{2,1,0:T(8,128)(2,1)S(1)}, bf16[4,64,1024]{2,1,0:T(8,128)(2,1)S(1)}, u32[]{:S(2)}, u32[]{:S(2)}) collective-permute-start(bf16[4,64,1024]{2,1,0:T(8,128)(2,1)S(1)} %get-tuple-element.73.refs_3_.refs_0_), channel_id=1, source_target_pairs={{4,8},{8,4},{5,9},{9,5},{6,10},{10,6},{7,11},{11,7},{20,24},{24,20... | collective-permute-start | bytes 1572872 | tf_op jit(solution)/shard_map/ppermute | solution.py:467
  27.1 25.7 %collective-permute-start.3 = (bf16[3,96,1024]{2,1,0:T(8,128)(2,1)S(1)}, bf16[3,96,1024]{2,1,0:T(8,128)(2,1)S(1)}, u32[]{:S(2)}, u32[]{:S(2)}) collective-permute-start(bf16[3,96,1024]{2,1,0:T(8,128)(2,1)S(1)} %get-tuple-element.72), channel_id=1, source_target_pairs={{0,4},{12,8},{1,5},{13,9},{2,6},{14,10},{3,7},{15,11},{16,20},{28,... | collective-permute-start | bytes 1769480 | tf_op jit(solution)/shard_map/ppermute | solution.py:469
  33.6 16.7 %collective-permute-start.7 = (bf16[4,32,1024]{2,1,0:T(8,128)(2,1)S(1)}, bf16[4,32,1024]{2,1,0:T(8,128)(2,1)S(1)}, u32[]{:S(2)}, u32[]{:S(2)}) collective-permute-start(bf16[4,32,1024]{2,1,0:T(8,128)(2,1)S(1)} %shard_map.69.refs_1_.b_ref), channel_id=1, source_target_pairs={{4,0},{8,12},{5,1},{9,13},{6,2},{10,14},{7,3},{11,15},{20,16},{24,... | collective-permute-start | bytes 786440 | tf_op jit(solution)/shard_map/ppermute | solution.py:476
  40.7 23.5 %collective-permute-start.11 = (bf16[4,96,1024]{2,1,0:T(8,128)(2,1)S(1)}, bf16[4,96,1024]{2,1,0:T(8,128)(2,1)S(1)}, u32[]{:S(2)}, u32[]{:S(2)}) collective-permute-start(bf16[4,96,1024]{2,1,0:T(8,128)(2,1)S(1)} %get-tuple-element.75.refs_3_.refs_0_), channel_id=1, source_target_pairs={{4,8},{8,4},{5,9},{9,5},{6,10},{10,6},{7,11},{11,7},{20,24},{24,20... | collective-permute-start | bytes 2359304 | tf_op jit(solution)/shard_map/ppermute | solution.py:467
  41.4 8.9 %copy-start.3 = (bf16[3,1024,128]{2,1,0:T(8,128)(2,1)S(1)}, bf16[3,1024,128]{2,1,0:T(8,128)(2,1)}, u32[]{:S(2)}) copy-start(bf16[3,1024,128]{2,1,0:T(8,128)(2,1)} %s_ref.19) | copy-start | bytes 2359300
  41.4 27.2 %collective-permute-start.15 = (bf16[3,96,1024]{2,1,0:T(8,128)(2,1)S(1)}, bf16[3,96,1024]{2,1,0:T(8,128)(2,1)S(1)}, u32[]{:S(2)}, u32[]{:S(2)}) collective-permute-start(bf16[3,96,1024]{2,1,0:T(8,128)(2,1)S(1)} %get-tuple-element.83), channel_id=1, source_target_pairs={{0,4},{12,8},{1,5},{13,9},{2,6},{14,10},{3,7},{15,11},{16,20},{28,... | collective-permute-start | bytes 1769480 | tf_op jit(solution)/shard_map/ppermute | solution.py:469
  49.0 16.7 %collective-permute-start.13 = (bf16[4,64,1024]{2,1,0:T(8,128)(2,1)S(1)}, bf16[4,64,1024]{2,1,0:T(8,128)(2,1)S(1)}, u32[]{:S(2)}, u32[]{:S(2)}) collective-permute-start(bf16[4,64,1024]{2,1,0:T(8,128)(2,1)S(1)} %shard_map.71.refs_0_.b_ref), channel_id=1, source_target_pairs={{4,0},{8,12},{5,1},{9,13},{6,2},{10,14},{7,3},{11,15},{20,16},{24,... | collective-permute-start | bytes 1572872 | tf_op jit(solution)/shard_map/ppermute | solution.py:476
  55.1 24.0 %collective-permute-start.14 = (bf16[4,96,1024]{2,1,0:T(8,128)(2,1)S(1)}, bf16[4,96,1024]{2,1,0:T(8,128)(2,1)S(1)}, u32[]{:S(2)}, u32[]{:S(2)}) collective-permute-start(bf16[4,96,1024]{2,1,0:T(8,128)(2,1)S(1)} %get-tuple-element.78.refs_3_.refs_0_), channel_id=1, source_target_pairs={{4,8},{8,4},{5,9},{9,5},{6,10},{10,6},{7,11},{11,7},{20,24},{24,20... | collective-permute-start | bytes 2359304 | tf_op jit(solution)/shard_map/ppermute | solution.py:467
  55.8 28.8 %collective-permute-start.10 = (bf16[3,96,1024]{2,1,0:T(8,128)(2,1)S(1)}, bf16[3,96,1024]{2,1,0:T(8,128)(2,1)S(1)}, u32[]{:S(2)}, u32[]{:S(2)}) collective-permute-start(bf16[3,96,1024]{2,1,0:T(8,128)(2,1)S(1)} %get-tuple-element.77), channel_id=1, source_target_pairs={{0,4},{12,8},{1,5},{13,9},{2,6},{14,10},{3,7},{15,11},{16,20},{28,... | collective-permute-start | bytes 1769480 | tf_op jit(solution)/shard_map/ppermute | solution.py:469
  64.4 16.2 %collective-permute-start.12 = (bf16[4,96,1024]{2,1,0:T(8,128)(2,1)S(1)}, bf16[4,96,1024]{2,1,0:T(8,128)(2,1)S(1)}, u32[]{:S(2)}, u32[]{:S(2)}) collective-permute-start(bf16[4,96,1024]{2,1,0:T(8,128)(2,1)S(1)} %shard_map.74.refs_2_.b_ref), channel_id=1, source_target_pairs={{4,0},{8,12},{5,1},{9,13},{6,2},{10,14},{7,3},{11,15},{20,16},{24,... | collective-permute-start | bytes 2359304 | tf_op jit(solution)/shard_map/ppermute | solution.py:476
  70.9 16.7 %collective-permute-start.17 = (bf16[4,96,1024]{2,1,0:T(8,128)(2,1)S(1)}, bf16[4,96,1024]{2,1,0:T(8,128)(2,1)S(1)}, u32[]{:S(2)}, u32[]{:S(2)}) collective-permute-start(bf16[4,96,1024]{2,1,0:T(8,128)(2,1)S(1)} %get-tuple-element.85.refs_3_.refs_0_), channel_id=1, source_target_pairs={{4,8},{8,4},{5,9},{9,5},{6,10},{10,6},{7,11},{11,7},{20,24},{24,20... | collective-permute-start | bytes 2359304 | tf_op jit(solution)/shard_map/ppermute | solution.py:467
  71.6 33.6 %collective-permute-start.21 = (bf16[3,96,1024]{2,1,0:T(8,128)(2,1)S(1)}, bf16[3,96,1024]{2,1,0:T(8,128)(2,1)S(1)}, u32[]{:S(2)}, u32[]{:S(2)}) collective-permute-start(bf16[3,96,1024]{2,1,0:T(8,128)(2,1)S(1)} %get-tuple-element.93), channel_id=1, source_target_pairs={{0,4},{12,8},{1,5},{13,9},{2,6},{14,10},{3,7},{15,11},{16,20},{28,... | collective-permute-start | bytes 1769480 | tf_op jit(solution)/shard_map/ppermute | solution.py:469
  79.3 22.0 %collective-permute-start.19 = (bf16[4,96,1024]{2,1,0:T(8,128)(2,1)S(1)}, bf16[4,96,1024]{2,1,0:T(8,128)(2,1)S(1)}, u32[]{:S(2)}, u32[]{:S(2)}) collective-permute-start(bf16[4,96,1024]{2,1,0:T(8,128)(2,1)S(1)} %shard_map.77.refs_2_.b_ref), channel_id=1, source_target_pairs={{4,0},{8,12},{5,1},{9,13},{6,2},{10,14},{7,3},{11,15},{20,16},{24,... | collective-permute-start | bytes 2359304 | tf_op jit(solution)/shard_map/ppermute | solution.py:476
  86.8 26.6 %collective-permute-start.20 = (bf16[4,96,1024]{2,1,0:T(8,128)(2,1)S(1)}, bf16[4,96,1024]{2,1,0:T(8,128)(2,1)S(1)}, u32[]{:S(2)}, u32[]{:S(2)}) collective-permute-start(bf16[4,96,1024]{2,1,0:T(8,128)(2,1)S(1)} %get-tuple-element.88.refs_3_.p_ref), channel_id=1, source_target_pairs={{4,8},{8,4},{5,9},{9,5},{6,10},{10,6},{7,11},{11,7},{20,24},{24,20... | collective-permute-start | bytes 2359304 | tf_op jit(solution)/shard_map/ppermute | solution.py:467
  87.8 26.5 %collective-permute-start.18 = (bf16[4,96,1024]{2,1,0:T(8,128)(2,1)S(1)}, bf16[4,96,1024]{2,1,0:T(8,128)(2,1)S(1)}, u32[]{:S(2)}, u32[]{:S(2)}) collective-permute-start(bf16[4,96,1024]{2,1,0:T(8,128)(2,1)S(1)} %shard_map.80.refs_2_.b_ref), channel_id=1, source_target_pairs={{4,0},{8,12},{5,1},{9,13},{6,2},{10,14},{7,3},{11,15},{20,16},{24,... | collective-permute-start | bytes 2359304 | tf_op jit(solution)/shard_map/ppermute | solution.py:476
  89.1 30.6 %collective-permute-start.16 = (bf16[3,96,1024]{2,1,0:T(8,128)(2,1)S(1)}, bf16[3,96,1024]{2,1,0:T(8,128)(2,1)S(1)}, u32[]{:S(2)}, u32[]{:S(2)}) collective-permute-start(bf16[3,96,1024]{2,1,0:T(8,128)(2,1)S(1)} %get-tuple-element.87), channel_id=1, source_target_pairs={{0,4},{12,8},{1,5},{13,9},{2,6},{14,10},{3,7},{15,11},{16,20},{28,... | collective-permute-start | bytes 1769480 | tf_op jit(solution)/shard_map/ppermute | solution.py:469
  106.7 15.1 %collective-permute-start.23 = (bf16[4,96,1024]{2,1,0:T(8,128)(2,1)S(1)}, bf16[4,96,1024]{2,1,0:T(8,128)(2,1)S(1)}, u32[]{:S(2)}, u32[]{:S(2)}) collective-permute-start(bf16[4,96,1024]{2,1,0:T(8,128)(2,1)S(1)} %get-tuple-element.95.refs_0_.p_ref), channel_id=1, source_target_pairs={{4,8},{8,4},{5,9},{9,5},{6,10},{10,6},{7,11},{11,7},{20,24},{24,20... | collective-permute-start | bytes 2359304 | tf_op jit(solution)/shard_map/ppermute | solution.py:467
  107.4 34.4 %collective-permute-start.27 = (bf16[3,64,1024]{2,1,0:T(8,128)(2,1)S(1)}, bf16[3,64,1024]{2,1,0:T(8,128)(2,1)S(1)}, u32[]{:S(2)}, u32[]{:S(2)}) collective-permute-start(bf16[3,64,1024]{2,1,0:T(8,128)(2,1)S(1)} %get-tuple-element.107), channel_id=1, source_target_pairs={{0,4},{12,8},{1,5},{13,9},{2,6},{14,10},{3,7},{15,11},{16,20},{28,... | collective-permute-start | bytes 1179656 | tf_op jit(solution)/shard_map/ppermute | solution.py:469
  118.3 12.3 %collective-permute-start.28 = (f32[3,384,128]{2,1,0:T(8,128)S(1)}, f32[3,384,128]{2,1,0:T(8,128)S(1)}, u32[]{:S(2)}, u32[]{:S(2)}) collective-permute-start(f32[3,384,128]{2,1,0:T(8,128)S(1)} %constant_dynamic-update-slice_fusion), channel_id=1, source_target_pairs={{0,1},{1,0},{2,3},{3,2},{4,5},{5,4},{6,7},{7,6},{8,9},{9,8},{10,11... | collective-permute-start | bytes 1769480 | tf_op jit(solution)/shard_map/ppermute | solution.py:395
  118.4 18.0 %collective-permute-start.25 = (bf16[3,96,1024]{2,1,0:T(8,128)(2,1)S(1)}, bf16[3,96,1024]{2,1,0:T(8,128)(2,1)S(1)}, u32[]{:S(2)}, u32[]{:S(2)}) collective-permute-start(bf16[3,96,1024]{2,1,0:T(8,128)(2,1)S(1)} %get-tuple-element.102), channel_id=1, source_target_pairs={{4,0},{8,12},{5,1},{9,13},{6,2},{10,14},{7,3},{11,15},{20,16},{24,... | collective-permute-start | bytes 1769480 | tf_op jit(solution)/shard_map/ppermute | solution.py:476
  121.0 22.6 %collective-permute-start.26 = (bf16[4,96,1024]{2,1,0:T(8,128)(2,1)S(1)}, bf16[4,96,1024]{2,1,0:T(8,128)(2,1)S(1)}, u32[]{:S(2)}, u32[]{:S(2)}) collective-permute-start(bf16[4,96,1024]{2,1,0:T(8,128)(2,1)S(1)} %get-tuple-element.99.refs_0_.p_ref), channel_id=1, source_target_pairs={{4,8},{8,4},{5,9},{9,5},{6,10},{10,6},{7,11},{11,7},{20,24},{24,20... | collective-permute-start | bytes 2359304 | tf_op jit(solution)/shard_map/ppermute | solution.py:467
  121.7 30.8 %collective-permute-start.22 = (bf16[3,32,1024]{2,1,0:T(8,128)(2,1)S(1)}, bf16[3,32,1024]{2,1,0:T(8,128)(2,1)S(1)}, u32[]{:S(2)}, u32[]{:S(2)}) collective-permute-start(bf16[3,32,1024]{2,1,0:T(8,128)(2,1)S(1)} %get-tuple-element.98), channel_id=1, source_target_pairs={{0,4},{12,8},{1,5},{13,9},{2,6},{14,10},{3,7},{15,11},{16,20},{28,... | collective-permute-start | bytes 589832 | tf_op jit(solution)/shard_map/ppermute | solution.py:469
  130.6 18.0 %collective-permute-start.24 = (bf16[3,96,1024]{2,1,0:T(8,128)(2,1)S(1)}, bf16[3,96,1024]{2,1,0:T(8,128)(2,1)S(1)}, u32[]{:S(2)}, u32[]{:S(2)}) collective-permute-start(bf16[3,96,1024]{2,1,0:T(8,128)(2,1)S(1)} %get-tuple-element.101), channel_id=1, source_target_pairs={{4,0},{8,12},{5,1},{9,13},{6,2},{10,14},{7,3},{11,15},{20,16},{24,... | collective-permute-start | bytes 1769480 | tf_op jit(solution)/shard_map/ppermute | solution.py:476
  136.4 12.2 %collective-permute-start.29 = (bf16[3,384,128]{2,1,0:T(8,128)(2,1)S(1)}, bf16[3,384,128]{2,1,0:T(8,128)(2,1)S(1)}, u32[]{:S(2)}, u32[]{:S(2)}) collective-permute-start(bf16[3,384,128]{2,1,0:T(8,128)(2,1)S(1)} %add_convert_fusion.1.refs_0_), channel_id=1, source_target_pairs={{0,2},{1,3},{2,0},{3,1},{4,6},{5,7},{6,4},{7,5},{8,10},{9,11},{10,... | collective-permute-start | bytes 884744 | tf_op jit(solution)/shard_map/ppermute | solution.py:395
  142.8 11.3 %collective-permute-start.32 = (bf16[4,64,1024]{2,1,0:T(8,128)(2,1)S(1)}, bf16[4,64,1024]{2,1,0:T(8,128)(2,1)S(1)}, u32[]{:S(2)}, u32[]{:S(2)}) collective-permute-start(bf16[4,64,1024]{2,1,0:T(8,128)(2,1)S(1)} %shard_map.88.refs_0_.p_ref), channel_id=1, source_target_pairs={{4,8},{8,4},{5,9},{9,5},{6,10},{10,6},{7,11},{11,7},{20,24},{24,20... | collective-permute-start | bytes 1572872 | tf_op jit(solution)/shard_map/ppermute | solution.py:467
  144.4 19.5 %collective-permute-start.31 = (bf16[3,96,1024]{2,1,0:T(8,128)(2,1)S(1)}, bf16[3,96,1024]{2,1,0:T(8,128)(2,1)S(1)}, u32[]{:S(2)}, u32[]{:S(2)}) collective-permute-start(bf16[3,96,1024]{2,1,0:T(8,128)(2,1)S(1)} %get-tuple-element.111), channel_id=1, source_target_pairs={{4,0},{8,12},{5,1},{9,13},{6,2},{10,14},{7,3},{11,15},{20,16},{24,... | collective-permute-start | bytes 1769480 | tf_op jit(solution)/shard_map/ppermute | solution.py:476
  153.5 14.4 %collective-permute-start.30 = (bf16[4,32,1024]{2,1,0:T(8,128)(2,1)S(1)}, bf16[4,32,1024]{2,1,0:T(8,128)(2,1)S(1)}, u32[]{:S(2)}, u32[]{:S(2)}) collective-permute-start(bf16[4,32,1024]{2,1,0:T(8,128)(2,1)S(1)} %shard_map.91.refs_0_.p_ref), channel_id=1, source_target_pairs={{4,8},{8,4},{5,9},{9,5},{6,10},{10,6},{7,11},{11,7},{20,24},{24,20... | collective-permute-start | bytes 786440 | tf_op jit(solution)/shard_map/ppermute | solution.py:467
  155.0 16.9 %collective-permute-start.34 = (bf16[3,64,1024]{2,1,0:T(8,128)(2,1)S(1)}, bf16[3,64,1024]{2,1,0:T(8,128)(2,1)S(1)}, u32[]{:S(2)}, u32[]{:S(2)}) collective-permute-start(bf16[3,64,1024]{2,1,0:T(8,128)(2,1)S(1)} %get-tuple-element.118), channel_id=1, source_target_pairs={{4,0},{8,12},{5,1},{9,13},{6,2},{10,14},{7,3},{11,15},{20,16},{24,... | collective-permute-start | bytes 1179656 | tf_op jit(solution)/shard_map/ppermute | solution.py:476
  167.8 1.9 collective-permute-start.35
  168.4 9.2 %collective-permute-start.33 = (bf16[3,32,1024]{2,1,0:T(8,128)(2,1)S(1)}, bf16[3,32,1024]{2,1,0:T(8,128)(2,1)S(1)}, u32[]{:S(2)}, u32[]{:S(2)}) collective-permute-start(bf16[3,32,1024]{2,1,0:T(8,128)(2,1)S(1)} %get-tuple-element.117), channel_id=1, source_target_pairs={{4,0},{8,12},{5,1},{9,13},{6,2},{10,14},{7,3},{11,15},{20,16},{24,... | collective-permute-start | bytes 589832 | tf_op jit(solution)/shard_map/ppermute | solution.py:476
  169.8 10.8 %collective-permute-start.36 = (bf16[3,288,128]{2,1,0:T(8,128)(2,1)S(1)}, bf16[3,288,128]{2,1,0:T(8,128)(2,1)S(1)}, u32[]{:S(2)}, u32[]{:S(2)}) collective-permute-start(bf16[3,288,128]{2,1,0:T(8,128)(2,1)S(1)} %add_convert_fusion.2.refs_2_), channel_id=1, source_target_pairs={{0,2},{1,3},{2,0},{3,1},{4,6},{5,7},{6,4},{7,5},{8,10},{9,11},{10,... | collective-permute-start | bytes 663560 | tf_op jit(solution)/shard_map/ppermute | solution.py:395
  183.2 1.4 collective-permute-start.37
  184.6 4.6 %collective-permute-start.38 = (bf16[3,96,128]{2,1,0:T(8,128)(2,1)S(1)}, bf16[3,96,128]{2,1,0:T(8,128)(2,1)S(1)}, u32[]{:S(2)}, u32[]{:S(2)}) collective-permute-start(bf16[3,96,128]{2,1,0:T(8,128)(2,1)S(1)} %add_convert_fusion.3.refs_4_), channel_id=1, source_target_pairs={{0,2},{1,3},{2,0},{3,1},{4,6},{5,7},{6,4},{7,5},{8,10},{9,11},{10,... | collective-permute-start | bytes 221192 | tf_op jit(solution)/shard_map/ppermute | solution.py:395
  189.2 2.3 %copy-start = (bf16[3,768,1024]{2,1,0:T(8,128)(2,1)S(1)}, bf16[3,768,1024]{2,1,0:T(8,128)(2,1)}, u32[]{:S(2)}) copy-start(bf16[3,768,1024]{2,1,0:T(8,128)(2,1)} %get-tuple-element.126.refs_6_.refs_4_) | copy-start | bytes 14155780
  191.5 23.7 %copy-start.2 = (bf16[4,224,1024]{2,1,0:T(8,128)(2,1)S(1)}, bf16[4,224,1024]{2,1,0:T(8,128)(2,1)}, u32[]{:S(2)}) copy-start(bf16[4,224,1024]{2,1,0:T(8,128)(2,1)} %get-tuple-element.124.in_ref) | copy-start | bytes 5505028
  191.5 25.3 %copy-start.1 = (bf16[3,768,1024]{2,1,0:T(8,128)(2,1)S(1)}, bf16[3,768,1024]{2,1,0:T(8,128)(2,1)}, u32[]{:S(2)}) copy-start(bf16[3,768,1024]{2,1,0:T(8,128)(2,1)} %get-tuple-element.126.refs_6_.refs_4_) | copy-start | bytes 14155780
  203.9 2.1 collective-permute-start.39
  206.1 9.1 %collective-permute-start.40 = (bf16[3,384,128]{2,1,0:T(8,128)(2,1)S(1)}, bf16[3,384,128]{2,1,0:T(8,128)(2,1)S(1)}, u32[]{:S(2)}, u32[]{:S(2)}) collective-permute-start(bf16[3,384,128]{2,1,0:T(8,128)(2,1)S(1)} %add_convert_fusion.refs_0_), channel_id=1, source_target_pairs={{0,2},{1,3},{2,0},{3,1},{4,6},{5,7},{6,4},{7,5},{8,10},{9,11},{10,... | collective-permute-start | bytes 884744 | tf_op jit(solution)/shard_map/ppermute | solution.py:395
  207.9 8.6 %collective-permute-start.41 = (bf16[3,384,128]{2,1,0:T(8,128)(2,1)S(1)}, bf16[3,384,128]{2,1,0:T(8,128)(2,1)S(1)}, u32[]{:S(2)}, u32[]{:S(2)}) collective-permute-start(bf16[3,384,128]{2,1,0:T(8,128)(2,1)S(1)} %add_convert_fusion.refs_0_), channel_id=1, source_target_pairs={{0,1},{1,0},{2,3},{3,2},{4,5},{5,4},{6,7},{7,6},{8,9},{9,8},{10,11... | collective-permute-start | bytes 884744 | tf_op jit(solution)/shard_map/ppermute | solution.py:395
  215.2 1.6 collective-permute-start.42
where the time goes:
time: 231 us; the launch traced here: 229 us
  starting transfers between devices  100 us (43%)
  Pallas kernels  81.5 us (35%)
  waiting for transfers between devices  37.7 us (16%)
  local copies, waits for them, and re-layouts  5.76 us (2%)
  other arithmetic  2.68 us (1%)
    ppermute x8, starting transfers between devices, merge_folded(): arrived[c + lead] = lax.ppermute(copied[0], 'exp', inwards)  62.6 us
    pallas_call x10, Pallas kernels, residual_chunk(): pl.pallas_call(residual_kernel, grid_spec=pltpu.PrefetchScalarGridSpec(nu...  34.6 us
    ppermute x10, waiting for transfers between devices, merge_folded(): moved[c] = lax.ppermute(leaving, 'exp', outwards)  20.5 us
    pallas_call x10, Pallas kernels, cluster_sums(): pl.pallas_call(functools.partial(sums_kernel, ahead is not None), grid_sp...  16.2 us
    ppermute x10, waiting for transfers between devices, swap(): return lax.ppermute(value, 'col', [(i, i ^ bit) for i in range(size)])  13.5 us
    ppermute x10, starting transfers between devices, merge_folded(): moved[c] = lax.ppermute(leaving, 'exp', outwards)  13.1 us
    pallas_call x1, Pallas kernels, power_step(): pl.pallas_call(functools.partial(power_kernel, splits, pieces), in_specs=...  12.4 us
    pallas_call x1, Pallas kernels, project(): pl.pallas_call(project_kernel, in_specs=[SMEM] + [vmem] * (len(mine) + le...  12.4 us
  transfers between devices with their start and end apart: 43, of which 10 were waited for; matrix products, arithmetic and copies ran while one was open for 2% of the time, Pallas kernels for 24%

commit v1 on v0

--- a/solution.py
+++ b/solution.py
@@ -426,8 +426,6 @@
     partner = lax.dynamic_slice_in_dim(member_mask, (place ^ 1) * experts, experts)
     mask = jnp.concatenate([mine, partner], axis=0)
     meta = jnp.concatenate([jnp.argmax(mine, axis=1).astype(jnp.int32), inner, place[None]])
-    opening = weights[:, : UNIT]
-    fisher, opening = lax.optimization_barrier((fisher, opening))
     near = [fisher.astype(jnp.float32)]
     for hop in (1, 2, 3):
         pairs = [(i, i ^ hop) for i in range(4)]
@@ -438,7 +436,7 @@
         denom = denom + jnp.sum(value[:, :, None] * rows[:, None, :], axis=0)
     fcols = jnp.concatenate(near[:2], axis=0).T
 
-    chunks = [(0, 1), (0, 2), (0, 3), (3, 3), (3, 3), (1, 3), (1, 3), (2, 3), (2, 2), (2, 1)]
+    chunks = [(0, 2), (0, 2), (0, 2), (3, 3), (3, 3), (1, 3), (1, 3), (2, 3), (2, 2), (2, 1)]
     groups = [(0, 1, 2, 3, 4), (5, 6, 7), (8, 9)]
     lead, lag = 2, 2
     spans, used = [], [0] * 4
@@ -450,7 +448,7 @@
     arrived, sums, others, base, moved, firsts = {}, {}, {}, {}, {}, {}
     held, after, terms, ready = (), (), [], {}
     for c in range(lead):
-        block = weights[:, spans[c][0] : sum(spans[c])] if c else opening
+        block = weights[:, spans[c][0] : sum(spans[c])]
         arrived[c] = lax.ppermute(block, "exp", inwards)
     order = []
     for step in range(count):

time: 231 us -> 232 us (level)
  starting transfers between devices: 100 us -> 103 us
    ppermute x2, waiting for transfers between devices: 0.01 us -> 4.6 us  [merge_folded(): arrived[c] = lax.ppermute(block, 'exp', inwards)]
    ppermute x8, waiting for transfers between devices: 3.6 us -> 0.02 us  [merge_folded(): arrived[c + lead] = lax.ppermute(copied[0], 'exp', inwards)]
    ppermute x8, starting transfers between devices: 62.6 us -> 65.4 us  [merge_folded(): arrived[c + lead] = lax.ppermute(copied[0], 'exp', inwards)]
  transfers between devices with their start and end apart: 43 -> 43, of which waited for: 10 -> 9; matrix products, arithmetic and copies ran while one was open for 2% -> 3% of each run, Pallas kernels for 24% -> 23%
where the time goes in v1:
time: 232 us; the launch traced here: 231 us
  starting transfers between devices  103 us (44%)
  Pallas kernels  80.4 us (35%)
  waiting for transfers between devices  37.6 us (16%)
  local copies, waits for them, and re-layouts  5.72 us (2%)
  other arithmetic  2.67 us (1%)
    ppermute x8, starting transfers between devices, merge_folded(): arrived[c + lead] = lax.ppermute(copied[0], 'exp', inwards)  65.4 us
    pallas_call x10, Pallas kernels, residual_chunk(): pl.pallas_call(residual_kernel, grid_spec=pltpu.PrefetchScalarGridSpec(nu...  34.3 us
    ppermute x10, waiting for transfers between devices, merge_folded(): moved[c] = lax.ppermute(leaving, 'exp', outwards)  19.4 us
    pallas_call x10, Pallas kernels, cluster_sums(): pl.pallas_call(functools.partial(sums_kernel, ahead is not None), grid_sp...  15.4 us
    ppermute x10, waiting for transfers between devices, swap(): return lax.ppermute(value, 'col', [(i, i ^ bit) for i in range(size)])  13.5 us
    ppermute x10, starting transfers between devices, merge_folded(): moved[c] = lax.ppermute(leaving, 'exp', outwards)  12.9 us
    pallas_call x1, Pallas kernels, power_step(): pl.pallas_call(functools.partial(power_kernel, splits, pieces), in_specs=...  12.4 us
    pallas_call x1, Pallas kernels, project(): pl.pallas_call(project_kernel, in_specs=[SMEM] + [vmem] * (len(mine) + le...  12.4 us
  transfers between devices with their start and end apart: 43, of which 9 were waited for; matrix products, arithmetic and copies ran while one was open for 3% of the time, Pallas kernels for 23%

profile of v1, /device:TPU:0, one launch (start us, length us, event | category | flops | bytes accessed | tf_op | source)
XLA Modules:
  0.0 230.7 jit_solution(5963246394053662143)
XLA Ops:
  0.6 3.1 %collective-permute-start.1 = (bf16[3,768]{1,0:T(4,128)(2,1)}, bf16[3,768]{1,0:T(4,128)(2,1)S(1)}, u32[]{:S(2)}, u32[]{:S(2)}) collective-permute-start(bf16[3,768]{1,0:T(4,128)(2,1)} %param.5), channel_id=1, source_target_pairs={{0,4},{4,0},{8,12},{12,8},{1,5},{5,1},{9,13},{13,9},{2,6},{6,2},{1... | collective-permute-start | bytes 13832 | tf_op jit(solution)/shard_map/ppermute | solution.py:432
  3.7 2.6 %collective-permute-start.5 = (bf16[3,768]{1,0:T(4,128)(2,1)}, bf16[3,768]{1,0:T(4,128)(2,1)S(1)}, u32[]{:S(2)}, u32[]{:S(2)}) collective-permute-start(bf16[3,768]{1,0:T(4,128)(2,1)} %param.5), channel_id=1, source_target_pairs={{0,8},{4,12},{8,0},{12,4},{1,9},{5,13},{9,1},{13,5},{2,10},{6,14},... | collective-permute-start | bytes 13832 | tf_op jit(solution)/shard_map/ppermute | solution.py:432
  6.3 1.9 fusion
  8.2 2.8 %collective-permute-start.2 = (bf16[3,64,1024]{2,1,0:T(8,128)(2,1)}, bf16[3,64,1024]{2,1,0:T(8,128)(2,1)S(1)}, u32[]{:S(2)}, u32[]{:S(2)}) collective-permute-start(bf16[3,64,1024]{2,1,0:T(8,128)(2,1)} %get-tuple-element.127), channel_id=1, source_target_pairs={{0,4},{12,8},{1,5},{13,9},{2,6},{14,10},{3,7},{15,11},{16,20},{28,... | collective-permute-start | bytes 1179656 | tf_op jit(solution)/shard_map/ppermute | solution.py:452
  11.1 1.3 collective-permute-start
  16.3 4.6 %collective-permute-done.2.a_ref = bf16[3,64,1024]{2,1,0:T(8,128)(2,1)S(1)} collective-permute-done((bf16[3,64,1024]{2,1,0:T(8,128)(2,1)}, bf16[3,64,1024]{2,1,0:T(8,128)(2,1)S(1)}, u32[]{:S(2)}, u32[]{:S(2)}) %collective-permute-start.2) | collective-permute-done | bytes 393248 | tf_op jit(solution)/shard_map/ppermute | solution.py:452
  22.9 8.1 %collective-permute-start.9 = (bf16[3,64,1024]{2,1,0:T(8,128)(2,1)S(1)}, bf16[3,64,1024]{2,1,0:T(8,128)(2,1)S(1)}, u32[]{:S(2)}, u32[]{:S(2)}) collective-permute-start(bf16[3,64,1024]{2,1,0:T(8,128)(2,1)S(1)} %get-tuple-element.70), channel_id=1, source_target_pairs={{0,4},{12,8},{1,5},{13,9},{2,6},{14,10},{3,7},{15,11},{16,20},{28,... | collective-permute-start | bytes 1179656 | tf_op jit(solution)/shard_map/ppermute | solution.py:467
  31.0 1.4 shard_map.68
  33.1 5.9 %collective-permute-start.3 = (bf16[3,96,1024]{2,1,0:T(8,128)(2,1)S(1)}, bf16[3,96,1024]{2,1,0:T(8,128)(2,1)S(1)}, u32[]{:S(2)}, u32[]{:S(2)}) collective-permute-start(bf16[3,96,1024]{2,1,0:T(8,128)(2,1)S(1)} %get-tuple-element.68), channel_id=1, source_target_pairs={{0,4},{12,8},{1,5},{13,9},{2,6},{14,10},{3,7},{15,11},{16,20},{28,... | collective-permute-start | bytes 1769480 | tf_op jit(solution)/shard_map/ppermute | solution.py:467
  40.5 1.4 shard_map.70
  43.0 1.3 collective-permute-start.13
  44.3 10.5 %collective-permute-start.15 = (bf16[3,96,1024]{2,1,0:T(8,128)(2,1)S(1)}, bf16[3,96,1024]{2,1,0:T(8,128)(2,1)S(1)}, u32[]{:S(2)}, u32[]{:S(2)}) collective-permute-start(bf16[3,96,1024]{2,1,0:T(8,128)(2,1)S(1)} %get-tuple-element.79), channel_id=1, source_target_pairs={{0,4},{12,8},{1,5},{13,9},{2,6},{14,10},{3,7},{15,11},{16,20},{28,... | collective-permute-start | bytes 1769480 | tf_op jit(solution)/shard_map/ppermute | solution.py:467
  54.8 3.0 %shard_map.72 = (bf16[3,768,1024]{2,1,0:T(8,128)(2,1)}, bf16[4,224,1024]{2,1,0:T(8,128)(2,1)}, f32[3,64,128]{2,1,0:T(8,128)S(1)}) custom-call(s32[5]{0:T(128)S(1)} %pad_add_fusion.meta, bf16[3,768,1024]{2,1,0:T(8,128)(2,1)} %w_ref.39, bf16[4,64,1024]{2,1,0:T(8,128)(2,1)S(1)} %shard_map.69.refs_1_.b_ref, ...), custom_call_target="tpu_custom_call" | custom-call | flops 10000000000 | bytes 1 | tf_op jit(solution)/shard_map/pallas_call | solution.py:195
  57.8 2.2 shard_map.73
  62.2 5.8 %collective-permute-start.10 = (bf16[3,96,1024]{2,1,0:T(8,128)(2,1)S(1)}, bf16[3,96,1024]{2,1,0:T(8,128)(2,1)S(1)}, u32[]{:S(2)}, u32[]{:S(2)}) collective-permute-start(bf16[3,96,1024]{2,1,0:T(8,128)(2,1)S(1)} %get-tuple-element.73), channel_id=1, source_target_pairs={{0,4},{12,8},{1,5},{13,9},{2,6},{14,10},{3,7},{15,11},{16,20},{28,... | collective-permute-start | bytes 1769480 | tf_op jit(solution)/shard_map/ppermute | solution.py:467
  68.1 3.0 %shard_map.75 = (bf16[3,768,1024]{2,1,0:T(8,128)(2,1)}, bf16[4,224,1024]{2,1,0:T(8,128)(2,1)}, f32[3,64,128]{2,1,0:T(8,128)S(1)}) custom-call(s32[5]{0:T(128)S(1)} %pad_add_fusion.meta, bf16[3,768,1024]{2,1,0:T(8,128)(2,1)} %w_ref.39, bf16[4,64,1024]{2,1,0:T(8,128)(2,1)S(1)} %shard_map.71.refs_0_.b_ref, ...), custom_call_target="tpu_custom_call", output_to_operand_aliasing={{0}: (5, {}), {1}: (6, {})} | custom-call | flops 10000000000 | bytes 1 | tf_op jit(solution)/shard_map/pallas_call | solution.py:195
  71.1 2.2 shard_map.76
  74.0 4.3 %collective-permute-start.21 = (bf16[3,96,1024]{2,1,0:T(8,128)(2,1)S(1)}, bf16[3,96,1024]{2,1,0:T(8,128)(2,1)S(1)}, u32[]{:S(2)}, u32[]{:S(2)}) collective-permute-start(bf16[3,96,1024]{2,1,0:T(8,128)(2,1)S(1)} %get-tuple-element.89), channel_id=1, source_target_pairs={{0,4},{12,8},{1,5},{13,9},{2,6},{14,10},{3,7},{15,11},{16,20},{28,... | collective-permute-start | bytes 1769480 | tf_op jit(solution)/shard_map/ppermute | solution.py:467
  79.9 3.0 %shard_map.78 = (bf16[3,768,1024]{2,1,0:T(8,128)(2,1)}, bf16[4,224,1024]{2,1,0:T(8,128)(2,1)}, f32[3,64,128]{2,1,0:T(8,128)S(1)}) custom-call(s32[5]{0:T(128)S(1)} %pad_add_fusion.meta, bf16[3,768,1024]{2,1,0:T(8,128)(2,1)} %w_ref.39, bf16[4,64,1024]{2,1,0:T(8,128)(2,1)S(1)} %shard_map.74.refs_2_.b_ref, ...), custom_call_target="tpu_custom_call", output_to_operand_aliasing={{0}: (5, {}), {1}: (6, {})} | custom-call | flops 10000000000 | bytes 1 | tf_op jit(solution)/shard_map/pallas_call | solution.py:195
  82.9 2.2 shard_map.79
  85.9 9.9 %collective-permute-start.16 = (bf16[3,96,1024]{2,1,0:T(8,128)(2,1)S(1)}, bf16[3,96,1024]{2,1,0:T(8,128)(2,1)S(1)}, u32[]{:S(2)}, u32[]{:S(2)}) collective-permute-start(bf16[3,96,1024]{2,1,0:T(8,128)(2,1)S(1)} %get-tuple-element.83), channel_id=1, source_target_pairs={{0,4},{12,8},{1,5},{13,9},{2,6},{14,10},{3,7},{15,11},{16,20},{28,... | collective-permute-start | bytes 1769480 | tf_op jit(solution)/shard_map/ppermute | solution.py:467
  97.4 3.9 %shard_map.81 = (bf16[3,768,1024]{2,1,0:T(8,128)(2,1)}, bf16[4,224,1024]{2,1,0:T(8,128)(2,1)}, f32[3,96,128]{2,1,0:T(8,128)S(1)}) custom-call(s32[5]{0:T(128)S(1)} %pad_add_fusion.meta, bf16[3,768,1024]{2,1,0:T(8,128)(2,1)} %w_ref.39, bf16[4,96,1024]{2,1,0:T(8,128)(2,1)S(1)} %shard_map.77.refs_2_.b_ref, ...), custom_call_target="tpu_custom_call", output_to_operand_aliasing={{0}: (5, {}), {1}: (6, {})} | custom-call | flops 10000000000 | bytes 1 | tf_op jit(solution)/shard_map/pallas_call | solution.py:195
  101.3 1.4 shard_map.82
  105.6 13.9 %collective-permute-start.27 = (bf16[3,64,1024]{2,1,0:T(8,128)(2,1)S(1)}, bf16[3,64,1024]{2,1,0:T(8,128)(2,1)S(1)}, u32[]{:S(2)}, u32[]{:S(2)}) collective-permute-start(bf16[3,64,1024]{2,1,0:T(8,128)(2,1)S(1)} %get-tuple-element.103), channel_id=1, source_target_pairs={{0,4},{12,8},{1,5},{13,9},{2,6},{14,10},{3,7},{15,11},{16,20},{28,... | collective-permute-start | bytes 1179656 | tf_op jit(solution)/shard_map/ppermute | solution.py:467
  119.5 4.0 %shard_map.84 = (bf16[3,768,1024]{2,1,0:T(8,128)(2,1)}, bf16[4,224,1024]{2,1,0:T(8,128)(2,1)}, f32[3,96,128]{2,1,0:T(8,128)S(1)}) custom-call(s32[5]{0:T(128)S(1)} %pad_add_fusion.meta, bf16[3,768,1024]{2,1,0:T(8,128)(2,1)} %w_ref.39, bf16[4,96,1024]{2,1,0:T(8,128)(2,1)S(1)} %shard_map.80.refs_2_.b_ref, ...), custom_call_target="tpu_custom_call", output_to_operand_aliasing={{0}: (5, {}), {1}: (6, {})} | custom-call | flops 10000000000 | bytes 1 | tf_op jit(solution)/shard_map/pallas_call | solution.py:195
  123.6 1.3 shard_map.85
  125.6 6.9 %collective-permute-start.22 = (bf16[3,32,1024]{2,1,0:T(8,128)(2,1)S(1)}, bf16[3,32,1024]{2,1,0:T(8,128)(2,1)S(1)}, u32[]{:S(2)}, u32[]{:S(2)}) collective-permute-start(bf16[3,32,1024]{2,1,0:T(8,128)(2,1)S(1)} %get-tuple-element.94), channel_id=1, source_target_pairs={{0,4},{12,8},{1,5},{13,9},{2,6},{14,10},{3,7},{15,11},{16,20},{28,... | collective-permute-start | bytes 589832 | tf_op jit(solution)/shard_map/ppermute | solution.py:467
  132.6 1.6 collective-permute-start.29
  134.9 1.3 collective-permute-start.24
  136.2 4.0 %shard_map.87 = (bf16[3,768,1024]{2,1,0:T(8,128)(2,1)}, bf16[4,224,1024]{2,1,0:T(8,128)(2,1)}, f32[3,96,128]{2,1,0:T(8,128)S(1)}) custom-call(s32[5]{0:T(128)S(1)} %pad_add_fusion.meta, bf16[3,768,1024]{2,1,0:T(8,128)(2,1)} %w_ref.39, bf16[4,96,1024]{2,1,0:T(8,128)(2,1)S(1)} %get-tuple-element.92.refs_2_.b_ref, ...), custom_call_target="tpu_custom_call", output_to_operand_aliasing={{0}: (5, {}), {1}: (6, {})} | custom-call | flops 10000000000 | bytes 1 | tf_op jit(solution)/shard_map/pallas_call | solution.py:195
  144.1 7.5 %collective-permute-done.24.r_ref = bf16[3,96,1024]{2,1,0:T(8,128)(2,1)S(1)} collective-permute-done((bf16[3,96,1024]{2,1,0:T(8,128)(2,1)S(1)}, bf16[3,96,1024]{2,1,0:T(8,128)(2,1)S(1)}, u32[]{:S(2)}, u32[]{:S(2)}) %collective-permute-start.24) | collective-permute-done | bytes 589856 | tf_op jit(solution)/shard_map/ppermute | solution.py:474
  151.7 3.9 %shard_map.90 = (bf16[3,768,1024]{2,1,0:T(8,128)(2,1)}, bf16[4,224,1024]{2,1,0:T(8,128)(2,1)}, f32[3,96,128]{2,1,0:T(8,128)S(1)}) custom-call(s32[5]{0:T(128)S(1)} %pad_add_fusion.meta, bf16[3,768,1024]{2,1,0:T(8,128)(2,1)} %w_ref.39, bf16[4,96,1024]{2,1,0:T(8,128)(2,1)S(1)} %get-tuple-element.96.refs_2_.b_ref, ...), custom_call_target="tpu_custom_call", output_to_operand_aliasing={{0}: (5, {}), {1}: (6, {})} | custom-call | flops 10000000000 | bytes 1 | tf_op jit(solution)/shard_map/pallas_call | solution.py:195
  159.5 5.8 %collective-permute-done.31.r_ref = bf16[3,96,1024]{2,1,0:T(8,128)(2,1)S(1)} collective-permute-done((bf16[3,96,1024]{2,1,0:T(8,128)(2,1)S(1)}, bf16[3,96,1024]{2,1,0:T(8,128)(2,1)S(1)}, u32[]{:S(2)}, u32[]{:S(2)}) %collective-permute-start.31) | collective-permute-done | bytes 589856 | tf_op jit(solution)/shard_map/ppermute | solution.py:474
  165.4 4.0 %shard_map.93 = (bf16[3,768,1024]{2,1,0:T(8,128)(2,1)}, bf16[4,224,1024]{2,1,0:T(8,128)(2,1)}, f32[3,96,128]{2,1,0:T(8,128)S(1)}) custom-call(s32[5]{0:T(128)S(1)} %pad_add_fusion.meta, bf16[3,768,1024]{2,1,0:T(8,128)(2,1)} %w_ref.39, bf16[4,96,1024]{2,1,0:T(8,128)(2,1)S(1)} %get-tuple-element.105.refs_2_.b_ref, ...), custom_call_target="tpu_custom_call", output_to_operand_aliasing={{0}: (5, {}), {1}: (6, {})} | custom-call | flops 10000000000 | bytes 1 | tf_op jit(solution)/shard_map/pallas_call | solution.py:195
  171.4 1.8 collective-permute-start.36
  173.2 6.0 %collective-permute-done.33.refs_3_.r_ref = bf16[3,32,1024]{2,1,0:T(8,128)(2,1)S(1)} collective-permute-done((bf16[3,32,1024]{2,1,0:T(8,128)(2,1)S(1)}, bf16[3,32,1024]{2,1,0:T(8,128)(2,1)S(1)}, u32[]{:S(2)}, u32[]{:S(2)}) %collective-permute-start.33) | collective-permute-done | bytes 196640 | tf_op jit(solution)/shard_map/ppermute | solution.py:474
  179.2 3.0 %shard_map.95 = (bf16[3,768,1024]{2,1,0:T(8,128)(2,1)}, bf16[4,224,1024]{2,1,0:T(8,128)(2,1)}, f32[3,64,128]{2,1,0:T(8,128)S(1)}) custom-call(s32[5]{0:T(128)S(1)} %pad_add_fusion.meta, bf16[3,768,1024]{2,1,0:T(8,128)(2,1)} %w_ref.39, bf16[4,64,1024]{2,1,0:T(8,128)(2,1)S(1)} %get-tuple-element.110.refs_2_.b_ref, ...), custom_call_target="tpu_custom_call", output_to_operand_aliasing={{0}: (5, {}), {1}: (6, {})} | custom-call | flops 10000000000 | bytes 1 | tf_op jit(solution)/shard_map/pallas_call | solution.py:195
  182.2 2.6 %shard_map.96 = (bf16[3,768,1024]{2,1,0:T(8,128)(2,1)}, bf16[4,224,1024]{2,1,0:T(8,128)(2,1)}, f32[3,32,128]{2,1,0:T(8,128)S(1)}) custom-call(s32[5]{0:T(128)S(1)} %pad_add_fusion.meta, bf16[3,768,1024]{2,1,0:T(8,128)(2,1)} %w_ref.39, bf16[4,32,1024]{2,1,0:T(8,128)(2,1)S(1)} %get-tuple-element.112.refs_2_.b_ref, ...), custom_call_target="tpu_custom_call", output_to_operand_aliasing={{0}: (5, {}), {1}: (6, {})} | custom-call | flops 10000000000 | bytes 1 | tf_op jit(solution)/shard_map/pallas_call | solution.py:195
  184.8 1.4 collective-permute-done.37
  186.2 1.8 collective-permute-start.38
  188.0 2.6 %collective-permute-done.38.refs_5_ = bf16[3,96,128]{2,1,0:T(8,128)(2,1)S(1)} collective-permute-done((bf16[3,96,128]{2,1,0:T(8,128)(2,1)S(1)}, bf16[3,96,128]{2,1,0:T(8,128)(2,1)S(1)}, u32[]{:S(2)}, u32[]{:S(2)}) %collective-permute-start.38) | collective-permute-done | bytes 73760 | tf_op jit(solution)/shard_map/ppermute | solution.py:395
  190.6 2.3 %copy-done = bf16[3,768,1024]{2,1,0:T(8,128)(2,1)S(1)} copy-done((bf16[3,768,1024]{2,1,0:T(8,128)(2,1)S(1)}, bf16[3,768,1024]{2,1,0:T(8,128)(2,1)}, u32[]{:S(2)}) %copy-start) | copy-done | bytes 4718616
  192.9 12.4 %shard_map.98 = (f32[3,384,128]{2,1,0:T(8,128)S(1)}, f32[3,384,128]{2,1,0:T(8,128)S(1)}) custom-call(s32[1]{0:T(128)} %bitcast.3.side, bf16[3,384,128]{2,1,0:T(8,128)(2,1)S(1)} %add_convert_fusion.1.refs_0_, bf16[3,384,128]{2,1,0:T(8,128)(2,1)S(1)} %collective-permute-done.29.refs_3_.refs_1_, bf16[3,288,128]{2,1,0:T(8,128)(2,1)S(1)} %add_convert_fusion.2.refs_2_, ...), custom_call_target="tpu_custom_call" | custom-call | tf_op jit(solution)/shard_map/pallas_call | solution.py:339
  205.4 2.0 collective-permute-done.39
  207.5 1.8 collective-permute-start.40
  209.3 7.3 %collective-permute-done.40.refs_1_ = bf16[3,384,128]{2,1,0:T(8,128)(2,1)S(1)} collective-permute-done((bf16[3,384,128]{2,1,0:T(8,128)(2,1)S(1)}, bf16[3,384,128]{2,1,0:T(8,128)(2,1)S(1)}, u32[]{:S(2)}, u32[]{:S(2)}) %collective-permute-start.40) | collective-permute-done | bytes 294944 | tf_op jit(solution)/shard_map/ppermute | solution.py:395
  216.6 1.3 shard_map.97
  218.2 12.4 %shard_map.99 = (bf16[3,768,128]{2,1,0:T(8,128)(2,1)}, bf16[3,128,1024]{2,1,0:T(8,128)(2,1)}) custom-call(s32[1]{0:T(128)} %bitcast.3.side, bf16[3,384,128]{2,1,0:T(8,128)(2,1)S(1)} %add_convert_fusion.refs_0_, bf16[3,384,128]{2,1,0:T(8,128)(2,1)S(1)} %collective-permute-done.40.refs_1_, bf16[3,384,128]{2,1,0:T(8,128)(2,1)S(1)} %collective-permute-done.41.refs_2_, ...), custom_call_target="tpu_custom_call" | custom-call | tf_op jit(solution)/shard_map/pallas_call | solution.py:377
  (115 shorter events, 30.3 us)
Async XLA Ops:
  0.6 14.7 %collective-permute-start.1 = (bf16[3,768]{1,0:T(4,128)(2,1)}, bf16[3,768]{1,0:T(4,128)(2,1)S(1)}, u32[]{:S(2)}, u32[]{:S(2)}) collective-permute-start(bf16[3,768]{1,0:T(4,128)(2,1)} %param.5), channel_id=1, source_target_pairs={{0,4},{4,0},{8,12},{12,8},{1,5},{5,1},{9,13},{13,9},{2,6},{6,2},{1... | collective-permute-start | bytes 13832 | tf_op jit(solution)/shard_map/ppermute | solution.py:432
  3.7 11.7 %collective-permute-start.5 = (bf16[3,768]{1,0:T(4,128)(2,1)}, bf16[3,768]{1,0:T(4,128)(2,1)S(1)}, u32[]{:S(2)}, u32[]{:S(2)}) collective-permute-start(bf16[3,768]{1,0:T(4,128)(2,1)} %param.5), channel_id=1, source_target_pairs={{0,8},{4,12},{8,0},{12,4},{1,9},{5,13},{9,1},{13,5},{2,10},{6,14},... | collective-permute-start | bytes 13832 | tf_op jit(solution)/shard_map/ppermute | solution.py:432
  6.3 9.7 %collective-permute-start.6 = (bf16[3,768]{1,0:T(4,128)(2,1)}, bf16[3,768]{1,0:T(4,128)(2,1)S(1)}, u32[]{:S(2)}, u32[]{:S(2)}) collective-permute-start(bf16[3,768]{1,0:T(4,128)(2,1)} %param.5), channel_id=1, source_target_pairs={{0,12},{4,8},{8,4},{12,0},{1,13},{5,9},{9,5},{13,1},{2,14},{6,10},... | collective-permute-start | bytes 13832 | tf_op jit(solution)/shard_map/ppermute | solution.py:432
  8.2 12.7 %collective-permute-start.2 = (bf16[3,64,1024]{2,1,0:T(8,128)(2,1)}, bf16[3,64,1024]{2,1,0:T(8,128)(2,1)S(1)}, u32[]{:S(2)}, u32[]{:S(2)}) collective-permute-start(bf16[3,64,1024]{2,1,0:T(8,128)(2,1)} %get-tuple-element.127), channel_id=1, source_target_pairs={{0,4},{12,8},{1,5},{13,9},{2,6},{14,10},{3,7},{15,11},{16,20},{28,... | collective-permute-start | bytes 1179656 | tf_op jit(solution)/shard_map/ppermute | solution.py:452
  11.1 20.0 %collective-permute-start = (bf16[3,64,1024]{2,1,0:T(8,128)(2,1)S(1)}, bf16[3,64,1024]{2,1,0:T(8,128)(2,1)S(1)}, u32[]{:S(2)}, u32[]{:S(2)}) collective-permute-start(bf16[3,64,1024]{2,1,0:T(8,128)(2,1)S(1)} %get-tuple-element.128), channel_id=1, source_target_pairs={{0,4},{12,8},{1,5},{13,9},{2,6},{14,10},{3,7},{15,11},{16,20},{28,... | collective-permute-start | bytes 1179656 | tf_op jit(solution)/shard_map/ppermute | solution.py:452
  22.2 16.9 %collective-permute-start.4 = (bf16[4,64,1024]{2,1,0:T(8,128)(2,1)S(1)}, bf16[4,64,1024]{2,1,0:T(8,128)(2,1)S(1)}, u32[]{:S(2)}, u32[]{:S(2)}) collective-permute-start(bf16[4,64,1024]{2,1,0:T(8,128)(2,1)S(1)} %get-tuple-element.67.refs_1_.refs_0_), channel_id=1, source_target_pairs={{4,8},{8,4},{5,9},{9,5},{6,10},{10,6},{7,11},{11,7},{20,24},{24,20... | collective-permute-start | bytes 1572872 | tf_op jit(solution)/shard_map/ppermute | solution.py:465
  22.9 17.7 %collective-permute-start.9 = (bf16[3,64,1024]{2,1,0:T(8,128)(2,1)S(1)}, bf16[3,64,1024]{2,1,0:T(8,128)(2,1)S(1)}, u32[]{:S(2)}, u32[]{:S(2)}) collective-permute-start(bf16[3,64,1024]{2,1,0:T(8,128)(2,1)S(1)} %get-tuple-element.70), channel_id=1, source_target_pairs={{0,4},{12,8},{1,5},{13,9},{2,6},{14,10},{3,7},{15,11},{16,20},{28,... | collective-permute-start | bytes 1179656 | tf_op jit(solution)/shard_map/ppermute | solution.py:467
  32.4 10.4 %collective-permute-start.8 = (bf16[4,64,1024]{2,1,0:T(8,128)(2,1)S(1)}, bf16[4,64,1024]{2,1,0:T(8,128)(2,1)S(1)}, u32[]{:S(2)}, u32[]{:S(2)}) collective-permute-start(bf16[4,64,1024]{2,1,0:T(8,128)(2,1)S(1)} %get-tuple-element.69.refs_3_.refs_0_), channel_id=1, source_target_pairs={{4,8},{8,4},{5,9},{9,5},{6,10},{10,6},{7,11},{11,7},{20,24},{24,20... | collective-permute-start | bytes 1572872 | tf_op jit(solution)/shard_map/ppermute | solution.py:465
  33.1 24.7 %collective-permute-start.3 = (bf16[3,96,1024]{2,1,0:T(8,128)(2,1)S(1)}, bf16[3,96,1024]{2,1,0:T(8,128)(2,1)S(1)}, u32[]{:S(2)}, u32[]{:S(2)}) collective-permute-start(bf16[3,96,1024]{2,1,0:T(8,128)(2,1)S(1)} %get-tuple-element.68), channel_id=1, source_target_pairs={{0,4},{12,8},{1,5},{13,9},{2,6},{14,10},{3,7},{15,11},{16,20},{28,... | collective-permute-start | bytes 1769480 | tf_op jit(solution)/shard_map/ppermute | solution.py:467
  39.2 15.6 %collective-permute-start.7 = (bf16[4,64,1024]{2,1,0:T(8,128)(2,1)S(1)}, bf16[4,64,1024]{2,1,0:T(8,128)(2,1)S(1)}, u32[]{:S(2)}, u32[]{:S(2)}) collective-permute-start(bf16[4,64,1024]{2,1,0:T(8,128)(2,1)S(1)} %shard_map.69.refs_1_.b_ref), channel_id=1, source_target_pairs={{4,0},{8,12},{5,1},{9,13},{6,2},{10,14},{7,3},{11,15},{20,16},{24,... | collective-permute-start | bytes 1572872 | tf_op jit(solution)/shard_map/ppermute | solution.py:474
  41.9 12.9 %copy-start.3 = (bf16[3,1024,128]{2,1,0:T(8,128)(2,1)S(1)}, bf16[3,1024,128]{2,1,0:T(8,128)(2,1)}, u32[]{:S(2)}) copy-start(bf16[3,1024,128]{2,1,0:T(8,128)(2,1)} %s_ref.19) | copy-start | bytes 2359300
  41.9 18.8 %collective-permute-start.11 = (bf16[4,64,1024]{2,1,0:T(8,128)(2,1)S(1)}, bf16[4,64,1024]{2,1,0:T(8,128)(2,1)S(1)}, u32[]{:S(2)}, u32[]{:S(2)}) collective-permute-start(bf16[4,64,1024]{2,1,0:T(8,128)(2,1)S(1)} %get-tuple-element.71.refs_3_.refs_0_), channel_id=1, source_target_pairs={{4,8},{8,4},{5,9},{9,5},{6,10},{10,6},{7,11},{11,7},{20,24},{24,20... | collective-permute-start | bytes 1572872 | tf_op jit(solution)/shard_map/ppermute | solution.py:465
  43.0 25.1 %collective-permute-start.13 = (bf16[4,64,1024]{2,1,0:T(8,128)(2,1)S(1)}, bf16[4,64,1024]{2,1,0:T(8,128)(2,1)S(1)}, u32[]{:S(2)}, u32[]{:S(2)}) collective-permute-start(bf16[4,64,1024]{2,1,0:T(8,128)(2,1)S(1)} %shard_map.71.refs_0_.b_ref), channel_id=1, source_target_pairs={{4,0},{8,12},{5,1},{9,13},{6,2},{10,14},{7,3},{11,15},{20,16},{24,... | collective-permute-start | bytes 1572872 | tf_op jit(solution)/shard_map/ppermute | solution.py:474
  44.3 26.8 %collective-permute-start.15 = (bf16[3,96,1024]{2,1,0:T(8,128)(2,1)S(1)}, bf16[3,96,1024]{2,1,0:T(8,128)(2,1)S(1)}, u32[]{:S(2)}, u32[]{:S(2)}) collective-permute-start(bf16[3,96,1024]{2,1,0:T(8,128)(2,1)S(1)} %get-tuple-element.79), channel_id=1, source_target_pairs={{0,4},{12,8},{1,5},{13,9},{2,6},{14,10},{3,7},{15,11},{16,20},{28,... | collective-permute-start | bytes 1769480 | tf_op jit(solution)/shard_map/ppermute | solution.py:467
  60.0 18.4 %collective-permute-start.14 = (bf16[4,96,1024]{2,1,0:T(8,128)(2,1)S(1)}, bf16[4,96,1024]{2,1,0:T(8,128)(2,1)S(1)}, u32[]{:S(2)}, u32[]{:S(2)}) collective-permute-start(bf16[4,96,1024]{2,1,0:T(8,128)(2,1)S(1)} %get-tuple-element.74.refs_3_.refs_0_), channel_id=1, source_target_pairs={{4,8},{8,4},{5,9},{9,5},{6,10},{10,6},{7,11},{11,7},{20,24},{24,20... | collective-permute-start | bytes 2359304 | tf_op jit(solution)/shard_map/ppermute | solution.py:465
  60.9 19.0 %collective-permute-start.12 = (bf16[4,64,1024]{2,1,0:T(8,128)(2,1)S(1)}, bf16[4,64,1024]{2,1,0:T(8,128)(2,1)S(1)}, u32[]{:S(2)}, u32[]{:S(2)}) collective-permute-start(bf16[4,64,1024]{2,1,0:T(8,128)(2,1)S(1)} %shard_map.74.refs_2_.b_ref), channel_id=1, source_target_pairs={{4,0},{8,12},{5,1},{9,13},{6,2},{10,14},{7,3},{11,15},{20,16},{24,... | collective-permute-start | bytes 1572872 | tf_op jit(solution)/shard_map/ppermute | solution.py:474
  62.2 20.7 %collective-permute-start.10 = (bf16[3,96,1024]{2,1,0:T(8,128)(2,1)S(1)}, bf16[3,96,1024]{2,1,0:T(8,128)(2,1)S(1)}, u32[]{:S(2)}, u32[]{:S(2)}) collective-permute-start(bf16[3,96,1024]{2,1,0:T(8,128)(2,1)S(1)} %get-tuple-element.73), channel_id=1, source_target_pairs={{0,4},{12,8},{1,5},{13,9},{2,6},{14,10},{3,7},{15,11},{16,20},{28,... | collective-permute-start | bytes 1769480 | tf_op jit(solution)/shard_map/ppermute | solution.py:467
  73.3 22.5 %collective-permute-start.17 = (bf16[4,96,1024]{2,1,0:T(8,128)(2,1)S(1)}, bf16[4,96,1024]{2,1,0:T(8,128)(2,1)S(1)}, u32[]{:S(2)}, u32[]{:S(2)}) collective-permute-start(bf16[4,96,1024]{2,1,0:T(8,128)(2,1)S(1)} %get-tuple-element.81.refs_3_.refs_0_), channel_id=1, source_target_pairs={{4,8},{8,4},{5,9},{9,5},{6,10},{10,6},{7,11},{11,7},{20,24},{24,20... | collective-permute-start | bytes 2359304 | tf_op jit(solution)/shard_map/ppermute | solution.py:465
  74.0 27.2 %collective-permute-start.21 = (bf16[3,96,1024]{2,1,0:T(8,128)(2,1)S(1)}, bf16[3,96,1024]{2,1,0:T(8,128)(2,1)S(1)}, u32[]{:S(2)}, u32[]{:S(2)}) collective-permute-start(bf16[3,96,1024]{2,1,0:T(8,128)(2,1)S(1)} %get-tuple-element.89), channel_id=1, source_target_pairs={{0,4},{12,8},{1,5},{13,9},{2,6},{14,10},{3,7},{15,11},{16,20},{28,... | collective-permute-start | bytes 1769480 | tf_op jit(solution)/shard_map/ppermute | solution.py:467
  78.6 18.8 %collective-permute-start.19 = (bf16[4,96,1024]{2,1,0:T(8,128)(2,1)S(1)}, bf16[4,96,1024]{2,1,0:T(8,128)(2,1)S(1)}, u32[]{:S(2)}, u32[]{:S(2)}) collective-permute-start(bf16[4,96,1024]{2,1,0:T(8,128)(2,1)S(1)} %shard_map.77.refs_2_.b_ref), channel_id=1, source_target_pairs={{4,0},{8,12},{5,1},{9,13},{6,2},{10,14},{7,3},{11,15},{20,16},{24,... | collective-permute-start | bytes 2359304 | tf_op jit(solution)/shard_map/ppermute | solution.py:474
  85.2 18.3 %collective-permute-start.20 = (bf16[4,96,1024]{2,1,0:T(8,128)(2,1)S(1)}, bf16[4,96,1024]{2,1,0:T(8,128)(2,1)S(1)}, u32[]{:S(2)}, u32[]{:S(2)}) collective-permute-start(bf16[4,96,1024]{2,1,0:T(8,128)(2,1)S(1)} %get-tuple-element.84.refs_3_.p_ref), channel_id=1, source_target_pairs={{4,8},{8,4},{5,9},{9,5},{6,10},{10,6},{7,11},{11,7},{20,24},{24,20... | collective-permute-start | bytes 2359304 | tf_op jit(solution)/shard_map/ppermute | solution.py:465
  85.9 37.7 %collective-permute-start.16 = (bf16[3,96,1024]{2,1,0:T(8,128)(2,1)S(1)}, bf16[3,96,1024]{2,1,0:T(8,128)(2,1)S(1)}, u32[]{:S(2)}, u32[]{:S(2)}) collective-permute-start(bf16[3,96,1024]{2,1,0:T(8,128)(2,1)S(1)} %get-tuple-element.83), channel_id=1, source_target_pairs={{0,4},{12,8},{1,5},{13,9},{2,6},{14,10},{3,7},{15,11},{16,20},{28,... | collective-permute-start | bytes 1769480 | tf_op jit(solution)/shard_map/ppermute | solution.py:467
  96.0 23.4 %collective-permute-start.18 = (bf16[4,96,1024]{2,1,0:T(8,128)(2,1)S(1)}, bf16[4,96,1024]{2,1,0:T(8,128)(2,1)S(1)}, u32[]{:S(2)}, u32[]{:S(2)}) collective-permute-start(bf16[4,96,1024]{2,1,0:T(8,128)(2,1)S(1)} %shard_map.80.refs_2_.b_ref), channel_id=1, source_target_pairs={{4,0},{8,12},{5,1},{9,13},{6,2},{10,14},{7,3},{11,15},{20,16},{24,... | collective-permute-start | bytes 2359304 | tf_op jit(solution)/shard_map/ppermute | solution.py:474
  102.7 29.9 %collective-permute-start.23 = (bf16[4,96,1024]{2,1,0:T(8,128)(2,1)S(1)}, bf16[4,96,1024]{2,1,0:T(8,128)(2,1)S(1)}, u32[]{:S(2)}, u32[]{:S(2)}) collective-permute-start(bf16[4,96,1024]{2,1,0:T(8,128)(2,1)S(1)} %get-tuple-element.91.refs_0_.p_ref), channel_id=1, source_target_pairs={{4,8},{8,4},{5,9},{9,5},{6,10},{10,6},{7,11},{11,7},{20,24},{24,20... | collective-permute-start | bytes 2359304 | tf_op jit(solution)/shard_map/ppermute | solution.py:465
  104.3 30.7 %collective-permute-start.25 = (bf16[3,96,1024]{2,1,0:T(8,128)(2,1)S(1)}, bf16[3,96,1024]{2,1,0:T(8,128)(2,1)S(1)}, u32[]{:S(2)}, u32[]{:S(2)}) collective-permute-start(bf16[3,96,1024]{2,1,0:T(8,128)(2,1)S(1)} %get-tuple-element.98), channel_id=1, source_target_pairs={{4,0},{8,12},{5,1},{9,13},{6,2},{10,14},{7,3},{11,15},{20,16},{24,... | collective-permute-start | bytes 1769480 | tf_op jit(solution)/shard_map/ppermute | solution.py:474
  105.6 34.6 %collective-permute-start.27 = (bf16[3,64,1024]{2,1,0:T(8,128)(2,1)S(1)}, bf16[3,64,1024]{2,1,0:T(8,128)(2,1)S(1)}, u32[]{:S(2)}, u32[]{:S(2)}) collective-permute-start(bf16[3,64,1024]{2,1,0:T(8,128)(2,1)S(1)} %get-tuple-element.103), channel_id=1, source_target_pairs={{0,4},{12,8},{1,5},{13,9},{2,6},{14,10},{3,7},{15,11},{16,20},{28,... | collective-permute-start | bytes 1179656 | tf_op jit(solution)/shard_map/ppermute | solution.py:467
  123.5 2.1 collective-permute-start.28
  124.9 17.1 %collective-permute-start.26 = (bf16[4,96,1024]{2,1,0:T(8,128)(2,1)S(1)}, bf16[4,96,1024]{2,1,0:T(8,128)(2,1)S(1)}, u32[]{:S(2)}, u32[]{:S(2)}) collective-permute-start(bf16[4,96,1024]{2,1,0:T(8,128)(2,1)S(1)} %get-tuple-element.95.refs_0_.p_ref), channel_id=1, source_target_pairs={{4,8},{8,4},{5,9},{9,5},{6,10},{10,6},{7,11},{11,7},{20,24},{24,20... | collective-permute-start | bytes 2359304 | tf_op jit(solution)/shard_map/ppermute | solution.py:465
  125.6 30.0 %collective-permute-start.22 = (bf16[3,32,1024]{2,1,0:T(8,128)(2,1)S(1)}, bf16[3,32,1024]{2,1,0:T(8,128)(2,1)S(1)}, u32[]{:S(2)}, u32[]{:S(2)}) collective-permute-start(bf16[3,32,1024]{2,1,0:T(8,128)(2,1)S(1)} %get-tuple-element.94), channel_id=1, source_target_pairs={{0,4},{12,8},{1,5},{13,9},{2,6},{14,10},{3,7},{15,11},{16,20},{28,... | collective-permute-start | bytes 589832 | tf_op jit(solution)/shard_map/ppermute | solution.py:467
  132.6 11.5 %collective-permute-start.29 = (bf16[3,384,128]{2,1,0:T(8,128)(2,1)S(1)}, bf16[3,384,128]{2,1,0:T(8,128)(2,1)S(1)}, u32[]{:S(2)}, u32[]{:S(2)}) collective-permute-start(bf16[3,384,128]{2,1,0:T(8,128)(2,1)S(1)} %add_convert_fusion.1.refs_0_), channel_id=1, source_target_pairs={{0,2},{1,3},{2,0},{3,1},{4,6},{5,7},{6,4},{7,5},{8,10},{9,11},{10,... | collective-permute-start | bytes 884744 | tf_op jit(solution)/shard_map/ppermute | solution.py:395
  134.9 16.7 %collective-permute-start.24 = (bf16[3,96,1024]{2,1,0:T(8,128)(2,1)S(1)}, bf16[3,96,1024]{2,1,0:T(8,128)(2,1)S(1)}, u32[]{:S(2)}, u32[]{:S(2)}) collective-permute-start(bf16[3,96,1024]{2,1,0:T(8,128)(2,1)S(1)} %get-tuple-element.97), channel_id=1, source_target_pairs={{4,0},{8,12},{5,1},{9,13},{6,2},{10,14},{7,3},{11,15},{20,16},{24,... | collective-permute-start | bytes 1769480 | tf_op jit(solution)/shard_map/ppermute | solution.py:474
  141.3 16.2 %collective-permute-start.32 = (bf16[4,64,1024]{2,1,0:T(8,128)(2,1)S(1)}, bf16[4,64,1024]{2,1,0:T(8,128)(2,1)S(1)}, u32[]{:S(2)}, u32[]{:S(2)}) collective-permute-start(bf16[4,64,1024]{2,1,0:T(8,128)(2,1)S(1)} %shard_map.88.refs_0_.p_ref), channel_id=1, source_target_pairs={{4,8},{8,4},{5,9},{9,5},{6,10},{10,6},{7,11},{11,7},{20,24},{24,20... | collective-permute-start | bytes 1572872 | tf_op jit(solution)/shard_map/ppermute | solution.py:465
  142.8 22.5 %collective-permute-start.31 = (bf16[3,96,1024]{2,1,0:T(8,128)(2,1)S(1)}, bf16[3,96,1024]{2,1,0:T(8,128)(2,1)S(1)}, u32[]{:S(2)}, u32[]{:S(2)}) collective-permute-start(bf16[3,96,1024]{2,1,0:T(8,128)(2,1)S(1)} %get-tuple-element.107), channel_id=1, source_target_pairs={{4,0},{8,12},{5,1},{9,13},{6,2},{10,14},{7,3},{11,15},{20,16},{24,... | collective-permute-start | bytes 1769480 | tf_op jit(solution)/shard_map/ppermute | solution.py:474
  156.6 12.9 %collective-permute-start.30 = (bf16[4,32,1024]{2,1,0:T(8,128)(2,1)S(1)}, bf16[4,32,1024]{2,1,0:T(8,128)(2,1)S(1)}, u32[]{:S(2)}, u32[]{:S(2)}) collective-permute-start(bf16[4,32,1024]{2,1,0:T(8,128)(2,1)S(1)} %shard_map.91.refs_0_.p_ref), channel_id=1, source_target_pairs={{4,8},{8,4},{5,9},{9,5},{6,10},{10,6},{7,11},{11,7},{20,24},{24,20... | collective-permute-start | bytes 786440 | tf_op jit(solution)/shard_map/ppermute | solution.py:465
  158.2 15.0 %collective-permute-start.34 = (bf16[3,64,1024]{2,1,0:T(8,128)(2,1)S(1)}, bf16[3,64,1024]{2,1,0:T(8,128)(2,1)S(1)}, u32[]{:S(2)}, u32[]{:S(2)}) collective-permute-start(bf16[3,64,1024]{2,1,0:T(8,128)(2,1)S(1)} %get-tuple-element.114), channel_id=1, source_target_pairs={{4,0},{8,12},{5,1},{9,13},{6,2},{10,14},{7,3},{11,15},{20,16},{24,... | collective-permute-start | bytes 1179656 | tf_op jit(solution)/shard_map/ppermute | solution.py:474
  169.3 1.9 collective-permute-start.35
  170.0 9.2 %collective-permute-start.33 = (bf16[3,32,1024]{2,1,0:T(8,128)(2,1)S(1)}, bf16[3,32,1024]{2,1,0:T(8,128)(2,1)S(1)}, u32[]{:S(2)}, u32[]{:S(2)}) collective-permute-start(bf16[3,32,1024]{2,1,0:T(8,128)(2,1)S(1)} %get-tuple-element.113), channel_id=1, source_target_pairs={{4,0},{8,12},{5,1},{9,13},{6,2},{10,14},{7,3},{11,15},{20,16},{24,... | collective-permute-start | bytes 589832 | tf_op jit(solution)/shard_map/ppermute | solution.py:474
  171.4 10.8 %collective-permute-start.36 = (bf16[3,288,128]{2,1,0:T(8,128)(2,1)S(1)}, bf16[3,288,128]{2,1,0:T(8,128)(2,1)S(1)}, u32[]{:S(2)}, u32[]{:S(2)}) collective-permute-start(bf16[3,288,128]{2,1,0:T(8,128)(2,1)S(1)} %add_convert_fusion.2.refs_2_), channel_id=1, source_target_pairs={{0,2},{1,3},{2,0},{3,1},{4,6},{5,7},{6,4},{7,5},{8,10},{9,11},{10,... | collective-permute-start | bytes 663560 | tf_op jit(solution)/shard_map/ppermute | solution.py:395
  184.8 1.4 collective-permute-start.37
  186.2 4.4 %collective-permute-start.38 = (bf16[3,96,128]{2,1,0:T(8,128)(2,1)S(1)}, bf16[3,96,128]{2,1,0:T(8,128)(2,1)S(1)}, u32[]{:S(2)}, u32[]{:S(2)}) collective-permute-start(bf16[3,96,128]{2,1,0:T(8,128)(2,1)S(1)} %add_convert_fusion.3.refs_4_), channel_id=1, source_target_pairs={{0,2},{1,3},{2,0},{3,1},{4,6},{5,7},{6,4},{7,5},{8,10},{9,11},{10,... | collective-permute-start | bytes 221192 | tf_op jit(solution)/shard_map/ppermute | solution.py:395
  190.6 2.3 %copy-start = (bf16[3,768,1024]{2,1,0:T(8,128)(2,1)S(1)}, bf16[3,768,1024]{2,1,0:T(8,128)(2,1)}, u32[]{:S(2)}) copy-start(bf16[3,768,1024]{2,1,0:T(8,128)(2,1)} %get-tuple-element.122.refs_6_.refs_4_) | copy-start | bytes 14155780
  192.9 23.7 %copy-start.2 = (bf16[4,224,1024]{2,1,0:T(8,128)(2,1)S(1)}, bf16[4,224,1024]{2,1,0:T(8,128)(2,1)}, u32[]{:S(2)}) copy-start(bf16[4,224,1024]{2,1,0:T(8,128)(2,1)} %get-tuple-element.120.in_ref) | copy-start | bytes 5505028
  192.9 25.3 %copy-start.1 = (bf16[3,768,1024]{2,1,0:T(8,128)(2,1)S(1)}, bf16[3,768,1024]{2,1,0:T(8,128)(2,1)}, u32[]{:S(2)}) copy-start(bf16[3,768,1024]{2,1,0:T(8,128)(2,1)} %get-tuple-element.122.refs_6_.refs_4_) | copy-start | bytes 14155780
  205.3 2.1 collective-permute-start.39
  207.5 9.1 %collective-permute-start.40 = (bf16[3,384,128]{2,1,0:T(8,128)(2,1)S(1)}, bf16[3,384,128]{2,1,0:T(8,128)(2,1)S(1)}, u32[]{:S(2)}, u32[]{:S(2)}) collective-permute-start(bf16[3,384,128]{2,1,0:T(8,128)(2,1)S(1)} %add_convert_fusion.refs_0_), channel_id=1, source_target_pairs={{0,2},{1,3},{2,0},{3,1},{4,6},{5,7},{6,4},{7,5},{8,10},{9,11},{10,... | collective-permute-start | bytes 884744 | tf_op jit(solution)/shard_map/ppermute | solution.py:395
  209.3 8.6 %collective-permute-start.41 = (bf16[3,384,128]{2,1,0:T(8,128)(2,1)S(1)}, bf16[3,384,128]{2,1,0:T(8,128)(2,1)S(1)}, u32[]{:S(2)}, u32[]{:S(2)}) collective-permute-start(bf16[3,384,128]{2,1,0:T(8,128)(2,1)S(1)} %add_convert_fusion.refs_0_), channel_id=1, source_target_pairs={{0,1},{1,0},{2,3},{3,2},{4,5},{5,4},{6,7},{7,6},{8,9},{9,8},{10,11... | collective-permute-start | bytes 884744 | tf_op jit(solution)/shard_map/ppermute | solution.py:395
  216.6 1.6 collective-permute-start.42

commit v2 on v0

--- a/solution.py
+++ b/solution.py
@@ -438,7 +438,7 @@
         denom = denom + jnp.sum(value[:, :, None] * rows[:, None, :], axis=0)
     fcols = jnp.concatenate(near[:2], axis=0).T
 
-    chunks = [(0, 1), (0, 2), (0, 3), (3, 3), (3, 3), (1, 3), (1, 3), (2, 3), (2, 2), (2, 1)]
+    chunks = [(0, 1), (0, 2), (0, 3), (3, 3), (3, 3), (1, 3), (1, 3), (2, 2), (2, 2), (2, 2)]
     groups = [(0, 1, 2, 3, 4), (5, 6, 7), (8, 9)]
     lead, lag = 2, 2
     spans, used = [], [0] * 4
@@ -455,7 +455,7 @@
     order = []
     for step in range(count):
         order += [("sums", step), ("base", step - 1), ("residual", step - lag)]
-    order += [("base", count - 1)] + [("residual", c) for c in range(count - lag, count)]
+    order += [("residual", count - 2), ("base", count - 1), ("residual", count - 1)]
     for kind, c in order:
         if c < 0:
             continue
@@ -476,8 +476,6 @@
             moved[c] = lax.ppermute(leaving, "exp", outwards)
             after = (base[c],)
         else:
-            if c == count - 2:
-                after = after + (moved[count - 1],)
             *held, firsts[c] = residual_chunk(
                 meta,
                 weights,

time: 231 us -> 233 us (level)
  waiting for transfers between devices: 37.7 us -> 42.3 us
    ppermute x10, waiting for transfers between devices: 13.5 us -> 18.6 us  [swap(): return lax.ppermute(value, 'col', [(i, i ^ bit) for i in range(size)])]
  transfers between devices with their start and end apart: 43 -> 43, of which waited for: 10 -> 12; matrix products, arithmetic and copies ran while one was open for 2% -> 2% of each run, Pallas kernels for 24% -> 23%
where the time goes in v2:
time: 233 us; the launch traced here: 232 us
  starting transfers between devices  99 us (42%)
  Pallas kernels  80.4 us (35%)
  waiting for transfers between devices  42.3 us (18%)
  local copies, waits for them, and re-layouts  5.76 us (2%)
  other arithmetic  2.67 us (1%)
    ppermute x8, starting transfers between devices, merge_folded(): arrived[c + lead] = lax.ppermute(copied[0], 'exp', inwards)  62.5 us
    pallas_call x10, Pallas kernels, residual_chunk(): pl.pallas_call(residual_kernel, grid_spec=pltpu.PrefetchScalarGridSpec(nu...  34.1 us
    ppermute x10, waiting for transfers between devices, merge_folded(): moved[c] = lax.ppermute(leaving, 'exp', outwards)  20 us
    ppermute x10, waiting for transfers between devices, swap(): return lax.ppermute(value, 'col', [(i, i ^ bit) for i in range(size)])  18.6 us
    pallas_call x10, Pallas kernels, cluster_sums(): pl.pallas_call(functools.partial(sums_kernel, ahead is not None), grid_sp...  15.5 us
    ppermute x10, starting transfers between devices, merge_folded(): moved[c] = lax.ppermute(leaving, 'exp', outwards)  13.1 us
    pallas_call x1, Pallas kernels, power_step(): pl.pallas_call(functools.partial(power_kernel, splits, pieces), in_specs=...  12.4 us
    pallas_call x1, Pallas kernels, project(): pl.pallas_call(project_kernel, in_specs=[SMEM] + [vmem] * (len(mine) + le...  12.4 us
  transfers between devices with their start and end apart: 43, of which 12 were waited for; matrix products, arithmetic and copies ran while one was open for 2% of the time, Pallas kernels for 23%

profile of v2, /device:TPU:0, one launch (start us, length us, event | category | flops | bytes accessed | tf_op | source)
XLA Modules:
  0.0 231.8 jit_solution(297430554828650284)
XLA Ops:
  1.6 3.1 %collective-permute-start.1 = (bf16[3,768]{1,0:T(4,128)(2,1)}, bf16[3,768]{1,0:T(4,128)(2,1)S(1)}, u32[]{:S(2)}, u32[]{:S(2)}) collective-permute-start(bf16[3,768]{1,0:T(4,128)(2,1)} %param.5), channel_id=1, source_target_pairs={{0,4},{4,0},{8,12},{12,8},{1,5},{5,1},{9,13},{13,9},{2,6},{6,2},{1... | collective-permute-start | bytes 13832 | tf_op jit(solution)/shard_map/ppermute | solution.py:434
  4.7 2.6 %collective-permute-start.5 = (bf16[3,768]{1,0:T(4,128)(2,1)}, bf16[3,768]{1,0:T(4,128)(2,1)S(1)}, u32[]{:S(2)}, u32[]{:S(2)}) collective-permute-start(bf16[3,768]{1,0:T(4,128)(2,1)} %param.5), channel_id=1, source_target_pairs={{0,8},{4,12},{8,0},{12,4},{1,9},{5,13},{9,1},{13,5},{2,10},{6,14},... | collective-permute-start | bytes 13832 | tf_op jit(solution)/shard_map/ppermute | solution.py:434
  7.3 2.8 %collective-permute-start.2 = (bf16[3,32,1024]{2,1,0:T(8,128)(2,1)S(1)}, bf16[3,32,1024]{2,1,0:T(8,128)(2,1)S(1)}, u32[]{:S(2)}, u32[]{:S(2)}) collective-permute-start(bf16[3,32,1024]{2,1,0:T(8,128)(2,1)S(1)} %slice.7), channel_id=1, source_target_pairs={{0,4},{12,8},{1,5},{13,9},{2,6},{14,10},{3,7},{15,11},{16,20},{28,... | collective-permute-start | bytes 589832 | tf_op jit(solution)/shard_map/ppermute | solution.py:454
  11.1 1.3 collective-permute-start
  18.3 6.7 %collective-permute-start.9 = (bf16[3,96,1024]{2,1,0:T(8,128)(2,1)S(1)}, bf16[3,96,1024]{2,1,0:T(8,128)(2,1)S(1)}, u32[]{:S(2)}, u32[]{:S(2)}) collective-permute-start(bf16[3,96,1024]{2,1,0:T(8,128)(2,1)S(1)} %get-tuple-element.74), channel_id=1, source_target_pairs={{0,4},{12,8},{1,5},{13,9},{2,6},{14,10},{3,7},{15,11},{16,20},{28,... | collective-permute-start | bytes 1769480 | tf_op jit(solution)/shard_map/ppermute | solution.py:469
  25.1 1.4 shard_map.68
  27.1 6.4 %collective-permute-start.3 = (bf16[3,96,1024]{2,1,0:T(8,128)(2,1)S(1)}, bf16[3,96,1024]{2,1,0:T(8,128)(2,1)S(1)}, u32[]{:S(2)}, u32[]{:S(2)}) collective-permute-start(bf16[3,96,1024]{2,1,0:T(8,128)(2,1)S(1)} %get-tuple-element.72), channel_id=1, source_target_pairs={{0,4},{12,8},{1,5},{13,9},{2,6},{14,10},{3,7},{15,11},{16,20},{28,... | collective-permute-start | bytes 1769480 | tf_op jit(solution)/shard_map/ppermute | solution.py:469
  34.9 3.6 %collective-permute-done.9.a_ref = bf16[3,96,1024]{2,1,0:T(8,128)(2,1)S(1)} collective-permute-done((bf16[3,96,1024]{2,1,0:T(8,128)(2,1)S(1)}, bf16[3,96,1024]{2,1,0:T(8,128)(2,1)S(1)}, u32[]{:S(2)}, u32[]{:S(2)}) %collective-permute-start.9) | collective-permute-done | bytes 589856 | tf_op jit(solution)/shard_map/ppermute | solution.py:469
  38.5 2.2 shard_map.70
  41.4 7.4 %collective-permute-start.15 = (bf16[3,96,1024]{2,1,0:T(8,128)(2,1)S(1)}, bf16[3,96,1024]{2,1,0:T(8,128)(2,1)S(1)}, u32[]{:S(2)}, u32[]{:S(2)}) collective-permute-start(bf16[3,96,1024]{2,1,0:T(8,128)(2,1)S(1)} %get-tuple-element.83), channel_id=1, source_target_pairs={{0,4},{12,8},{1,5},{13,9},{2,6},{14,10},{3,7},{15,11},{16,20},{28,... | collective-permute-start | bytes 1769480 | tf_op jit(solution)/shard_map/ppermute | solution.py:469
  50.3 2.5 %shard_map.72 = (bf16[3,768,1024]{2,1,0:T(8,128)(2,1)}, bf16[4,224,1024]{2,1,0:T(8,128)(2,1)}, f32[3,32,128]{2,1,0:T(8,128)S(1)}) custom-call(s32[5]{0:T(128)S(1)} %pad_add_fusion.meta, bf16[3,768,1024]{2,1,0:T(8,128)(2,1)} %w_ref.39, bf16[4,32,1024]{2,1,0:T(8,128)(2,1)S(1)} %shard_map.69.refs_1_.b_ref, ...), custom_call_target="tpu_custom_call" | custom-call | flops 10000000000 | bytes 1 | tf_op jit(solution)/shard_map/pallas_call | solution.py:195
  52.9 2.2 shard_map.73
  55.8 8.3 %collective-permute-start.10 = (bf16[3,96,1024]{2,1,0:T(8,128)(2,1)S(1)}, bf16[3,96,1024]{2,1,0:T(8,128)(2,1)S(1)}, u32[]{:S(2)}, u32[]{:S(2)}) collective-permute-start(bf16[3,96,1024]{2,1,0:T(8,128)(2,1)S(1)} %get-tuple-element.77), channel_id=1, source_target_pairs={{0,4},{12,8},{1,5},{13,9},{2,6},{14,10},{3,7},{15,11},{16,20},{28,... | collective-permute-start | bytes 1769480 | tf_op jit(solution)/shard_map/ppermute | solution.py:469
  65.7 3.0 %shard_map.75 = (bf16[3,768,1024]{2,1,0:T(8,128)(2,1)}, bf16[4,224,1024]{2,1,0:T(8,128)(2,1)}, f32[3,64,128]{2,1,0:T(8,128)S(1)}) custom-call(s32[5]{0:T(128)S(1)} %pad_add_fusion.meta, bf16[3,768,1024]{2,1,0:T(8,128)(2,1)} %w_ref.39, bf16[4,64,1024]{2,1,0:T(8,128)(2,1)S(1)} %shard_map.71.refs_0_.b_ref, ...), custom_call_target="tpu_custom_call", output_to_operand_aliasing={{0}: (5, {}), {1}: (6, {})} | custom-call | flops 10000000000 | bytes 1 | tf_op jit(solution)/shard_map/pallas_call | solution.py:195
  68.6 2.2 shard_map.76
  71.6 7.5 %collective-permute-start.21 = (bf16[3,96,1024]{2,1,0:T(8,128)(2,1)S(1)}, bf16[3,96,1024]{2,1,0:T(8,128)(2,1)S(1)}, u32[]{:S(2)}, u32[]{:S(2)}) collective-permute-start(bf16[3,96,1024]{2,1,0:T(8,128)(2,1)S(1)} %get-tuple-element.93), channel_id=1, source_target_pairs={{0,4},{12,8},{1,5},{13,9},{2,6},{14,10},{3,7},{15,11},{16,20},{28,... | collective-permute-start | bytes 1769480 | tf_op jit(solution)/shard_map/ppermute | solution.py:469
  80.6 4.0 %shard_map.78 = (bf16[3,768,1024]{2,1,0:T(8,128)(2,1)}, bf16[4,224,1024]{2,1,0:T(8,128)(2,1)}, f32[3,96,128]{2,1,0:T(8,128)S(1)}) custom-call(s32[5]{0:T(128)S(1)} %pad_add_fusion.meta, bf16[3,768,1024]{2,1,0:T(8,128)(2,1)} %w_ref.39, bf16[4,96,1024]{2,1,0:T(8,128)(2,1)S(1)} %shard_map.74.refs_2_.b_ref, ...), custom_call_target="tpu_custom_call", output_to_operand_aliasing={{0}: (5, {}), {1}: (6, {})} | custom-call | flops 10000000000 | bytes 1 | tf_op jit(solution)/shard_map/pallas_call | solution.py:195
  84.6 1.4 shard_map.79
  88.3 12.9 %collective-permute-start.16 = (bf16[3,64,1024]{2,1,0:T(8,128)(2,1)S(1)}, bf16[3,64,1024]{2,1,0:T(8,128)(2,1)S(1)}, u32[]{:S(2)}, u32[]{:S(2)}) collective-permute-start(bf16[3,64,1024]{2,1,0:T(8,128)(2,1)S(1)} %get-tuple-element.87), channel_id=1, source_target_pairs={{0,4},{12,8},{1,5},{13,9},{2,6},{14,10},{3,7},{15,11},{16,20},{28,... | collective-permute-start | bytes 1179656 | tf_op jit(solution)/shard_map/ppermute | solution.py:469
  101.3 3.9 %shard_map.81 = (bf16[3,768,1024]{2,1,0:T(8,128)(2,1)}, bf16[4,224,1024]{2,1,0:T(8,128)(2,1)}, f32[3,96,128]{2,1,0:T(8,128)S(1)}) custom-call(s32[5]{0:T(128)S(1)} %pad_add_fusion.meta, bf16[3,768,1024]{2,1,0:T(8,128)(2,1)} %w_ref.39, bf16[4,96,1024]{2,1,0:T(8,128)(2,1)S(1)} %shard_map.77.refs_2_.b_ref, ...), custom_call_target="tpu_custom_call", output_to_operand_aliasing={{0}: (5, {}), {1}: (6, {})} | custom-call | flops 10000000000 | bytes 1 | tf_op jit(solution)/shard_map/pallas_call | solution.py:195
  105.2 1.4 shard_map.82
  107.4 6.1 %collective-permute-start.27 = (bf16[3,64,1024]{2,1,0:T(8,128)(2,1)S(1)}, bf16[3,64,1024]{2,1,0:T(8,128)(2,1)S(1)}, u32[]{:S(2)}, u32[]{:S(2)}) collective-permute-start(bf16[3,64,1024]{2,1,0:T(8,128)(2,1)S(1)} %get-tuple-element.107), channel_id=1, source_target_pairs={{0,4},{12,8},{1,5},{13,9},{2,6},{14,10},{3,7},{15,11},{16,20},{28,... | collective-permute-start | bytes 1179656 | tf_op jit(solution)/shard_map/ppermute | solution.py:469
  114.3 3.9 %shard_map.84 = (bf16[3,768,1024]{2,1,0:T(8,128)(2,1)}, bf16[4,224,1024]{2,1,0:T(8,128)(2,1)}, f32[3,96,128]{2,1,0:T(8,128)S(1)}) custom-call(s32[5]{0:T(128)S(1)} %pad_add_fusion.meta, bf16[3,768,1024]{2,1,0:T(8,128)(2,1)} %w_ref.39, bf16[4,96,1024]{2,1,0:T(8,128)(2,1)S(1)} %shard_map.80.refs_2_.b_ref, ...), custom_call_target="tpu_custom_call", output_to_operand_aliasing={{0}: (5, {}), {1}: (6, {})} | custom-call | flops 10000000000 | bytes 1 | tf_op jit(solution)/shard_map/pallas_call | solution.py:195
  119.7 1.3 shard_map.85
  121.7 7.2 %collective-permute-start.22 = (bf16[3,64,1024]{2,1,0:T(8,128)(2,1)S(1)}, bf16[3,64,1024]{2,1,0:T(8,128)(2,1)S(1)}, u32[]{:S(2)}, u32[]{:S(2)}) collective-permute-start(bf16[3,64,1024]{2,1,0:T(8,128)(2,1)S(1)} %get-tuple-element.98), channel_id=1, source_target_pairs={{0,4},{12,8},{1,5},{13,9},{2,6},{14,10},{3,7},{15,11},{16,20},{28,... | collective-permute-start | bytes 1179656 | tf_op jit(solution)/shard_map/ppermute | solution.py:469
  131.1 5.3 %collective-permute-done.25.r_ref = bf16[3,96,1024]{2,1,0:T(8,128)(2,1)S(1)} collective-permute-done((bf16[3,96,1024]{2,1,0:T(8,128)(2,1)S(1)}, bf16[3,96,1024]{2,1,0:T(8,128)(2,1)S(1)}, u32[]{:S(2)}, u32[]{:S(2)}) %collective-permute-start.25) | collective-permute-done | bytes 589856 | tf_op jit(solution)/shard_map/ppermute | solution.py:476
  136.4 1.5 collective-permute-start.29
  137.9 3.9 %shard_map.87 = (bf16[3,768,1024]{2,1,0:T(8,128)(2,1)}, bf16[4,224,1024]{2,1,0:T(8,128)(2,1)}, f32[3,96,128]{2,1,0:T(8,128)S(1)}) custom-call(s32[5]{0:T(128)S(1)} %pad_add_fusion.meta, bf16[3,768,1024]{2,1,0:T(8,128)(2,1)} %w_ref.39, bf16[4,96,1024]{2,1,0:T(8,128)(2,1)S(1)} %get-tuple-element.96.refs_2_.b_ref, ...), custom_call_target="tpu_custom_call", output_to_operand_aliasing={{0}: (5, {}), {1}: (6, {})} | custom-call | flops 10000000000 | bytes 1 | tf_op jit(solution)/shard_map/pallas_call | solution.py:195
  145.6 3.4 %collective-permute-done.24.r_ref = bf16[3,96,1024]{2,1,0:T(8,128)(2,1)S(1)} collective-permute-done((bf16[3,96,1024]{2,1,0:T(8,128)(2,1)S(1)}, bf16[3,96,1024]{2,1,0:T(8,128)(2,1)S(1)}, u32[]{:S(2)}, u32[]{:S(2)}) %collective-permute-start.24) | collective-permute-done | bytes 589856 | tf_op jit(solution)/shard_map/ppermute | solution.py:476
  149.0 3.9 %shard_map.90 = (bf16[3,768,1024]{2,1,0:T(8,128)(2,1)}, bf16[4,224,1024]{2,1,0:T(8,128)(2,1)}, f32[3,96,128]{2,1,0:T(8,128)S(1)}) custom-call(s32[5]{0:T(128)S(1)} %pad_add_fusion.meta, bf16[3,768,1024]{2,1,0:T(8,128)(2,1)} %w_ref.39, bf16[4,96,1024]{2,1,0:T(8,128)(2,1)S(1)} %get-tuple-element.100.refs_2_.b_ref, ...), custom_call_target="tpu_custom_call", output_to_operand_aliasing={{0}: (5, {}), {1}: (6, {})} | custom-call | flops 10000000000 | bytes 1 | tf_op jit(solution)/shard_map/pallas_call | solution.py:195
  155.5 1.5 collective-permute-start.32
  157.0 3.0 %shard_map.93 = (bf16[3,768,1024]{2,1,0:T(8,128)(2,1)}, bf16[4,224,1024]{2,1,0:T(8,128)(2,1)}, f32[3,64,128]{2,1,0:T(8,128)S(1)}) custom-call(s32[5]{0:T(128)S(1)} %pad_add_fusion.meta, bf16[3,768,1024]{2,1,0:T(8,128)(2,1)} %w_ref.39, bf16[4,64,1024]{2,1,0:T(8,128)(2,1)S(1)} %get-tuple-element.109.refs_2_.b_ref, ...), custom_call_target="tpu_custom_call", output_to_operand_aliasing={{0}: (5, {}), {1}: (6, {})} | custom-call | flops 10000000000 | bytes 1 | tf_op jit(solution)/shard_map/pallas_call | solution.py:195
  160.1 8.0 %collective-permute-done.32.r_ref = bf16[3,64,1024]{2,1,0:T(8,128)(2,1)S(1)} collective-permute-done((bf16[3,64,1024]{2,1,0:T(8,128)(2,1)S(1)}, bf16[3,64,1024]{2,1,0:T(8,128)(2,1)S(1)}, u32[]{:S(2)}, u32[]{:S(2)}) %collective-permute-start.32) | collective-permute-done | bytes 393248 | tf_op jit(solution)/shard_map/ppermute | solution.py:476
  168.1 3.0 %shard_map.94 = (bf16[3,768,1024]{2,1,0:T(8,128)(2,1)}, bf16[4,224,1024]{2,1,0:T(8,128)(2,1)}, f32[3,64,128]{2,1,0:T(8,128)S(1)}) custom-call(s32[5]{0:T(128)S(1)} %pad_add_fusion.meta, bf16[3,768,1024]{2,1,0:T(8,128)(2,1)} %w_ref.39, bf16[4,64,1024]{2,1,0:T(8,128)(2,1)S(1)} %get-tuple-element.111.refs_2_.b_ref, ...), custom_call_target="tpu_custom_call", output_to_operand_aliasing={{0}: (5, {}), {1}: (6, {})} | custom-call | flops 10000000000 | bytes 1 | tf_op jit(solution)/shard_map/pallas_call | solution.py:195
  171.8 1.3 collective-permute-start.34
  174.4 4.5 %collective-permute-done.36.refs_3_ = bf16[3,256,128]{2,1,0:T(8,128)(2,1)S(1)} collective-permute-done((bf16[3,256,128]{2,1,0:T(8,128)(2,1)S(1)}, bf16[3,256,128]{2,1,0:T(8,128)(2,1)S(1)}, u32[]{:S(2)}, u32[]{:S(2)}) %collective-permute-start.36) | collective-permute-done | bytes 196640 | tf_op jit(solution)/shard_map/ppermute | solution.py:395
  178.9 3.3 %collective-permute-done.34.r_ref = bf16[3,64,1024]{2,1,0:T(8,128)(2,1)S(1)} collective-permute-done((bf16[3,64,1024]{2,1,0:T(8,128)(2,1)S(1)}, bf16[3,64,1024]{2,1,0:T(8,128)(2,1)S(1)}, u32[]{:S(2)}, u32[]{:S(2)}) %collective-permute-start.34) | collective-permute-done | bytes 393248 | tf_op jit(solution)/shard_map/ppermute | solution.py:476
  182.2 3.0 %shard_map.96 = (bf16[3,768,1024]{2,1,0:T(8,128)(2,1)}, bf16[4,224,1024]{2,1,0:T(8,128)(2,1)}, f32[3,64,128]{2,1,0:T(8,128)S(1)}) custom-call(s32[5]{0:T(128)S(1)} %pad_add_fusion.meta, bf16[3,768,1024]{2,1,0:T(8,128)(2,1)} %w_ref.39, bf16[4,64,1024]{2,1,0:T(8,128)(2,1)S(1)} %get-tuple-element.120.b_ref.refs_2_, ...), custom_call_target="tpu_custom_call", output_to_operand_aliasing={{0}: (5, {}), {1}: (6, {})} | custom-call | flops 10000000000 | bytes 1 | tf_op jit(solution)/shard_map/pallas_call | solution.py:195
  185.3 1.4 collective-permute-done.37
  186.7 1.8 collective-permute-start.38
  188.5 3.1 %collective-permute-done.38.refs_5_ = bf16[3,128,128]{2,1,0:T(8,128)(2,1)S(1)} collective-permute-done((bf16[3,128,128]{2,1,0:T(8,128)(2,1)S(1)}, bf16[3,128,128]{2,1,0:T(8,128)(2,1)S(1)}, u32[]{:S(2)}, u32[]{:S(2)}) %collective-permute-start.38) | collective-permute-done | bytes 98336 | tf_op jit(solution)/shard_map/ppermute | solution.py:395
  191.6 2.3 %copy-done = bf16[3,768,1024]{2,1,0:T(8,128)(2,1)S(1)} copy-done((bf16[3,768,1024]{2,1,0:T(8,128)(2,1)S(1)}, bf16[3,768,1024]{2,1,0:T(8,128)(2,1)}, u32[]{:S(2)}) %copy-start) | copy-done | bytes 4718616
  194.0 12.4 %shard_map.98 = (f32[3,384,128]{2,1,0:T(8,128)S(1)}, f32[3,384,128]{2,1,0:T(8,128)S(1)}) custom-call(s32[1]{0:T(128)} %bitcast.3.side, bf16[3,384,128]{2,1,0:T(8,128)(2,1)S(1)} %add_convert_fusion.1.refs_0_, bf16[3,384,128]{2,1,0:T(8,128)(2,1)S(1)} %collective-permute-done.29.refs_3_.refs_1_, bf16[3,256,128]{2,1,0:T(8,128)(2,1)S(1)} %add_convert_fusion.2.refs_2_, ...), custom_call_target="tpu_custom_call" | custom-call | tf_op jit(solution)/shard_map/pallas_call | solution.py:339
  206.5 2.0 collective-permute-done.39
  208.5 1.8 collective-permute-start.40
  210.3 7.3 %collective-permute-done.40.refs_1_ = bf16[3,384,128]{2,1,0:T(8,128)(2,1)S(1)} collective-permute-done((bf16[3,384,128]{2,1,0:T(8,128)(2,1)S(1)}, bf16[3,384,128]{2,1,0:T(8,128)(2,1)S(1)}, u32[]{:S(2)}, u32[]{:S(2)}) %collective-permute-start.40) | collective-permute-done | bytes 294944 | tf_op jit(solution)/shard_map/ppermute | solution.py:395
  217.6 1.3 shard_map.97
  219.2 12.4 %shard_map.99 = (bf16[3,768,128]{2,1,0:T(8,128)(2,1)}, bf16[3,128,1024]{2,1,0:T(8,128)(2,1)}) custom-call(s32[1]{0:T(128)} %bitcast.3.side, bf16[3,384,128]{2,1,0:T(8,128)(2,1)S(1)} %add_convert_fusion.refs_0_, bf16[3,384,128]{2,1,0:T(8,128)(2,1)S(1)} %collective-permute-done.40.refs_1_, bf16[3,384,128]{2,1,0:T(8,128)(2,1)S(1)} %collective-permute-done.41.refs_2_, ...), custom_call_target="tpu_custom_call" | custom-call | tf_op jit(solution)/shard_map/pallas_call | solution.py:377
  (116 shorter events, 33.4 us)
Async XLA Ops:
  1.6 13.8 %collective-permute-start.1 = (bf16[3,768]{1,0:T(4,128)(2,1)}, bf16[3,768]{1,0:T(4,128)(2,1)S(1)}, u32[]{:S(2)}, u32[]{:S(2)}) collective-permute-start(bf16[3,768]{1,0:T(4,128)(2,1)} %param.5), channel_id=1, source_target_pairs={{0,4},{4,0},{8,12},{12,8},{1,5},{5,1},{9,13},{13,9},{2,6},{6,2},{1... | collective-permute-start | bytes 13832 | tf_op jit(solution)/shard_map/ppermute | solution.py:434
  4.7 10.8 %collective-permute-start.5 = (bf16[3,768]{1,0:T(4,128)(2,1)}, bf16[3,768]{1,0:T(4,128)(2,1)S(1)}, u32[]{:S(2)}, u32[]{:S(2)}) collective-permute-start(bf16[3,768]{1,0:T(4,128)(2,1)} %param.5), channel_id=1, source_target_pairs={{0,8},{4,12},{8,0},{12,4},{1,9},{5,13},{9,1},{13,5},{2,10},{6,14},... | collective-permute-start | bytes 13832 | tf_op jit(solution)/shard_map/ppermute | solution.py:434
  7.3 8.7 %collective-permute-start.6 = (bf16[3,768]{1,0:T(4,128)(2,1)}, bf16[3,768]{1,0:T(4,128)(2,1)S(1)}, u32[]{:S(2)}, u32[]{:S(2)}) collective-permute-start(bf16[3,768]{1,0:T(4,128)(2,1)} %param.5), channel_id=1, source_target_pairs={{0,12},{4,8},{8,4},{12,0},{1,13},{5,9},{9,5},{13,1},{2,14},{6,10},... | collective-permute-start | bytes 13832 | tf_op jit(solution)/shard_map/ppermute | solution.py:434
  7.3 9.1 %collective-permute-start.2 = (bf16[3,32,1024]{2,1,0:T(8,128)(2,1)S(1)}, bf16[3,32,1024]{2,1,0:T(8,128)(2,1)S(1)}, u32[]{:S(2)}, u32[]{:S(2)}) collective-permute-start(bf16[3,32,1024]{2,1,0:T(8,128)(2,1)S(1)} %slice.7), channel_id=1, source_target_pairs={{0,4},{12,8},{1,5},{13,9},{2,6},{14,10},{3,7},{15,11},{16,20},{28,... | collective-permute-start | bytes 589832 | tf_op jit(solution)/shard_map/ppermute | solution.py:454
  11.1 14.0 %collective-permute-start = (bf16[3,64,1024]{2,1,0:T(8,128)(2,1)S(1)}, bf16[3,64,1024]{2,1,0:T(8,128)(2,1)S(1)}, u32[]{:S(2)}, u32[]{:S(2)}) collective-permute-start(bf16[3,64,1024]{2,1,0:T(8,128)(2,1)S(1)} %slice.6), channel_id=1, source_target_pairs={{0,4},{12,8},{1,5},{13,9},{2,6},{14,10},{3,7},{15,11},{16,20},{28,... | collective-permute-start | bytes 1179656 | tf_op jit(solution)/shard_map/ppermute | solution.py:454
  17.6 16.0 %collective-permute-start.4 = (bf16[4,32,1024]{2,1,0:T(8,128)(2,1)S(1)}, bf16[4,32,1024]{2,1,0:T(8,128)(2,1)S(1)}, u32[]{:S(2)}, u32[]{:S(2)}) collective-permute-start(bf16[4,32,1024]{2,1,0:T(8,128)(2,1)S(1)} %get-tuple-element.71.refs_1_.refs_0_), channel_id=1, source_target_pairs={{4,8},{8,4},{5,9},{9,5},{6,10},{10,6},{7,11},{11,7},{20,24},{24,20... | collective-permute-start | bytes 786440 | tf_op jit(solution)/shard_map/ppermute | solution.py:467
  18.3 20.2 %collective-permute-start.9 = (bf16[3,96,1024]{2,1,0:T(8,128)(2,1)S(1)}, bf16[3,96,1024]{2,1,0:T(8,128)(2,1)S(1)}, u32[]{:S(2)}, u32[]{:S(2)}) collective-permute-start(bf16[3,96,1024]{2,1,0:T(8,128)(2,1)S(1)} %get-tuple-element.74), channel_id=1, source_target_pairs={{0,4},{12,8},{1,5},{13,9},{2,6},{14,10},{3,7},{15,11},{16,20},{28,... | collective-permute-start | bytes 1769480 | tf_op jit(solution)/shard_map/ppermute | solution.py:469
  26.4 22.4 %collective-permute-start.8 = (bf16[4,64,1024]{2,1,0:T(8,128)(2,1)S(1)}, bf16[4,64,1024]{2,1,0:T(8,128)(2,1)S(1)}, u32[]{:S(2)}, u32[]{:S(2)}) collective-permute-start(bf16[4,64,1024]{2,1,0:T(8,128)(2,1)S(1)} %get-tuple-element.73.refs_3_.refs_0_), channel_id=1, source_target_pairs={{4,8},{8,4},{5,9},{9,5},{6,10},{10,6},{7,11},{11,7},{20,24},{24,20... | collective-permute-start | bytes 1572872 | tf_op jit(solution)/shard_map/ppermute | solution.py:467
  27.1 25.7 %collective-permute-start.3 = (bf16[3,96,1024]{2,1,0:T(8,128)(2,1)S(1)}, bf16[3,96,1024]{2,1,0:T(8,128)(2,1)S(1)}, u32[]{:S(2)}, u32[]{:S(2)}) collective-permute-start(bf16[3,96,1024]{2,1,0:T(8,128)(2,1)S(1)} %get-tuple-element.72), channel_id=1, source_target_pairs={{0,4},{12,8},{1,5},{13,9},{2,6},{14,10},{3,7},{15,11},{16,20},{28,... | collective-permute-start | bytes 1769480 | tf_op jit(solution)/shard_map/ppermute | solution.py:469
  33.6 16.7 %collective-permute-start.7 = (bf16[4,32,1024]{2,1,0:T(8,128)(2,1)S(1)}, bf16[4,32,1024]{2,1,0:T(8,128)(2,1)S(1)}, u32[]{:S(2)}, u32[]{:S(2)}) collective-permute-start(bf16[4,32,1024]{2,1,0:T(8,128)(2,1)S(1)} %shard_map.69.refs_1_.b_ref), channel_id=1, source_target_pairs={{4,0},{8,12},{5,1},{9,13},{6,2},{10,14},{7,3},{11,15},{20,16},{24,... | collective-permute-start | bytes 786440 | tf_op jit(solution)/shard_map/ppermute | solution.py:476
  40.7 23.5 %collective-permute-start.11 = (bf16[4,96,1024]{2,1,0:T(8,128)(2,1)S(1)}, bf16[4,96,1024]{2,1,0:T(8,128)(2,1)S(1)}, u32[]{:S(2)}, u32[]{:S(2)}) collective-permute-start(bf16[4,96,1024]{2,1,0:T(8,128)(2,1)S(1)} %get-tuple-element.75.refs_3_.refs_0_), channel_id=1, source_target_pairs={{4,8},{8,4},{5,9},{9,5},{6,10},{10,6},{7,11},{11,7},{20,24},{24,20... | collective-permute-start | bytes 2359304 | tf_op jit(solution)/shard_map/ppermute | solution.py:467
  41.4 8.9 %copy-start.3 = (bf16[3,1024,128]{2,1,0:T(8,128)(2,1)S(1)}, bf16[3,1024,128]{2,1,0:T(8,128)(2,1)}, u32[]{:S(2)}) copy-start(bf16[3,1024,128]{2,1,0:T(8,128)(2,1)} %s_ref.19) | copy-start | bytes 2359300
  41.4 27.2 %collective-permute-start.15 = (bf16[3,96,1024]{2,1,0:T(8,128)(2,1)S(1)}, bf16[3,96,1024]{2,1,0:T(8,128)(2,1)S(1)}, u32[]{:S(2)}, u32[]{:S(2)}) collective-permute-start(bf16[3,96,1024]{2,1,0:T(8,128)(2,1)S(1)} %get-tuple-element.83), channel_id=1, source_target_pairs={{0,4},{12,8},{1,5},{13,9},{2,6},{14,10},{3,7},{15,11},{16,20},{28,... | collective-permute-start | bytes 1769480 | tf_op jit(solution)/shard_map/ppermute | solution.py:469
  49.0 16.7 %collective-permute-start.13 = (bf16[4,64,1024]{2,1,0:T(8,128)(2,1)S(1)}, bf16[4,64,1024]{2,1,0:T(8,128)(2,1)S(1)}, u32[]{:S(2)}, u32[]{:S(2)}) collective-permute-start(bf16[4,64,1024]{2,1,0:T(8,128)(2,1)S(1)} %shard_map.71.refs_0_.b_ref), channel_id=1, source_target_pairs={{4,0},{8,12},{5,1},{9,13},{6,2},{10,14},{7,3},{11,15},{20,16},{24,... | collective-permute-start | bytes 1572872 | tf_op jit(solution)/shard_map/ppermute | solution.py:476
  55.1 24.0 %collective-permute-start.14 = (bf16[4,96,1024]{2,1,0:T(8,128)(2,1)S(1)}, bf16[4,96,1024]{2,1,0:T(8,128)(2,1)S(1)}, u32[]{:S(2)}, u32[]{:S(2)}) collective-permute-start(bf16[4,96,1024]{2,1,0:T(8,128)(2,1)S(1)} %get-tuple-element.78.refs_3_.refs_0_), channel_id=1, source_target_pairs={{4,8},{8,4},{5,9},{9,5},{6,10},{10,6},{7,11},{11,7},{20,24},{24,20... | collective-permute-start | bytes 2359304 | tf_op jit(solution)/shard_map/ppermute | solution.py:467
  55.8 28.8 %collective-permute-start.10 = (bf16[3,96,1024]{2,1,0:T(8,128)(2,1)S(1)}, bf16[3,96,1024]{2,1,0:T(8,128)(2,1)S(1)}, u32[]{:S(2)}, u32[]{:S(2)}) collective-permute-start(bf16[3,96,1024]{2,1,0:T(8,128)(2,1)S(1)} %get-tuple-element.77), channel_id=1, source_target_pairs={{0,4},{12,8},{1,5},{13,9},{2,6},{14,10},{3,7},{15,11},{16,20},{28,... | collective-permute-start | bytes 1769480 | tf_op jit(solution)/shard_map/ppermute | solution.py:469
  64.4 16.2 %collective-permute-start.12 = (bf16[4,96,1024]{2,1,0:T(8,128)(2,1)S(1)}, bf16[4,96,1024]{2,1,0:T(8,128)(2,1)S(1)}, u32[]{:S(2)}, u32[]{:S(2)}) collective-permute-start(bf16[4,96,1024]{2,1,0:T(8,128)(2,1)S(1)} %shard_map.74.refs_2_.b_ref), channel_id=1, source_target_pairs={{4,0},{8,12},{5,1},{9,13},{6,2},{10,14},{7,3},{11,15},{20,16},{24,... | collective-permute-start | bytes 2359304 | tf_op jit(solution)/shard_map/ppermute | solution.py:476
  70.9 15.9 %collective-permute-start.17 = (bf16[4,96,1024]{2,1,0:T(8,128)(2,1)S(1)}, bf16[4,96,1024]{2,1,0:T(8,128)(2,1)S(1)}, u32[]{:S(2)}, u32[]{:S(2)}) collective-permute-start(bf16[4,96,1024]{2,1,0:T(8,128)(2,1)S(1)} %get-tuple-element.85.refs_3_.refs_0_), channel_id=1, source_target_pairs={{4,8},{8,4},{5,9},{9,5},{6,10},{10,6},{7,11},{11,7},{20,24},{24,20... | collective-permute-start | bytes 2359304 | tf_op jit(solution)/shard_map/ppermute | solution.py:467
  71.6 33.6 %collective-permute-start.21 = (bf16[3,96,1024]{2,1,0:T(8,128)(2,1)S(1)}, bf16[3,96,1024]{2,1,0:T(8,128)(2,1)S(1)}, u32[]{:S(2)}, u32[]{:S(2)}) collective-permute-start(bf16[3,96,1024]{2,1,0:T(8,128)(2,1)S(1)} %get-tuple-element.93), channel_id=1, source_target_pairs={{0,4},{12,8},{1,5},{13,9},{2,6},{14,10},{3,7},{15,11},{16,20},{28,... | collective-permute-start | bytes 1769480 | tf_op jit(solution)/shard_map/ppermute | solution.py:469
  79.3 22.0 %collective-permute-start.19 = (bf16[4,96,1024]{2,1,0:T(8,128)(2,1)S(1)}, bf16[4,96,1024]{2,1,0:T(8,128)(2,1)S(1)}, u32[]{:S(2)}, u32[]{:S(2)}) collective-permute-start(bf16[4,96,1024]{2,1,0:T(8,128)(2,1)S(1)} %shard_map.77.refs_2_.b_ref), channel_id=1, source_target_pairs={{4,0},{8,12},{5,1},{9,13},{6,2},{10,14},{7,3},{11,15},{20,16},{24,... | collective-permute-start | bytes 2359304 | tf_op jit(solution)/shard_map/ppermute | solution.py:476
  86.1 27.4 %collective-permute-start.20 = (bf16[4,96,1024]{2,1,0:T(8,128)(2,1)S(1)}, bf16[4,96,1024]{2,1,0:T(8,128)(2,1)S(1)}, u32[]{:S(2)}, u32[]{:S(2)}) collective-permute-start(bf16[4,96,1024]{2,1,0:T(8,128)(2,1)S(1)} %get-tuple-element.88.refs_3_.p_ref), channel_id=1, source_target_pairs={{4,8},{8,4},{5,9},{9,5},{6,10},{10,6},{7,11},{11,7},{20,24},{24,20... | collective-permute-start | bytes 2359304 | tf_op jit(solution)/shard_map/ppermute | solution.py:467
  87.0 27.3 %collective-permute-start.18 = (bf16[4,96,1024]{2,1,0:T(8,128)(2,1)S(1)}, bf16[4,96,1024]{2,1,0:T(8,128)(2,1)S(1)}, u32[]{:S(2)}, u32[]{:S(2)}) collective-permute-start(bf16[4,96,1024]{2,1,0:T(8,128)(2,1)S(1)} %shard_map.80.refs_2_.b_ref), channel_id=1, source_target_pairs={{4,0},{8,12},{5,1},{9,13},{6,2},{10,14},{7,3},{11,15},{20,16},{24,... | collective-permute-start | bytes 2359304 | tf_op jit(solution)/shard_map/ppermute | solution.py:476
  88.3 31.4 %collective-permute-start.16 = (bf16[3,64,1024]{2,1,0:T(8,128)(2,1)S(1)}, bf16[3,64,1024]{2,1,0:T(8,128)(2,1)S(1)}, u32[]{:S(2)}, u32[]{:S(2)}) collective-permute-start(bf16[3,64,1024]{2,1,0:T(8,128)(2,1)S(1)} %get-tuple-element.87), channel_id=1, source_target_pairs={{0,4},{12,8},{1,5},{13,9},{2,6},{14,10},{3,7},{15,11},{16,20},{28,... | collective-permute-start | bytes 1179656 | tf_op jit(solution)/shard_map/ppermute | solution.py:469
  106.6 15.0 %collective-permute-start.23 = (bf16[4,96,1024]{2,1,0:T(8,128)(2,1)S(1)}, bf16[4,96,1024]{2,1,0:T(8,128)(2,1)S(1)}, u32[]{:S(2)}, u32[]{:S(2)}) collective-permute-start(bf16[4,96,1024]{2,1,0:T(8,128)(2,1)S(1)} %get-tuple-element.95.refs_0_.p_ref), channel_id=1, source_target_pairs={{4,8},{8,4},{5,9},{9,5},{6,10},{10,6},{7,11},{11,7},{20,24},{24,20... | collective-permute-start | bytes 2359304 | tf_op jit(solution)/shard_map/ppermute | solution.py:467
  107.4 34.4 %collective-permute-start.27 = (bf16[3,64,1024]{2,1,0:T(8,128)(2,1)S(1)}, bf16[3,64,1024]{2,1,0:T(8,128)(2,1)S(1)}, u32[]{:S(2)}, u32[]{:S(2)}) collective-permute-start(bf16[3,64,1024]{2,1,0:T(8,128)(2,1)S(1)} %get-tuple-element.107), channel_id=1, source_target_pairs={{0,4},{12,8},{1,5},{13,9},{2,6},{14,10},{3,7},{15,11},{16,20},{28,... | collective-permute-start | bytes 1179656 | tf_op jit(solution)/shard_map/ppermute | solution.py:469
  118.3 11.5 %collective-permute-start.28 = (f32[3,384,128]{2,1,0:T(8,128)S(1)}, f32[3,384,128]{2,1,0:T(8,128)S(1)}, u32[]{:S(2)}, u32[]{:S(2)}) collective-permute-start(f32[3,384,128]{2,1,0:T(8,128)S(1)} %constant_dynamic-update-slice_fusion), channel_id=1, source_target_pairs={{0,1},{1,0},{2,3},{3,2},{4,5},{5,4},{6,7},{7,6},{8,9},{9,8},{10,11... | collective-permute-start | bytes 1769480 | tf_op jit(solution)/shard_map/ppermute | solution.py:395
  118.4 18.0 %collective-permute-start.25 = (bf16[3,96,1024]{2,1,0:T(8,128)(2,1)S(1)}, bf16[3,96,1024]{2,1,0:T(8,128)(2,1)S(1)}, u32[]{:S(2)}, u32[]{:S(2)}) collective-permute-start(bf16[3,96,1024]{2,1,0:T(8,128)(2,1)S(1)} %get-tuple-element.102), channel_id=1, source_target_pairs={{4,0},{8,12},{5,1},{9,13},{6,2},{10,14},{7,3},{11,15},{20,16},{24,... | collective-permute-start | bytes 1769480 | tf_op jit(solution)/shard_map/ppermute | solution.py:476
  121.0 22.6 %collective-permute-start.26 = (bf16[4,64,1024]{2,1,0:T(8,128)(2,1)S(1)}, bf16[4,64,1024]{2,1,0:T(8,128)(2,1)S(1)}, u32[]{:S(2)}, u32[]{:S(2)}) collective-permute-start(bf16[4,64,1024]{2,1,0:T(8,128)(2,1)S(1)} %get-tuple-element.99.refs_0_.p_ref), channel_id=1, source_target_pairs={{4,8},{8,4},{5,9},{9,5},{6,10},{10,6},{7,11},{11,7},{20,24},{24,20... | collective-permute-start | bytes 1572872 | tf_op jit(solution)/shard_map/ppermute | solution.py:467
  121.7 31.2 %collective-permute-start.22 = (bf16[3,64,1024]{2,1,0:T(8,128)(2,1)S(1)}, bf16[3,64,1024]{2,1,0:T(8,128)(2,1)S(1)}, u32[]{:S(2)}, u32[]{:S(2)}) collective-permute-start(bf16[3,64,1024]{2,1,0:T(8,128)(2,1)S(1)} %get-tuple-element.98), channel_id=1, source_target_pairs={{0,4},{12,8},{1,5},{13,9},{2,6},{14,10},{3,7},{15,11},{16,20},{28,... | collective-permute-start | bytes 1179656 | tf_op jit(solution)/shard_map/ppermute | solution.py:469
  129.7 19.3 %collective-permute-start.24 = (bf16[3,96,1024]{2,1,0:T(8,128)(2,1)S(1)}, bf16[3,96,1024]{2,1,0:T(8,128)(2,1)S(1)}, u32[]{:S(2)}, u32[]{:S(2)}) collective-permute-start(bf16[3,96,1024]{2,1,0:T(8,128)(2,1)S(1)} %get-tuple-element.101), channel_id=1, source_target_pairs={{4,0},{8,12},{5,1},{9,13},{6,2},{10,14},{7,3},{11,15},{20,16},{24,... | collective-permute-start | bytes 1769480 | tf_op jit(solution)/shard_map/ppermute | solution.py:476
  136.4 12.6 %collective-permute-start.29 = (bf16[3,384,128]{2,1,0:T(8,128)(2,1)S(1)}, bf16[3,384,128]{2,1,0:T(8,128)(2,1)S(1)}, u32[]{:S(2)}, u32[]{:S(2)}) collective-permute-start(bf16[3,384,128]{2,1,0:T(8,128)(2,1)S(1)} %add_convert_fusion.1.refs_0_), channel_id=1, source_target_pairs={{0,2},{1,3},{2,0},{3,1},{4,6},{5,7},{6,4},{7,5},{8,10},{9,11},{10,... | collective-permute-start | bytes 884744 | tf_op jit(solution)/shard_map/ppermute | solution.py:395
  142.8 11.9 %collective-permute-start.31 = (bf16[4,64,1024]{2,1,0:T(8,128)(2,1)S(1)}, bf16[4,64,1024]{2,1,0:T(8,128)(2,1)S(1)}, u32[]{:S(2)}, u32[]{:S(2)}) collective-permute-start(bf16[4,64,1024]{2,1,0:T(8,128)(2,1)S(1)} %shard_map.88.refs_0_.p_ref), channel_id=1, source_target_pairs={{4,8},{8,4},{5,9},{9,5},{6,10},{10,6},{7,11},{11,7},{20,24},{24,20... | collective-permute-start | bytes 1572872 | tf_op jit(solution)/shard_map/ppermute | solution.py:467
  144.3 12.7 %collective-permute-start.33 = (bf16[3,64,1024]{2,1,0:T(8,128)(2,1)S(1)}, bf16[3,64,1024]{2,1,0:T(8,128)(2,1)S(1)}, u32[]{:S(2)}, u32[]{:S(2)}) collective-permute-start(bf16[3,64,1024]{2,1,0:T(8,128)(2,1)S(1)} %get-tuple-element.113), channel_id=1, source_target_pairs={{4,0},{8,12},{5,1},{9,13},{6,2},{10,14},{7,3},{11,15},{20,16},{24,... | collective-permute-start | bytes 1179656 | tf_op jit(solution)/shard_map/ppermute | solution.py:476
  154.0 17.1 %collective-permute-start.30 = (bf16[4,64,1024]{2,1,0:T(8,128)(2,1)S(1)}, bf16[4,64,1024]{2,1,0:T(8,128)(2,1)S(1)}, u32[]{:S(2)}, u32[]{:S(2)}) collective-permute-start(bf16[4,64,1024]{2,1,0:T(8,128)(2,1)S(1)} %shard_map.91.refs_0_.p_ref), channel_id=1, source_target_pairs={{4,8},{8,4},{5,9},{9,5},{6,10},{10,6},{7,11},{11,7},{20,24},{24,20... | collective-permute-start | bytes 1572872 | tf_op jit(solution)/shard_map/ppermute | solution.py:467
  155.5 12.6 %collective-permute-start.32 = (bf16[3,64,1024]{2,1,0:T(8,128)(2,1)S(1)}, bf16[3,64,1024]{2,1,0:T(8,128)(2,1)S(1)}, u32[]{:S(2)}, u32[]{:S(2)}) collective-permute-start(bf16[3,64,1024]{2,1,0:T(8,128)(2,1)S(1)} %get-tuple-element.112), channel_id=1, source_target_pairs={{4,0},{8,12},{5,1},{9,13},{6,2},{10,14},{7,3},{11,15},{20,16},{24,... | collective-permute-start | bytes 1179656 | tf_op jit(solution)/shard_map/ppermute | solution.py:476
  160.0 13.1 %collective-permute-start.35 = (f32[3,256,128]{2,1,0:T(8,128)S(1)}, f32[3,256,128]{2,1,0:T(8,128)S(1)}, u32[]{:S(2)}, u32[]{:S(2)}) collective-permute-start(f32[3,256,128]{2,1,0:T(8,128)S(1)} %constant_dynamic-update-slice_fusion.5), channel_id=1, source_target_pairs={{0,1},{1,0},{2,3},{3,2},{4,5},{5,4},{6,7},{7,6},{8,9},{9,8},{10,11... | collective-permute-start | bytes 1179656 | tf_op jit(solution)/shard_map/ppermute | solution.py:395
  171.8 10.4 %collective-permute-start.34 = (bf16[3,64,1024]{2,1,0:T(8,128)(2,1)S(1)}, bf16[3,64,1024]{2,1,0:T(8,128)(2,1)S(1)}, u32[]{:S(2)}, u32[]{:S(2)}) collective-permute-start(bf16[3,64,1024]{2,1,0:T(8,128)(2,1)S(1)} %get-tuple-element.121), channel_id=1, source_target_pairs={{4,0},{8,12},{5,1},{9,13},{6,2},{10,14},{7,3},{11,15},{20,16},{24,... | collective-permute-start | bytes 1179656 | tf_op jit(solution)/shard_map/ppermute | solution.py:476
  173.2 5.7 %collective-permute-start.36 = (bf16[3,256,128]{2,1,0:T(8,128)(2,1)S(1)}, bf16[3,256,128]{2,1,0:T(8,128)(2,1)S(1)}, u32[]{:S(2)}, u32[]{:S(2)}) collective-permute-start(bf16[3,256,128]{2,1,0:T(8,128)(2,1)S(1)} %add_convert_fusion.2.refs_2_), channel_id=1, source_target_pairs={{0,2},{1,3},{2,0},{3,1},{4,6},{5,7},{6,4},{7,5},{8,10},{9,11},{10,... | collective-permute-start | bytes 589832 | tf_op jit(solution)/shard_map/ppermute | solution.py:395
  185.2 1.5 collective-permute-start.37
  186.7 4.9 %collective-permute-start.38 = (bf16[3,128,128]{2,1,0:T(8,128)(2,1)S(1)}, bf16[3,128,128]{2,1,0:T(8,128)(2,1)S(1)}, u32[]{:S(2)}, u32[]{:S(2)}) collective-permute-start(bf16[3,128,128]{2,1,0:T(8,128)(2,1)S(1)} %add_convert_fusion.3.refs_4_), channel_id=1, source_target_pairs={{0,2},{1,3},{2,0},{3,1},{4,6},{5,7},{6,4},{7,5},{8,10},{9,11},{10,... | collective-permute-start | bytes 294920 | tf_op jit(solution)/shard_map/ppermute | solution.py:395
  191.6 2.3 %copy-start = (bf16[3,768,1024]{2,1,0:T(8,128)(2,1)S(1)}, bf16[3,768,1024]{2,1,0:T(8,128)(2,1)}, u32[]{:S(2)}) copy-start(bf16[3,768,1024]{2,1,0:T(8,128)(2,1)} %get-tuple-element.126.refs_6_.refs_4_) | copy-start | bytes 14155780
  194.0 23.7 %copy-start.2 = (bf16[4,224,1024]{2,1,0:T(8,128)(2,1)S(1)}, bf16[4,224,1024]{2,1,0:T(8,128)(2,1)}, u32[]{:S(2)}) copy-start(bf16[4,224,1024]{2,1,0:T(8,128)(2,1)} %get-tuple-element.124.in_ref) | copy-start | bytes 5505028
  194.0 25.2 %copy-start.1 = (bf16[3,768,1024]{2,1,0:T(8,128)(2,1)S(1)}, bf16[3,768,1024]{2,1,0:T(8,128)(2,1)}, u32[]{:S(2)}) copy-start(bf16[3,768,1024]{2,1,0:T(8,128)(2,1)} %get-tuple-element.126.refs_6_.refs_4_) | copy-start | bytes 14155780
  206.4 2.1 collective-permute-start.39
  208.5 9.1 %collective-permute-start.40 = (bf16[3,384,128]{2,1,0:T(8,128)(2,1)S(1)}, bf16[3,384,128]{2,1,0:T(8,128)(2,1)S(1)}, u32[]{:S(2)}, u32[]{:S(2)}) collective-permute-start(bf16[3,384,128]{2,1,0:T(8,128)(2,1)S(1)} %add_convert_fusion.refs_0_), channel_id=1, source_target_pairs={{0,2},{1,3},{2,0},{3,1},{4,6},{5,7},{6,4},{7,5},{8,10},{9,11},{10,... | collective-permute-start | bytes 884744 | tf_op jit(solution)/shard_map/ppermute | solution.py:395
  210.3 8.6 %collective-permute-start.41 = (bf16[3,384,128]{2,1,0:T(8,128)(2,1)S(1)}, bf16[3,384,128]{2,1,0:T(8,128)(2,1)S(1)}, u32[]{:S(2)}, u32[]{:S(2)}) collective-permute-start(bf16[3,384,128]{2,1,0:T(8,128)(2,1)S(1)} %add_convert_fusion.refs_0_), channel_id=1, source_target_pairs={{0,1},{1,0},{2,3},{3,2},{4,5},{5,4},{6,7},{7,6},{8,9},{9,8},{10,11... | collective-permute-start | bytes 884744 | tf_op jit(solution)/shard_map/ppermute | solution.py:395
  217.6 1.6 collective-permute-start.42

commit v3 on v0

--- a/solution.py
+++ b/solution.py
@@ -326,7 +326,9 @@
     for e in range(experts):
         back = contract(start[e], held[e], ((0,), (0,))).astype(jnp.bfloat16)
         keep_ref[e] = contract(held[e, pl.ds(own, half)], back, ((1,), (1,)))
-        send_ref[e] = contract(held[e, pl.ds(other, half)], back, ((1,), (1,)))
+        send_ref[e] = contract(held[e, pl.ds(other, half)], back, ((1,), (1,))).astype(
+            jnp.bfloat16
+        )
 
 
 def power_step(side, groups, delta):
@@ -340,7 +342,7 @@
         functools.partial(power_kernel, splits, pieces),
         in_specs=[SMEM] + [vmem] * sum(splits) + [HBM],
         out_specs=[vmem] * 2,
-        out_shape=[part, part],
+        out_shape=[part, jax.ShapeDtypeStruct(part.shape, jnp.bfloat16)],
         scratch_shapes=[
             pltpu.VMEM((experts, units, rank), jnp.float32),
             pltpu.VMEM(delta.shape, jnp.bfloat16),
@@ -405,7 +407,7 @@
 
 
 def sum_halves(keep, send, size):
-    total = (keep + swap(send, 1, size)).astype(jnp.bfloat16)
+    total = (keep + swap(send, 1, size).astype(jnp.float32)).astype(jnp.bfloat16)
     bit = 2
     while 2 * bit < size:
         total = (total.astype(jnp.float32) + swap(total, bit, size).astype(jnp.float32)).astype(

time: 231 us -> 231 us (level)
  no operation moved by 1% of the time
where the time goes in v3:
time: 231 us; the launch traced here: 229 us
  starting transfers between devices  100 us (43%)
  Pallas kernels  81.5 us (35%)
  waiting for transfers between devices  37.3 us (16%)
  local copies, waits for them, and re-layouts  5.76 us (2%)
  other arithmetic  2.68 us (1%)
    ppermute x8, starting transfers between devices, merge_folded(): arrived[c + lead] = lax.ppermute(copied[0], 'exp', inwards)  62.6 us
    pallas_call x10, Pallas kernels, residual_chunk(): pl.pallas_call(residual_kernel, grid_spec=pltpu.PrefetchScalarGridSpec(nu...  34.6 us
    ppermute x10, waiting for transfers between devices, merge_folded(): moved[c] = lax.ppermute(leaving, 'exp', outwards)  20.5 us
    pallas_call x10, Pallas kernels, cluster_sums(): pl.pallas_call(functools.partial(sums_kernel, ahead is not None), grid_sp...  16.2 us
    ppermute x10, starting transfers between devices, merge_folded(): moved[c] = lax.ppermute(leaving, 'exp', outwards)  13.1 us
    ppermute x10, waiting for transfers between devices, swap(): return lax.ppermute(value, 'col', [(i, i ^ bit) for i in range(size)])  13.1 us
    pallas_call x1, Pallas kernels, power_step(): pl.pallas_call(functools.partial(power_kernel, splits, pieces), in_specs=...  12.4 us
    pallas_call x1, Pallas kernels, project(): pl.pallas_call(project_kernel, in_specs=[SMEM] + [vmem] * (len(mine) + le...  12.4 us
  transfers between devices with their start and end apart: 43, of which 10 were waited for; matrix products, arithmetic and copies ran while one was open for 2% of the time, Pallas kernels for 24%

profile of v3, /device:TPU:0, one launch (start us, length us, event | category | flops | bytes accessed | tf_op | source)
XLA Modules:
  0.0 228.9 jit_solution(6271045814208174502)
XLA Ops:
  1.6 3.1 %collective-permute-start.1 = (bf16[3,768]{1,0:T(4,128)(2,1)}, bf16[3,768]{1,0:T(4,128)(2,1)S(1)}, u32[]{:S(2)}, u32[]{:S(2)}) collective-permute-start(bf16[3,768]{1,0:T(4,128)(2,1)} %param.5), channel_id=1, source_target_pairs={{0,4},{4,0},{8,12},{12,8},{1,5},{5,1},{9,13},{13,9},{2,6},{6,2},{1... | collective-permute-start | bytes 13832 | tf_op jit(solution)/shard_map/ppermute | solution.py:436
  4.7 2.6 %collective-permute-start.5 = (bf16[3,768]{1,0:T(4,128)(2,1)}, bf16[3,768]{1,0:T(4,128)(2,1)S(1)}, u32[]{:S(2)}, u32[]{:S(2)}) collective-permute-start(bf16[3,768]{1,0:T(4,128)(2,1)} %param.5), channel_id=1, source_target_pairs={{0,8},{4,12},{8,0},{12,4},{1,9},{5,13},{9,1},{13,5},{2,10},{6,14},... | collective-permute-start | bytes 13832 | tf_op jit(solution)/shard_map/ppermute | solution.py:436
  7.3 2.8 %collective-permute-start.2 = (bf16[3,32,1024]{2,1,0:T(8,128)(2,1)S(1)}, bf16[3,32,1024]{2,1,0:T(8,128)(2,1)S(1)}, u32[]{:S(2)}, u32[]{:S(2)}) collective-permute-start(bf16[3,32,1024]{2,1,0:T(8,128)(2,1)S(1)} %slice.7), channel_id=1, source_target_pairs={{0,4},{12,8},{1,5},{13,9},{2,6},{14,10},{3,7},{15,11},{16,20},{28,... | collective-permute-start | bytes 589832 | tf_op jit(solution)/shard_map/ppermute | solution.py:456
  11.1 1.3 collective-permute-start
  18.3 6.7 %collective-permute-start.9 = (bf16[3,96,1024]{2,1,0:T(8,128)(2,1)S(1)}, bf16[3,96,1024]{2,1,0:T(8,128)(2,1)S(1)}, u32[]{:S(2)}, u32[]{:S(2)}) collective-permute-start(bf16[3,96,1024]{2,1,0:T(8,128)(2,1)S(1)} %get-tuple-element.74), channel_id=1, source_target_pairs={{0,4},{12,8},{1,5},{13,9},{2,6},{14,10},{3,7},{15,11},{16,20},{28,... | collective-permute-start | bytes 1769480 | tf_op jit(solution)/shard_map/ppermute | solution.py:471
  25.1 1.4 shard_map.68
  27.1 6.4 %collective-permute-start.3 = (bf16[3,96,1024]{2,1,0:T(8,128)(2,1)S(1)}, bf16[3,96,1024]{2,1,0:T(8,128)(2,1)S(1)}, u32[]{:S(2)}, u32[]{:S(2)}) collective-permute-start(bf16[3,96,1024]{2,1,0:T(8,128)(2,1)S(1)} %get-tuple-element.72), channel_id=1, source_target_pairs={{0,4},{12,8},{1,5},{13,9},{2,6},{14,10},{3,7},{15,11},{16,20},{28,... | collective-permute-start | bytes 1769480 | tf_op jit(solution)/shard_map/ppermute | solution.py:471
  34.9 3.6 %collective-permute-done.9.a_ref = bf16[3,96,1024]{2,1,0:T(8,128)(2,1)S(1)} collective-permute-done((bf16[3,96,1024]{2,1,0:T(8,128)(2,1)S(1)}, bf16[3,96,1024]{2,1,0:T(8,128)(2,1)S(1)}, u32[]{:S(2)}, u32[]{:S(2)}) %collective-permute-start.9) | collective-permute-done | bytes 589856 | tf_op jit(solution)/shard_map/ppermute | solution.py:471
  38.5 2.2 shard_map.70
  41.4 7.4 %collective-permute-start.15 = (bf16[3,96,1024]{2,1,0:T(8,128)(2,1)S(1)}, bf16[3,96,1024]{2,1,0:T(8,128)(2,1)S(1)}, u32[]{:S(2)}, u32[]{:S(2)}) collective-permute-start(bf16[3,96,1024]{2,1,0:T(8,128)(2,1)S(1)} %get-tuple-element.83), channel_id=1, source_target_pairs={{0,4},{12,8},{1,5},{13,9},{2,6},{14,10},{3,7},{15,11},{16,20},{28,... | collective-permute-start | bytes 1769480 | tf_op jit(solution)/shard_map/ppermute | solution.py:471
  50.3 2.5 %shard_map.72 = (bf16[3,768,1024]{2,1,0:T(8,128)(2,1)}, bf16[4,224,1024]{2,1,0:T(8,128)(2,1)}, f32[3,32,128]{2,1,0:T(8,128)S(1)}) custom-call(s32[5]{0:T(128)S(1)} %pad_add_fusion.meta, bf16[3,768,1024]{2,1,0:T(8,128)(2,1)} %w_ref.39, bf16[4,32,1024]{2,1,0:T(8,128)(2,1)S(1)} %shard_map.69.refs_1_.b_ref, ...), custom_call_target="tpu_custom_call" | custom-call | flops 10000000000 | bytes 1 | tf_op jit(solution)/shard_map/pallas_call | solution.py:195
  52.9 2.2 shard_map.73
  55.8 8.3 %collective-permute-start.10 = (bf16[3,96,1024]{2,1,0:T(8,128)(2,1)S(1)}, bf16[3,96,1024]{2,1,0:T(8,128)(2,1)S(1)}, u32[]{:S(2)}, u32[]{:S(2)}) collective-permute-start(bf16[3,96,1024]{2,1,0:T(8,128)(2,1)S(1)} %get-tuple-element.77), channel_id=1, source_target_pairs={{0,4},{12,8},{1,5},{13,9},{2,6},{14,10},{3,7},{15,11},{16,20},{28,... | collective-permute-start | bytes 1769480 | tf_op jit(solution)/shard_map/ppermute | solution.py:471
  65.7 3.0 %shard_map.75 = (bf16[3,768,1024]{2,1,0:T(8,128)(2,1)}, bf16[4,224,1024]{2,1,0:T(8,128)(2,1)}, f32[3,64,128]{2,1,0:T(8,128)S(1)}) custom-call(s32[5]{0:T(128)S(1)} %pad_add_fusion.meta, bf16[3,768,1024]{2,1,0:T(8,128)(2,1)} %w_ref.39, bf16[4,64,1024]{2,1,0:T(8,128)(2,1)S(1)} %shard_map.71.refs_0_.b_ref, ...), custom_call_target="tpu_custom_call", output_to_operand_aliasing={{0}: (5, {}), {1}: (6, {})} | custom-call | flops 10000000000 | bytes 1 | tf_op jit(solution)/shard_map/pallas_call | solution.py:195
  68.6 2.2 shard_map.76
  71.6 7.5 %collective-permute-start.21 = (bf16[3,96,1024]{2,1,0:T(8,128)(2,1)S(1)}, bf16[3,96,1024]{2,1,0:T(8,128)(2,1)S(1)}, u32[]{:S(2)}, u32[]{:S(2)}) collective-permute-start(bf16[3,96,1024]{2,1,0:T(8,128)(2,1)S(1)} %get-tuple-element.93), channel_id=1, source_target_pairs={{0,4},{12,8},{1,5},{13,9},{2,6},{14,10},{3,7},{15,11},{16,20},{28,... | collective-permute-start | bytes 1769480 | tf_op jit(solution)/shard_map/ppermute | solution.py:471
  80.6 4.0 %shard_map.78 = (bf16[3,768,1024]{2,1,0:T(8,128)(2,1)}, bf16[4,224,1024]{2,1,0:T(8,128)(2,1)}, f32[3,96,128]{2,1,0:T(8,128)S(1)}) custom-call(s32[5]{0:T(128)S(1)} %pad_add_fusion.meta, bf16[3,768,1024]{2,1,0:T(8,128)(2,1)} %w_ref.39, bf16[4,96,1024]{2,1,0:T(8,128)(2,1)S(1)} %shard_map.74.refs_2_.b_ref, ...), custom_call_target="tpu_custom_call", output_to_operand_aliasing={{0}: (5, {}), {1}: (6, {})} | custom-call | flops 10000000000 | bytes 1 | tf_op jit(solution)/shard_map/pallas_call | solution.py:195
  84.6 2.2 shard_map.79
  87.8 1.3 collective-permute-start.18
  89.1 12.2 %collective-permute-start.16 = (bf16[3,96,1024]{2,1,0:T(8,128)(2,1)S(1)}, bf16[3,96,1024]{2,1,0:T(8,128)(2,1)S(1)}, u32[]{:S(2)}, u32[]{:S(2)}) collective-permute-start(bf16[3,96,1024]{2,1,0:T(8,128)(2,1)S(1)} %get-tuple-element.87), channel_id=1, source_target_pairs={{0,4},{12,8},{1,5},{13,9},{2,6},{14,10},{3,7},{15,11},{16,20},{28,... | collective-permute-start | bytes 1769480 | tf_op jit(solution)/shard_map/ppermute | solution.py:471
  101.3 3.9 %shard_map.81 = (bf16[3,768,1024]{2,1,0:T(8,128)(2,1)}, bf16[4,224,1024]{2,1,0:T(8,128)(2,1)}, f32[3,96,128]{2,1,0:T(8,128)S(1)}) custom-call(s32[5]{0:T(128)S(1)} %pad_add_fusion.meta, bf16[3,768,1024]{2,1,0:T(8,128)(2,1)} %w_ref.39, bf16[4,96,1024]{2,1,0:T(8,128)(2,1)S(1)} %shard_map.77.refs_2_.b_ref, ...), custom_call_target="tpu_custom_call", output_to_operand_aliasing={{0}: (5, {}), {1}: (6, {})} | custom-call | flops 10000000000 | bytes 1 | tf_op jit(solution)/shard_map/pallas_call | solution.py:195
  105.2 1.4 shard_map.82
  107.4 6.1 %collective-permute-start.27 = (bf16[3,64,1024]{2,1,0:T(8,128)(2,1)S(1)}, bf16[3,64,1024]{2,1,0:T(8,128)(2,1)S(1)}, u32[]{:S(2)}, u32[]{:S(2)}) collective-permute-start(bf16[3,64,1024]{2,1,0:T(8,128)(2,1)S(1)} %get-tuple-element.107), channel_id=1, source_target_pairs={{0,4},{12,8},{1,5},{13,9},{2,6},{14,10},{3,7},{15,11},{16,20},{28,... | collective-permute-start | bytes 1179656 | tf_op jit(solution)/shard_map/ppermute | solution.py:471
  114.3 3.9 %shard_map.84 = (bf16[3,768,1024]{2,1,0:T(8,128)(2,1)}, bf16[4,224,1024]{2,1,0:T(8,128)(2,1)}, f32[3,96,128]{2,1,0:T(8,128)S(1)}) custom-call(s32[5]{0:T(128)S(1)} %pad_add_fusion.meta, bf16[3,768,1024]{2,1,0:T(8,128)(2,1)} %w_ref.39, bf16[4,96,1024]{2,1,0:T(8,128)(2,1)S(1)} %shard_map.80.refs_2_.b_ref, ...), custom_call_target="tpu_custom_call", output_to_operand_aliasing={{0}: (5, {}), {1}: (6, {})} | custom-call | flops 10000000000 | bytes 1 | tf_op jit(solution)/shard_map/pallas_call | solution.py:195
  119.7 1.3 shard_map.85
  121.7 8.0 %collective-permute-start.22 = (bf16[3,32,1024]{2,1,0:T(8,128)(2,1)S(1)}, bf16[3,32,1024]{2,1,0:T(8,128)(2,1)S(1)}, u32[]{:S(2)}, u32[]{:S(2)}) collective-permute-start(bf16[3,32,1024]{2,1,0:T(8,128)(2,1)S(1)} %get-tuple-element.98), channel_id=1, source_target_pairs={{0,4},{12,8},{1,5},{13,9},{2,6},{14,10},{3,7},{15,11},{16,20},{28,... | collective-permute-start | bytes 589832 | tf_op jit(solution)/shard_map/ppermute | solution.py:471
  132.0 4.4 %collective-permute-done.25.r_ref = bf16[3,96,1024]{2,1,0:T(8,128)(2,1)S(1)} collective-permute-done((bf16[3,96,1024]{2,1,0:T(8,128)(2,1)S(1)}, bf16[3,96,1024]{2,1,0:T(8,128)(2,1)S(1)}, u32[]{:S(2)}, u32[]{:S(2)}) %collective-permute-start.25) | collective-permute-done | bytes 589856 | tf_op jit(solution)/shard_map/ppermute | solution.py:478
  136.4 1.5 collective-permute-start.29
  137.9 3.9 %shard_map.87 = (bf16[3,768,1024]{2,1,0:T(8,128)(2,1)}, bf16[4,224,1024]{2,1,0:T(8,128)(2,1)}, f32[3,96,128]{2,1,0:T(8,128)S(1)}) custom-call(s32[5]{0:T(128)S(1)} %pad_add_fusion.meta, bf16[3,768,1024]{2,1,0:T(8,128)(2,1)} %w_ref.39, bf16[4,96,1024]{2,1,0:T(8,128)(2,1)S(1)} %get-tuple-element.96.refs_2_.b_ref, ...), custom_call_target="tpu_custom_call", output_to_operand_aliasing={{0}: (5, {}), {1}: (6, {})} | custom-call | flops 10000000000 | bytes 1 | tf_op jit(solution)/shard_map/pallas_call | solution.py:195
  145.7 2.9 %collective-permute-done.24.r_ref = bf16[3,96,1024]{2,1,0:T(8,128)(2,1)S(1)} collective-permute-done((bf16[3,96,1024]{2,1,0:T(8,128)(2,1)S(1)}, bf16[3,96,1024]{2,1,0:T(8,128)(2,1)S(1)}, u32[]{:S(2)}, u32[]{:S(2)}) %collective-permute-start.24) | collective-permute-done | bytes 589856 | tf_op jit(solution)/shard_map/ppermute | solution.py:478
  148.6 3.9 %shard_map.90 = (bf16[3,768,1024]{2,1,0:T(8,128)(2,1)}, bf16[4,224,1024]{2,1,0:T(8,128)(2,1)}, f32[3,96,128]{2,1,0:T(8,128)S(1)}) custom-call(s32[5]{0:T(128)S(1)} %pad_add_fusion.meta, bf16[3,768,1024]{2,1,0:T(8,128)(2,1)} %w_ref.39, bf16[4,96,1024]{2,1,0:T(8,128)(2,1)S(1)} %get-tuple-element.100.refs_2_.b_ref, ...), custom_call_target="tpu_custom_call", output_to_operand_aliasing={{0}: (5, {}), {1}: (6, {})} | custom-call | flops 10000000000 | bytes 1 | tf_op jit(solution)/shard_map/pallas_call | solution.py:195
  155.0 1.5 collective-permute-start.34
  156.4 7.4 %collective-permute-done.31.r_ref = bf16[3,96,1024]{2,1,0:T(8,128)(2,1)S(1)} collective-permute-done((bf16[3,96,1024]{2,1,0:T(8,128)(2,1)S(1)}, bf16[3,96,1024]{2,1,0:T(8,128)(2,1)S(1)}, u32[]{:S(2)}, u32[]{:S(2)}) %collective-permute-start.31) | collective-permute-done | bytes 589856 | tf_op jit(solution)/shard_map/ppermute | solution.py:478
  163.9 3.9 %shard_map.93 = (bf16[3,768,1024]{2,1,0:T(8,128)(2,1)}, bf16[4,224,1024]{2,1,0:T(8,128)(2,1)}, f32[3,96,128]{2,1,0:T(8,128)S(1)}) custom-call(s32[5]{0:T(128)S(1)} %pad_add_fusion.meta, bf16[3,768,1024]{2,1,0:T(8,128)(2,1)} %w_ref.39, bf16[4,96,1024]{2,1,0:T(8,128)(2,1)S(1)} %get-tuple-element.109.refs_2_.b_ref, ...), custom_call_target="tpu_custom_call", output_to_operand_aliasing={{0}: (5, {}), {1}: (6, {})} | custom-call | flops 10000000000 | bytes 1 | tf_op jit(solution)/shard_map/pallas_call | solution.py:195
  169.8 2.0 collective-permute-start.36
  171.8 5.8 %collective-permute-done.33.refs_3_.r_ref = bf16[3,32,1024]{2,1,0:T(8,128)(2,1)S(1)} collective-permute-done((bf16[3,32,1024]{2,1,0:T(8,128)(2,1)S(1)}, bf16[3,32,1024]{2,1,0:T(8,128)(2,1)S(1)}, u32[]{:S(2)}, u32[]{:S(2)}) %collective-permute-start.33) | collective-permute-done | bytes 196640 | tf_op jit(solution)/shard_map/ppermute | solution.py:478
  177.6 3.0 %shard_map.95 = (bf16[3,768,1024]{2,1,0:T(8,128)(2,1)}, bf16[4,224,1024]{2,1,0:T(8,128)(2,1)}, f32[3,64,128]{2,1,0:T(8,128)S(1)}) custom-call(s32[5]{0:T(128)S(1)} %pad_add_fusion.meta, bf16[3,768,1024]{2,1,0:T(8,128)(2,1)} %w_ref.39, bf16[4,64,1024]{2,1,0:T(8,128)(2,1)S(1)} %get-tuple-element.114.refs_2_.b_ref, ...), custom_call_target="tpu_custom_call", output_to_operand_aliasing={{0}: (5, {}), {1}: (6, {})} | custom-call | flops 10000000000 | bytes 1 | tf_op jit(solution)/shard_map/pallas_call | solution.py:195
  180.6 2.6 %shard_map.96 = (bf16[3,768,1024]{2,1,0:T(8,128)(2,1)}, bf16[4,224,1024]{2,1,0:T(8,128)(2,1)}, f32[3,32,128]{2,1,0:T(8,128)S(1)}) custom-call(s32[5]{0:T(128)S(1)} %pad_add_fusion.meta, bf16[3,768,1024]{2,1,0:T(8,128)(2,1)} %w_ref.39, bf16[4,32,1024]{2,1,0:T(8,128)(2,1)S(1)} %get-tuple-element.116.refs_2_.b_ref, ...), custom_call_target="tpu_custom_call", output_to_operand_aliasing={{0}: (5, {}), {1}: (6, {})} | custom-call | flops 10000000000 | bytes 1 | tf_op jit(solution)/shard_map/pallas_call | solution.py:195
  183.2 1.4 collective-permute-done.37
  184.6 2.0 collective-permute-start.38
  186.6 2.6 %collective-permute-done.38.refs_5_ = bf16[3,96,128]{2,1,0:T(8,128)(2,1)S(1)} collective-permute-done((bf16[3,96,128]{2,1,0:T(8,128)(2,1)S(1)}, bf16[3,96,128]{2,1,0:T(8,128)(2,1)S(1)}, u32[]{:S(2)}, u32[]{:S(2)}) %collective-permute-start.38) | collective-permute-done | bytes 73760 | tf_op jit(solution)/shard_map/ppermute | solution.py:397
  189.2 2.3 %copy-done = bf16[3,768,1024]{2,1,0:T(8,128)(2,1)S(1)} copy-done((bf16[3,768,1024]{2,1,0:T(8,128)(2,1)S(1)}, bf16[3,768,1024]{2,1,0:T(8,128)(2,1)}, u32[]{:S(2)}) %copy-start) | copy-done | bytes 4718616
  191.5 12.4 %shard_map.98 = (f32[3,384,128]{2,1,0:T(8,128)S(1)}, bf16[3,384,128]{2,1,0:T(8,128)(2,1)S(1)}) custom-call(s32[1]{0:T(128)} %bitcast.3.side, bf16[3,384,128]{2,1,0:T(8,128)(2,1)S(1)} %add_convert_fusion.1.refs_0_, bf16[3,384,128]{2,1,0:T(8,128)(2,1)S(1)} %collective-permute-done.29.refs_3_.refs_1_, bf16[3,288,128]{2,1,0:T(8,128)(2,1)S(1)} %add_convert_fusion.2.refs_2_, ...), custom_call_target="tpu_custom_call" | custom-call | tf_op jit(solution)/shard_map/pallas_call | solution.py:341
  204.0 1.6 collective-permute-done.39
  205.7 1.8 collective-permute-start.40
  207.5 7.3 %collective-permute-done.40.refs_1_ = bf16[3,384,128]{2,1,0:T(8,128)(2,1)S(1)} collective-permute-done((bf16[3,384,128]{2,1,0:T(8,128)(2,1)S(1)}, bf16[3,384,128]{2,1,0:T(8,128)(2,1)S(1)}, u32[]{:S(2)}, u32[]{:S(2)}) %collective-permute-start.40) | collective-permute-done | bytes 294944 | tf_op jit(solution)/shard_map/ppermute | solution.py:397
  214.8 1.3 shard_map.97
  216.4 12.4 %shard_map.99 = (bf16[3,768,128]{2,1,0:T(8,128)(2,1)}, bf16[3,128,1024]{2,1,0:T(8,128)(2,1)}) custom-call(s32[1]{0:T(128)} %bitcast.3.side, bf16[3,384,128]{2,1,0:T(8,128)(2,1)S(1)} %add_convert_fusion.refs_0_, bf16[3,384,128]{2,1,0:T(8,128)(2,1)S(1)} %collective-permute-done.40.refs_1_, bf16[3,384,128]{2,1,0:T(8,128)(2,1)S(1)} %collective-permute-done.41.refs_2_, ...), custom_call_target="tpu_custom_call" | custom-call | tf_op jit(solution)/shard_map/pallas_call | solution.py:379
  (116 shorter events, 31.8 us)
Async XLA Ops:
  1.6 13.8 %collective-permute-start.1 = (bf16[3,768]{1,0:T(4,128)(2,1)}, bf16[3,768]{1,0:T(4,128)(2,1)S(1)}, u32[]{:S(2)}, u32[]{:S(2)}) collective-permute-start(bf16[3,768]{1,0:T(4,128)(2,1)} %param.5), channel_id=1, source_target_pairs={{0,4},{4,0},{8,12},{12,8},{1,5},{5,1},{9,13},{13,9},{2,6},{6,2},{1... | collective-permute-start | bytes 13832 | tf_op jit(solution)/shard_map/ppermute | solution.py:436
  4.7 10.8 %collective-permute-start.5 = (bf16[3,768]{1,0:T(4,128)(2,1)}, bf16[3,768]{1,0:T(4,128)(2,1)S(1)}, u32[]{:S(2)}, u32[]{:S(2)}) collective-permute-start(bf16[3,768]{1,0:T(4,128)(2,1)} %param.5), channel_id=1, source_target_pairs={{0,8},{4,12},{8,0},{12,4},{1,9},{5,13},{9,1},{13,5},{2,10},{6,14},... | collective-permute-start | bytes 13832 | tf_op jit(solution)/shard_map/ppermute | solution.py:436
  7.3 8.7 %collective-permute-start.6 = (bf16[3,768]{1,0:T(4,128)(2,1)}, bf16[3,768]{1,0:T(4,128)(2,1)S(1)}, u32[]{:S(2)}, u32[]{:S(2)}) collective-permute-start(bf16[3,768]{1,0:T(4,128)(2,1)} %param.5), channel_id=1, source_target_pairs={{0,12},{4,8},{8,4},{12,0},{1,13},{5,9},{9,5},{13,1},{2,14},{6,10},... | collective-permute-start | bytes 13832 | tf_op jit(solution)/shard_map/ppermute | solution.py:436
  7.3 9.1 %collective-permute-start.2 = (bf16[3,32,1024]{2,1,0:T(8,128)(2,1)S(1)}, bf16[3,32,1024]{2,1,0:T(8,128)(2,1)S(1)}, u32[]{:S(2)}, u32[]{:S(2)}) collective-permute-start(bf16[3,32,1024]{2,1,0:T(8,128)(2,1)S(1)} %slice.7), channel_id=1, source_target_pairs={{0,4},{12,8},{1,5},{13,9},{2,6},{14,10},{3,7},{15,11},{16,20},{28,... | collective-permute-start | bytes 589832 | tf_op jit(solution)/shard_map/ppermute | solution.py:456
  11.1 14.0 %collective-permute-start = (bf16[3,64,1024]{2,1,0:T(8,128)(2,1)S(1)}, bf16[3,64,1024]{2,1,0:T(8,128)(2,1)S(1)}, u32[]{:S(2)}, u32[]{:S(2)}) collective-permute-start(bf16[3,64,1024]{2,1,0:T(8,128)(2,1)S(1)} %slice.6), channel_id=1, source_target_pairs={{0,4},{12,8},{1,5},{13,9},{2,6},{14,10},{3,7},{15,11},{16,20},{28,... | collective-permute-start | bytes 1179656 | tf_op jit(solution)/shard_map/ppermute | solution.py:456
  17.6 16.0 %collective-permute-start.4 = (bf16[4,32,1024]{2,1,0:T(8,128)(2,1)S(1)}, bf16[4,32,1024]{2,1,0:T(8,128)(2,1)S(1)}, u32[]{:S(2)}, u32[]{:S(2)}) collective-permute-start(bf16[4,32,1024]{2,1,0:T(8,128)(2,1)S(1)} %get-tuple-element.71.refs_1_.refs_0_), channel_id=1, source_target_pairs={{4,8},{8,4},{5,9},{9,5},{6,10},{10,6},{7,11},{11,7},{20,24},{24,20... | collective-permute-start | bytes 786440 | tf_op jit(solution)/shard_map/ppermute | solution.py:469
  18.3 20.2 %collective-permute-start.9 = (bf16[3,96,1024]{2,1,0:T(8,128)(2,1)S(1)}, bf16[3,96,1024]{2,1,0:T(8,128)(2,1)S(1)}, u32[]{:S(2)}, u32[]{:S(2)}) collective-permute-start(bf16[3,96,1024]{2,1,0:T(8,128)(2,1)S(1)} %get-tuple-element.74), channel_id=1, source_target_pairs={{0,4},{12,8},{1,5},{13,9},{2,6},{14,10},{3,7},{15,11},{16,20},{28,... | collective-permute-start | bytes 1769480 | tf_op jit(solution)/shard_map/ppermute | solution.py:471
  26.4 22.4 %collective-permute-start.8 = (bf16[4,64,1024]{2,1,0:T(8,128)(2,1)S(1)}, bf16[4,64,1024]{2,1,0:T(8,128)(2,1)S(1)}, u32[]{:S(2)}, u32[]{:S(2)}) collective-permute-start(bf16[4,64,1024]{2,1,0:T(8,128)(2,1)S(1)} %get-tuple-element.73.refs_3_.refs_0_), channel_id=1, source_target_pairs={{4,8},{8,4},{5,9},{9,5},{6,10},{10,6},{7,11},{11,7},{20,24},{24,20... | collective-permute-start | bytes 1572872 | tf_op jit(solution)/shard_map/ppermute | solution.py:469
  27.1 25.7 %collective-permute-start.3 = (bf16[3,96,1024]{2,1,0:T(8,128)(2,1)S(1)}, bf16[3,96,1024]{2,1,0:T(8,128)(2,1)S(1)}, u32[]{:S(2)}, u32[]{:S(2)}) collective-permute-start(bf16[3,96,1024]{2,1,0:T(8,128)(2,1)S(1)} %get-tuple-element.72), channel_id=1, source_target_pairs={{0,4},{12,8},{1,5},{13,9},{2,6},{14,10},{3,7},{15,11},{16,20},{28,... | collective-permute-start | bytes 1769480 | tf_op jit(solution)/shard_map/ppermute | solution.py:471
  33.6 16.7 %collective-permute-start.7 = (bf16[4,32,1024]{2,1,0:T(8,128)(2,1)S(1)}, bf16[4,32,1024]{2,1,0:T(8,128)(2,1)S(1)}, u32[]{:S(2)}, u32[]{:S(2)}) collective-permute-start(bf16[4,32,1024]{2,1,0:T(8,128)(2,1)S(1)} %shard_map.69.refs_1_.b_ref), channel_id=1, source_target_pairs={{4,0},{8,12},{5,1},{9,13},{6,2},{10,14},{7,3},{11,15},{20,16},{24,... | collective-permute-start | bytes 786440 | tf_op jit(solution)/shard_map/ppermute | solution.py:478
  40.7 23.5 %collective-permute-start.11 = (bf16[4,96,1024]{2,1,0:T(8,128)(2,1)S(1)}, bf16[4,96,1024]{2,1,0:T(8,128)(2,1)S(1)}, u32[]{:S(2)}, u32[]{:S(2)}) collective-permute-start(bf16[4,96,1024]{2,1,0:T(8,128)(2,1)S(1)} %get-tuple-element.75.refs_3_.refs_0_), channel_id=1, source_target_pairs={{4,8},{8,4},{5,9},{9,5},{6,10},{10,6},{7,11},{11,7},{20,24},{24,20... | collective-permute-start | bytes 2359304 | tf_op jit(solution)/shard_map/ppermute | solution.py:469
  41.4 8.9 %copy-start.3 = (bf16[3,1024,128]{2,1,0:T(8,128)(2,1)S(1)}, bf16[3,1024,128]{2,1,0:T(8,128)(2,1)}, u32[]{:S(2)}) copy-start(bf16[3,1024,128]{2,1,0:T(8,128)(2,1)} %s_ref.19) | copy-start | bytes 2359300
  41.4 27.2 %collective-permute-start.15 = (bf16[3,96,1024]{2,1,0:T(8,128)(2,1)S(1)}, bf16[3,96,1024]{2,1,0:T(8,128)(2,1)S(1)}, u32[]{:S(2)}, u32[]{:S(2)}) collective-permute-start(bf16[3,96,1024]{2,1,0:T(8,128)(2,1)S(1)} %get-tuple-element.83), channel_id=1, source_target_pairs={{0,4},{12,8},{1,5},{13,9},{2,6},{14,10},{3,7},{15,11},{16,20},{28,... | collective-permute-start | bytes 1769480 | tf_op jit(solution)/shard_map/ppermute | solution.py:471
  49.0 16.7 %collective-permute-start.13 = (bf16[4,64,1024]{2,1,0:T(8,128)(2,1)S(1)}, bf16[4,64,1024]{2,1,0:T(8,128)(2,1)S(1)}, u32[]{:S(2)}, u32[]{:S(2)}) collective-permute-start(bf16[4,64,1024]{2,1,0:T(8,128)(2,1)S(1)} %shard_map.71.refs_0_.b_ref), channel_id=1, source_target_pairs={{4,0},{8,12},{5,1},{9,13},{6,2},{10,14},{7,3},{11,15},{20,16},{24,... | collective-permute-start | bytes 1572872 | tf_op jit(solution)/shard_map/ppermute | solution.py:478
  55.1 24.0 %collective-permute-start.14 = (bf16[4,96,1024]{2,1,0:T(8,128)(2,1)S(1)}, bf16[4,96,1024]{2,1,0:T(8,128)(2,1)S(1)}, u32[]{:S(2)}, u32[]{:S(2)}) collective-permute-start(bf16[4,96,1024]{2,1,0:T(8,128)(2,1)S(1)} %get-tuple-element.78.refs_3_.refs_0_), channel_id=1, source_target_pairs={{4,8},{8,4},{5,9},{9,5},{6,10},{10,6},{7,11},{11,7},{20,24},{24,20... | collective-permute-start | bytes 2359304 | tf_op jit(solution)/shard_map/ppermute | solution.py:469
  55.8 28.8 %collective-permute-start.10 = (bf16[3,96,1024]{2,1,0:T(8,128)(2,1)S(1)}, bf16[3,96,1024]{2,1,0:T(8,128)(2,1)S(1)}, u32[]{:S(2)}, u32[]{:S(2)}) collective-permute-start(bf16[3,96,1024]{2,1,0:T(8,128)(2,1)S(1)} %get-tuple-element.77), channel_id=1, source_target_pairs={{0,4},{12,8},{1,5},{13,9},{2,6},{14,10},{3,7},{15,11},{16,20},{28,... | collective-permute-start | bytes 1769480 | tf_op jit(solution)/shard_map/ppermute | solution.py:471
  64.4 16.2 %collective-permute-start.12 = (bf16[4,96,1024]{2,1,0:T(8,128)(2,1)S(1)}, bf16[4,96,1024]{2,1,0:T(8,128)(2,1)S(1)}, u32[]{:S(2)}, u32[]{:S(2)}) collective-permute-start(bf16[4,96,1024]{2,1,0:T(8,128)(2,1)S(1)} %shard_map.74.refs_2_.b_ref), channel_id=1, source_target_pairs={{4,0},{8,12},{5,1},{9,13},{6,2},{10,14},{7,3},{11,15},{20,16},{24,... | collective-permute-start | bytes 2359304 | tf_op jit(solution)/shard_map/ppermute | solution.py:478
  70.9 16.7 %collective-permute-start.17 = (bf16[4,96,1024]{2,1,0:T(8,128)(2,1)S(1)}, bf16[4,96,1024]{2,1,0:T(8,128)(2,1)S(1)}, u32[]{:S(2)}, u32[]{:S(2)}) collective-permute-start(bf16[4,96,1024]{2,1,0:T(8,128)(2,1)S(1)} %get-tuple-element.85.refs_3_.refs_0_), channel_id=1, source_target_pairs={{4,8},{8,4},{5,9},{9,5},{6,10},{10,6},{7,11},{11,7},{20,24},{24,20... | collective-permute-start | bytes 2359304 | tf_op jit(solution)/shard_map/ppermute | solution.py:469
  71.6 33.6 %collective-permute-start.21 = (bf16[3,96,1024]{2,1,0:T(8,128)(2,1)S(1)}, bf16[3,96,1024]{2,1,0:T(8,128)(2,1)S(1)}, u32[]{:S(2)}, u32[]{:S(2)}) collective-permute-start(bf16[3,96,1024]{2,1,0:T(8,128)(2,1)S(1)} %get-tuple-element.93), channel_id=1, source_target_pairs={{0,4},{12,8},{1,5},{13,9},{2,6},{14,10},{3,7},{15,11},{16,20},{28,... | collective-permute-start | bytes 1769480 | tf_op jit(solution)/shard_map/ppermute | solution.py:471
  79.3 22.0 %collective-permute-start.19 = (bf16[4,96,1024]{2,1,0:T(8,128)(2,1)S(1)}, bf16[4,96,1024]{2,1,0:T(8,128)(2,1)S(1)}, u32[]{:S(2)}, u32[]{:S(2)}) collective-permute-start(bf16[4,96,1024]{2,1,0:T(8,128)(2,1)S(1)} %shard_map.77.refs_2_.b_ref), channel_id=1, source_target_pairs={{4,0},{8,12},{5,1},{9,13},{6,2},{10,14},{7,3},{11,15},{20,16},{24,... | collective-permute-start | bytes 2359304 | tf_op jit(solution)/shard_map/ppermute | solution.py:478
  86.8 26.6 %collective-permute-start.20 = (bf16[4,96,1024]{2,1,0:T(8,128)(2,1)S(1)}, bf16[4,96,1024]{2,1,0:T(8,128)(2,1)S(1)}, u32[]{:S(2)}, u32[]{:S(2)}) collective-permute-start(bf16[4,96,1024]{2,1,0:T(8,128)(2,1)S(1)} %get-tuple-element.88.refs_3_.p_ref), channel_id=1, source_target_pairs={{4,8},{8,4},{5,9},{9,5},{6,10},{10,6},{7,11},{11,7},{20,24},{24,20... | collective-permute-start | bytes 2359304 | tf_op jit(solution)/shard_map/ppermute | solution.py:469
  87.8 26.5 %collective-permute-start.18 = (bf16[4,96,1024]{2,1,0:T(8,128)(2,1)S(1)}, bf16[4,96,1024]{2,1,0:T(8,128)(2,1)S(1)}, u32[]{:S(2)}, u32[]{:S(2)}) collective-permute-start(bf16[4,96,1024]{2,1,0:T(8,128)(2,1)S(1)} %shard_map.80.refs_2_.b_ref), channel_id=1, source_target_pairs={{4,0},{8,12},{5,1},{9,13},{6,2},{10,14},{7,3},{11,15},{20,16},{24,... | collective-permute-start | bytes 2359304 | tf_op jit(solution)/shard_map/ppermute | solution.py:478
  89.1 30.6 %collective-permute-start.16 = (bf16[3,96,1024]{2,1,0:T(8,128)(2,1)S(1)}, bf16[3,96,1024]{2,1,0:T(8,128)(2,1)S(1)}, u32[]{:S(2)}, u32[]{:S(2)}) collective-permute-start(bf16[3,96,1024]{2,1,0:T(8,128)(2,1)S(1)} %get-tuple-element.87), channel_id=1, source_target_pairs={{0,4},{12,8},{1,5},{13,9},{2,6},{14,10},{3,7},{15,11},{16,20},{28,... | collective-permute-start | bytes 1769480 | tf_op jit(solution)/shard_map/ppermute | solution.py:471
  106.7 15.1 %collective-permute-start.23 = (bf16[4,96,1024]{2,1,0:T(8,128)(2,1)S(1)}, bf16[4,96,1024]{2,1,0:T(8,128)(2,1)S(1)}, u32[]{:S(2)}, u32[]{:S(2)}) collective-permute-start(bf16[4,96,1024]{2,1,0:T(8,128)(2,1)S(1)} %get-tuple-element.95.refs_0_.p_ref), channel_id=1, source_target_pairs={{4,8},{8,4},{5,9},{9,5},{6,10},{10,6},{7,11},{11,7},{20,24},{24,20... | collective-permute-start | bytes 2359304 | tf_op jit(solution)/shard_map/ppermute | solution.py:469
  107.4 34.4 %collective-permute-start.27 = (bf16[3,64,1024]{2,1,0:T(8,128)(2,1)S(1)}, bf16[3,64,1024]{2,1,0:T(8,128)(2,1)S(1)}, u32[]{:S(2)}, u32[]{:S(2)}) collective-permute-start(bf16[3,64,1024]{2,1,0:T(8,128)(2,1)S(1)} %get-tuple-element.107), channel_id=1, source_target_pairs={{0,4},{12,8},{1,5},{13,9},{2,6},{14,10},{3,7},{15,11},{16,20},{28,... | collective-permute-start | bytes 1179656 | tf_op jit(solution)/shard_map/ppermute | solution.py:471
  118.3 12.3 %collective-permute-start.28 = (f32[3,384,128]{2,1,0:T(8,128)S(1)}, f32[3,384,128]{2,1,0:T(8,128)S(1)}, u32[]{:S(2)}, u32[]{:S(2)}) collective-permute-start(f32[3,384,128]{2,1,0:T(8,128)S(1)} %constant_dynamic-update-slice_fusion), channel_id=1, source_target_pairs={{0,1},{1,0},{2,3},{3,2},{4,5},{5,4},{6,7},{7,6},{8,9},{9,8},{10,11... | collective-permute-start | bytes 1769480 | tf_op jit(solution)/shard_map/ppermute | solution.py:397
  118.4 18.0 %collective-permute-start.25 = (bf16[3,96,1024]{2,1,0:T(8,128)(2,1)S(1)}, bf16[3,96,1024]{2,1,0:T(8,128)(2,1)S(1)}, u32[]{:S(2)}, u32[]{:S(2)}) collective-permute-start(bf16[3,96,1024]{2,1,0:T(8,128)(2,1)S(1)} %get-tuple-element.102), channel_id=1, source_target_pairs={{4,0},{8,12},{5,1},{9,13},{6,2},{10,14},{7,3},{11,15},{20,16},{24,... | collective-permute-start | bytes 1769480 | tf_op jit(solution)/shard_map/ppermute | solution.py:478
  121.0 22.6 %collective-permute-start.26 = (bf16[4,96,1024]{2,1,0:T(8,128)(2,1)S(1)}, bf16[4,96,1024]{2,1,0:T(8,128)(2,1)S(1)}, u32[]{:S(2)}, u32[]{:S(2)}) collective-permute-start(bf16[4,96,1024]{2,1,0:T(8,128)(2,1)S(1)} %get-tuple-element.99.refs_0_.p_ref), channel_id=1, source_target_pairs={{4,8},{8,4},{5,9},{9,5},{6,10},{10,6},{7,11},{11,7},{20,24},{24,20... | collective-permute-start | bytes 2359304 | tf_op jit(solution)/shard_map/ppermute | solution.py:469
  121.7 30.8 %collective-permute-start.22 = (bf16[3,32,1024]{2,1,0:T(8,128)(2,1)S(1)}, bf16[3,32,1024]{2,1,0:T(8,128)(2,1)S(1)}, u32[]{:S(2)}, u32[]{:S(2)}) collective-permute-start(bf16[3,32,1024]{2,1,0:T(8,128)(2,1)S(1)} %get-tuple-element.98), channel_id=1, source_target_pairs={{0,4},{12,8},{1,5},{13,9},{2,6},{14,10},{3,7},{15,11},{16,20},{28,... | collective-permute-start | bytes 589832 | tf_op jit(solution)/shard_map/ppermute | solution.py:471
  130.6 18.0 %collective-permute-start.24 = (bf16[3,96,1024]{2,1,0:T(8,128)(2,1)S(1)}, bf16[3,96,1024]{2,1,0:T(8,128)(2,1)S(1)}, u32[]{:S(2)}, u32[]{:S(2)}) collective-permute-start(bf16[3,96,1024]{2,1,0:T(8,128)(2,1)S(1)} %get-tuple-element.101), channel_id=1, source_target_pairs={{4,0},{8,12},{5,1},{9,13},{6,2},{10,14},{7,3},{11,15},{20,16},{24,... | collective-permute-start | bytes 1769480 | tf_op jit(solution)/shard_map/ppermute | solution.py:478
  136.4 12.2 %collective-permute-start.29 = (bf16[3,384,128]{2,1,0:T(8,128)(2,1)S(1)}, bf16[3,384,128]{2,1,0:T(8,128)(2,1)S(1)}, u32[]{:S(2)}, u32[]{:S(2)}) collective-permute-start(bf16[3,384,128]{2,1,0:T(8,128)(2,1)S(1)} %add_convert_fusion.1.refs_0_), channel_id=1, source_target_pairs={{0,2},{1,3},{2,0},{3,1},{4,6},{5,7},{6,4},{7,5},{8,10},{9,11},{10,... | collective-permute-start | bytes 884744 | tf_op jit(solution)/shard_map/ppermute | solution.py:397
  142.8 11.3 %collective-permute-start.32 = (bf16[4,64,1024]{2,1,0:T(8,128)(2,1)S(1)}, bf16[4,64,1024]{2,1,0:T(8,128)(2,1)S(1)}, u32[]{:S(2)}, u32[]{:S(2)}) collective-permute-start(bf16[4,64,1024]{2,1,0:T(8,128)(2,1)S(1)} %shard_map.88.refs_0_.p_ref), channel_id=1, source_target_pairs={{4,8},{8,4},{5,9},{9,5},{6,10},{10,6},{7,11},{11,7},{20,24},{24,20... | collective-permute-start | bytes 1572872 | tf_op jit(solution)/shard_map/ppermute | solution.py:469
  144.4 19.5 %collective-permute-start.31 = (bf16[3,96,1024]{2,1,0:T(8,128)(2,1)S(1)}, bf16[3,96,1024]{2,1,0:T(8,128)(2,1)S(1)}, u32[]{:S(2)}, u32[]{:S(2)}) collective-permute-start(bf16[3,96,1024]{2,1,0:T(8,128)(2,1)S(1)} %get-tuple-element.111), channel_id=1, source_target_pairs={{4,0},{8,12},{5,1},{9,13},{6,2},{10,14},{7,3},{11,15},{20,16},{24,... | collective-permute-start | bytes 1769480 | tf_op jit(solution)/shard_map/ppermute | solution.py:478
  153.5 14.4 %collective-permute-start.30 = (bf16[4,32,1024]{2,1,0:T(8,128)(2,1)S(1)}, bf16[4,32,1024]{2,1,0:T(8,128)(2,1)S(1)}, u32[]{:S(2)}, u32[]{:S(2)}) collective-permute-start(bf16[4,32,1024]{2,1,0:T(8,128)(2,1)S(1)} %shard_map.91.refs_0_.p_ref), channel_id=1, source_target_pairs={{4,8},{8,4},{5,9},{9,5},{6,10},{10,6},{7,11},{11,7},{20,24},{24,20... | collective-permute-start | bytes 786440 | tf_op jit(solution)/shard_map/ppermute | solution.py:469
  155.0 16.9 %collective-permute-start.34 = (bf16[3,64,1024]{2,1,0:T(8,128)(2,1)S(1)}, bf16[3,64,1024]{2,1,0:T(8,128)(2,1)S(1)}, u32[]{:S(2)}, u32[]{:S(2)}) collective-permute-start(bf16[3,64,1024]{2,1,0:T(8,128)(2,1)S(1)} %get-tuple-element.118), channel_id=1, source_target_pairs={{4,0},{8,12},{5,1},{9,13},{6,2},{10,14},{7,3},{11,15},{20,16},{24,... | collective-permute-start | bytes 1179656 | tf_op jit(solution)/shard_map/ppermute | solution.py:478
  167.8 1.9 collective-permute-start.35
  168.4 9.2 %collective-permute-start.33 = (bf16[3,32,1024]{2,1,0:T(8,128)(2,1)S(1)}, bf16[3,32,1024]{2,1,0:T(8,128)(2,1)S(1)}, u32[]{:S(2)}, u32[]{:S(2)}) collective-permute-start(bf16[3,32,1024]{2,1,0:T(8,128)(2,1)S(1)} %get-tuple-element.117), channel_id=1, source_target_pairs={{4,0},{8,12},{5,1},{9,13},{6,2},{10,14},{7,3},{11,15},{20,16},{24,... | collective-permute-start | bytes 589832 | tf_op jit(solution)/shard_map/ppermute | solution.py:478
  169.8 10.8 %collective-permute-start.36 = (bf16[3,288,128]{2,1,0:T(8,128)(2,1)S(1)}, bf16[3,288,128]{2,1,0:T(8,128)(2,1)S(1)}, u32[]{:S(2)}, u32[]{:S(2)}) collective-permute-start(bf16[3,288,128]{2,1,0:T(8,128)(2,1)S(1)} %add_convert_fusion.2.refs_2_), channel_id=1, source_target_pairs={{0,2},{1,3},{2,0},{3,1},{4,6},{5,7},{6,4},{7,5},{8,10},{9,11},{10,... | collective-permute-start | bytes 663560 | tf_op jit(solution)/shard_map/ppermute | solution.py:397
  183.2 1.4 collective-permute-start.37
  184.6 4.6 %collective-permute-start.38 = (bf16[3,96,128]{2,1,0:T(8,128)(2,1)S(1)}, bf16[3,96,128]{2,1,0:T(8,128)(2,1)S(1)}, u32[]{:S(2)}, u32[]{:S(2)}) collective-permute-start(bf16[3,96,128]{2,1,0:T(8,128)(2,1)S(1)} %add_convert_fusion.3.refs_4_), channel_id=1, source_target_pairs={{0,2},{1,3},{2,0},{3,1},{4,6},{5,7},{6,4},{7,5},{8,10},{9,11},{10,... | collective-permute-start | bytes 221192 | tf_op jit(solution)/shard_map/ppermute | solution.py:397
  189.2 2.3 %copy-start = (bf16[3,768,1024]{2,1,0:T(8,128)(2,1)S(1)}, bf16[3,768,1024]{2,1,0:T(8,128)(2,1)}, u32[]{:S(2)}) copy-start(bf16[3,768,1024]{2,1,0:T(8,128)(2,1)} %get-tuple-element.126.refs_6_.refs_4_) | copy-start | bytes 14155780
  191.5 23.3 %copy-start.2 = (bf16[4,224,1024]{2,1,0:T(8,128)(2,1)S(1)}, bf16[4,224,1024]{2,1,0:T(8,128)(2,1)}, u32[]{:S(2)}) copy-start(bf16[4,224,1024]{2,1,0:T(8,128)(2,1)} %get-tuple-element.124.in_ref) | copy-start | bytes 5505028
  191.5 24.9 %copy-start.1 = (bf16[3,768,1024]{2,1,0:T(8,128)(2,1)S(1)}, bf16[3,768,1024]{2,1,0:T(8,128)(2,1)}, u32[]{:S(2)}) copy-start(bf16[3,768,1024]{2,1,0:T(8,128)(2,1)} %get-tuple-element.126.refs_6_.refs_4_) | copy-start | bytes 14155780
  203.9 1.6 collective-permute-start.39
  205.7 9.1 %collective-permute-start.40 = (bf16[3,384,128]{2,1,0:T(8,128)(2,1)S(1)}, bf16[3,384,128]{2,1,0:T(8,128)(2,1)S(1)}, u32[]{:S(2)}, u32[]{:S(2)}) collective-permute-start(bf16[3,384,128]{2,1,0:T(8,128)(2,1)S(1)} %add_convert_fusion.refs_0_), channel_id=1, source_target_pairs={{0,2},{1,3},{2,0},{3,1},{4,6},{5,7},{6,4},{7,5},{8,10},{9,11},{10,... | collective-permute-start | bytes 884744 | tf_op jit(solution)/shard_map/ppermute | solution.py:397
  207.5 8.6 %collective-permute-start.41 = (bf16[3,384,128]{2,1,0:T(8,128)(2,1)S(1)}, bf16[3,384,128]{2,1,0:T(8,128)(2,1)S(1)}, u32[]{:S(2)}, u32[]{:S(2)}) collective-permute-start(bf16[3,384,128]{2,1,0:T(8,128)(2,1)S(1)} %add_convert_fusion.refs_0_), channel_id=1, source_target_pairs={{0,1},{1,0},{2,3},{3,2},{4,5},{5,4},{6,7},{7,6},{8,9},{9,8},{10,11... | collective-permute-start | bytes 884744 | tf_op jit(solution)/shard_map/ppermute | solution.py:397
  214.8 1.6 collective-permute-start.42
